TPU v7x, 32 devices: a whole 2x2x4 slice. The times are simulated.
32 devices in a mesh: dp: 8 (over y, x, core), expert: 4 (over z).
Axes of the slice: x: 2, y: 2, z: 4, core: 2. Of those that a mesh axis runs over, the one named last changes fastest.
Arguments:
- hidden_in: bfloat16 [16, 1024, 2048], P('dp', 'expert'), may hold values from -6 to 6
- cotangent: bfloat16 [16, 1024, 2048], P('dp', 'expert'), may hold values from -6 to 6
- block_ids: int32 [16, 1024], P('dp'), may hold values from 0 to 7, never falling along the last dimension, each value on 1 to 256 neighbouring positions
- attn_routes: int32 [16, 1024, 2], P('dp', 'expert'), may hold values from 0 to 7, all different within a row; in each aligned block of 256 rows (0 to 255, 256 to 511, ..., all dimensions but the last counted through in order) at most 68 rows name the same one
- mlp_routes: int32 [16, 1024, 2], P('dp', 'expert'), may hold values from 0 to 7, all different within a row; in each aligned block of 256 rows (0 to 255, 256 to 511, ..., all dimensions but the last counted through in order) at most 68 rows name the same one
- adapter_index: int32 [16], P('dp'), may hold values from 0 to 7
- attn_gain: float32 [2048], replicated, may hold values from 0.5 to 1.5
- mlp_gain: float32 [2048], replicated, may hold values from 0.1 to 1.9
- attn_router: bfloat16 [2048, 8], replicated, may hold values from -0.125 to 0.125
- mlp_router: bfloat16 [2048, 8], replicated, may hold values from -0.125 to 0.125
- kv_weight: bfloat16 [2048, 4096], P('dp'), may hold values from -0.125 to 0.125
- query_weight: bfloat16 [8, 2048, 2048], P('expert', 'dp'), may hold values from -0.125 to 0.125
- output_weight: bfloat16 [8, 2048, 2048], P('expert', 'dp'), may hold values from -1 to 1
- inner_weight: bfloat16 [8, 2048, 11264], P('expert', 'dp'), may hold values from -0.125 to 0.125
- down_weight: bfloat16 [8, 5632, 2048], P('expert', 'dp'), may hold values from -0.21875 to 0.21875
- adapt_down: bfloat16 [2048, 128], replicated, may hold values from -0.125 to 0.125
- adapt_up: bfloat16 [4096, 128], replicated, may hold values from -1.5 to 1.5
Outputs:
- layer_out: bfloat16 [16, 1024, 2048], P('dp', 'expert')
- input_grad: float32 [16, 1024, 2048], P('dp', 'expert')
- down_grad: float32 [2048, 128], P(('dp', 'expert'))
- up_grad: float32 [4096, 128], P(('dp', 'expert'))
Inputs may be any that keep to these rules, and one draw needn't show every extreme that they name: `attn_routes`: each token names 2 different experts. In each aligned block of 256 positions of a sequence no expert is named more than 68 times, and in some block some expert exactly 68 times. `mlp_routes`: each token names 2 different experts. In each aligned block of 256 positions of a sequence no expert is named more than 68 times, and in some block some expert exactly 68 times. `block_ids`: along each sequence the block numbers never fall; each block holds 1 to 256 positions, some block exactly 256.
All inputs are finite; a program needn't handle non-finite values.
Results may differ from a plain program's by a relative error of at most 0.03.
Values may be sent and summed in bfloat16 or wider, within the bound.
No kernel may reach another device: no remote copies, remote signals or barrier semaphores. Data moves between devices by JAX's collectives and lax.ppermute only.
A program may use at most 640 MiB of HBM per device.

v0:
```python
import math

import jax
import jax.numpy as jnp
from jax import lax
from jax.sharding import PartitionSpec as P

HEADS = 16
HDIM = 128
FF = 5632
EXPERTS = 8
TOP = 2
RANK = 16
MICRO = 2


PRECISE = lax.Precision.HIGHEST
EPSILON = 1e-06
ROPE_BASE = 10000.0
MASKED_SCORE = -1e30


def rms_scale(values):
    return lax.rsqrt(jnp.mean(values * values, axis=-1, keepdims=True) + EPSILON)


def norm_back(values, scale_rows, norm_gain, grad_rows):
    scaled_grad = norm_gain * grad_rows
    return scale_rows * (
        scaled_grad
        - values * scale_rows * scale_rows * jnp.mean(scaled_grad * values, axis=-1, keepdims=True)
    )


def angle_tables(positions):
    half_dim = HDIM // 2
    frequency = ROPE_BASE ** (-(jnp.arange(half_dim, dtype=jnp.float32) * (2.0 / HDIM)))
    angles = positions.astype(jnp.float32)[:, None] * frequency[None, :]
    return (jnp.cos(angles), jnp.sin(angles))


def rotate(values, cos_tab, sin_tab):
    half_dim = HDIM // 2
    first_half = values[..., :half_dim]
    second_half = values[..., half_dim:]
    return jnp.concatenate(
        [
            first_half * cos_tab - second_half * sin_tab,
            second_half * cos_tab + first_half * sin_tab,
        ],
        axis=-1,
    )


def rotate_back(grad_rows, cos_tab, sin_tab):
    half_dim = HDIM // 2
    first_half = grad_rows[..., :half_dim]
    second_half = grad_rows[..., half_dim:]
    return jnp.concatenate(
        [
            first_half * cos_tab + second_half * sin_tab,
            second_half * cos_tab - first_half * sin_tab,
        ],
        axis=-1,
    )


def pair_gates(logits, route_ids):
    onehot = (route_ids[:, :, None] == jnp.arange(EXPERTS, dtype=jnp.int32)[None, None, :]).astype(
        jnp.float32
    )
    picked = jnp.sum(onehot * logits[:, None, :], axis=-1)
    logit_gap = picked[:, 0] - picked[:, 1]
    gate_pair = jnp.stack([jax.nn.sigmoid(logit_gap), jax.nn.sigmoid(-logit_gap)], axis=1)
    return (gate_pair, onehot)


def router_back(grad_gates, gate_pair, onehot, router):
    logit_step = (grad_gates[:, 0] - grad_gates[:, 1]) * gate_pair[:, 0] * gate_pair[:, 1]
    grad_logits = logit_step[:, None] * (onehot[:, 0] - onehot[:, 1])
    return jnp.dot(grad_logits, router.astype(jnp.float32).T, precision=PRECISE)


def slot_plan(route_ids, capacity):
    row_count = route_ids.shape[0]
    flat_routes = route_ids.reshape(row_count * TOP)
    expert_hits = (flat_routes[:, None] == jnp.arange(EXPERTS, dtype=jnp.int32)[None, :]).astype(
        jnp.int32
    )
    before = jnp.cumsum(expert_hits, axis=0) - expert_hits
    place_in = jnp.sum(before * expert_hits, axis=1)
    slot_ids = flat_routes * capacity + place_in
    send_table = (
        jnp.arange(EXPERTS * capacity, dtype=jnp.int32)[:, None] == slot_ids[None, :]
    ).astype(jnp.bfloat16)
    return (slot_ids, send_table)


def spread(send_table, values, capacity):
    placed = jnp.dot(send_table, values, preferred_element_type=jnp.float32).astype(jnp.bfloat16)
    return placed.reshape(EXPERTS, capacity, values.shape[-1])


def collect(buffer, slot_ids, row_count):
    flat_rows = buffer.reshape(buffer.shape[0] * buffer.shape[1], buffer.shape[2])
    return jnp.take(flat_rows, slot_ids, axis=0).reshape(row_count, TOP, buffer.shape[2])


def apply_experts(received, weight, einsum_form):
    exp_dev = weight.shape[0]
    by_expert = received.reshape(
        received.shape[0] // exp_dev, exp_dev, received.shape[1], received.shape[2]
    )
    result = jnp.einsum(einsum_form, by_expert, weight, preferred_element_type=jnp.float32)
    return result.reshape(received.shape[0], received.shape[1], result.shape[-1])


def attn_send(buffer):
    return lax.all_to_all(buffer, "expert", split_axis=0, concat_axis=0, tiled=True)


def attn_return(buffer):
    return lax.all_to_all(buffer, "expert", split_axis=0, concat_axis=0, tiled=True)


def mlp_send(buffer):
    return lax.all_to_all(buffer, "expert", split_axis=0, concat_axis=0, tiled=True)


def mlp_return(buffer):
    return lax.all_to_all(buffer, "expert", split_axis=0, concat_axis=0, tiled=True)


def gather_weights(kv_weight, query_weight, output_weight, inner_weight, down_weight):
    kv_full, query_full, output_full = (
        lax.all_gather(kv_weight, "dp", axis=0, tiled=True),
        lax.all_gather(query_weight, "dp", axis=1, tiled=True),
        lax.all_gather(output_weight, "dp", axis=1, tiled=True),
    )
    inner_full, down_full = (
        lax.all_gather(inner_weight, "dp", axis=1, tiled=True),
        lax.all_gather(down_weight, "dp", axis=1, tiled=True),
    )
    return (kv_full, query_full, output_full, inner_full, down_full)


def per_device(
    hidden_in,
    cotangent,
    block_ids,
    attn_routes,
    mlp_routes,
    adapter_index,
    attn_gain,
    mlp_gain,
    attn_router,
    mlp_router,
    kv_weight,
    query_weight,
    output_weight,
    inner_weight,
    down_weight,
    adapt_down,
    adapt_up,
):
    row_count = hidden_in.shape[1]
    model_width = hidden_in.shape[2]
    seq_len = block_ids.shape[1]
    capacity = (17 * row_count * TOP + 16 * EXPERTS - 1) // (16 * EXPERTS)
    scale_qk = 1.0 / math.sqrt(HDIM)
    first_row = lax.axis_index("expert") * row_count
    position = first_row + jnp.arange(row_count, dtype=jnp.int32)
    cos_tab, sin_tab = angle_tables(position)
    cos_k = cos_tab[:, None, :]
    sin_k = sin_tab[:, None, :]
    cos_q = cos_tab[:, None, None, :]
    sin_q = sin_tab[:, None, None, :]
    down_total = jnp.zeros(adapt_down.shape, jnp.float32)
    up_total = jnp.zeros(adapt_up.shape, jnp.float32)
    outputs = []
    input_grads = []
    for micro_id in range(MICRO):
        gathered = gather_weights(kv_weight, query_weight, output_weight, inner_weight, down_weight)
        kv_full, query_full, output_full, inner_full, down_full = gathered
        tokens = hidden_in[micro_id].astype(jnp.float32)
        upstream = cotangent[micro_id].astype(jnp.float32)
        seq_blocks = block_ids[micro_id]
        own_blocks = lax.dynamic_slice_in_dim(seq_blocks, first_row, row_count, 0)
        visible = seq_blocks[None, :] <= own_blocks[:, None]
        adapt_start = adapter_index[micro_id] * RANK
        down_sel = lax.dynamic_slice_in_dim(adapt_down, adapt_start, RANK, 1)
        up_sel = lax.dynamic_slice_in_dim(adapt_up, adapt_start, RANK, 1)
        scale_one = rms_scale(tokens)
        normed = tokens * scale_one * attn_gain
        normed_low = normed.astype(jnp.bfloat16)
        gates_a, onehot_a = pair_gates(
            jnp.dot(normed, attn_router.astype(jnp.float32), precision=PRECISE),
            attn_routes[micro_id],
        )
        slots_a, table_a = slot_plan(attn_routes[micro_id], capacity)
        token_table_a = jnp.sum(table_a.reshape(EXPERTS * capacity, row_count, TOP), axis=2)
        low_rank = jnp.dot(normed_low, down_sel, preferred_element_type=jnp.float32).astype(
            jnp.bfloat16
        )
        key_value = jnp.dot(normed_low, kv_full, preferred_element_type=jnp.float32) + jnp.einsum(
            "tr,or->to", low_rank, up_sel, preferred_element_type=jnp.float32
        )
        key_rot = rotate(
            key_value[:, :model_width].reshape(row_count, HEADS, HDIM), cos_k, sin_k
        ).astype(jnp.bfloat16)
        value_own = key_value[:, model_width:].astype(jnp.bfloat16)
        key_local = jnp.concatenate([key_rot.reshape(row_count, model_width), value_own], axis=1)
        key_all = lax.all_gather(key_local, "expert", axis=0, tiled=True)
        key_rows = key_all[:, :model_width].reshape(seq_len, HEADS, HDIM)
        value_rows = key_all[:, model_width:].reshape(seq_len, HEADS, HDIM)
        query_made = apply_experts(
            attn_send(spread(token_table_a, normed_low, capacity)), query_full, "slcd,lde->slce"
        ).astype(jnp.bfloat16)
        query_slots = collect(attn_return(query_made), slots_a, row_count)
        query_rot = rotate(
            query_slots.astype(jnp.float32).reshape(row_count, TOP, HEADS, HDIM), cos_q, sin_q
        ).astype(jnp.bfloat16)
        scores = (
            jnp.einsum("tjhd,khd->hjtk", query_rot, key_rows, preferred_element_type=jnp.float32)
            * scale_qk
        )
        masked = jnp.where(visible, scores, MASKED_SCORE)
        row_max = jnp.max(masked, axis=-1, keepdims=True)
        log_total = row_max + jnp.log(jnp.sum(jnp.exp(masked - row_max), axis=-1, keepdims=True))
        probs_low = jnp.where(visible, jnp.exp(masked - log_total), 0.0).astype(jnp.bfloat16)
        attended = jnp.einsum(
            "hjtk,khd->tjhd", probs_low, value_rows, preferred_element_type=jnp.float32
        ).astype(jnp.bfloat16)
        projected = apply_experts(
            attn_send(spread(table_a, attended.reshape(row_count * TOP, model_width), capacity)),
            output_full,
            "slcd,lde->slce",
        ).astype(jnp.bfloat16)
        attn_slots = collect(attn_return(projected), slots_a, row_count).astype(jnp.float32)
        middle = tokens + jnp.sum(gates_a[:, :, None] * attn_slots, axis=1)
        scale_two = rms_scale(middle)
        normed_two = middle * scale_two * mlp_gain
        gates_m, onehot_m = pair_gates(
            jnp.dot(normed_two, mlp_router.astype(jnp.float32), precision=PRECISE),
            mlp_routes[micro_id],
        )
        slots_m, table_m = slot_plan(mlp_routes[micro_id], capacity)
        token_table_m = jnp.sum(table_m.reshape(EXPERTS * capacity, row_count, TOP), axis=2)
        gate_up = apply_experts(
            mlp_send(spread(token_table_m, normed_two.astype(jnp.bfloat16), capacity)),
            inner_full,
            "slcd,lde->slce",
        )
        gate_part = gate_up[..., :FF]
        up_part = gate_up[..., FF:]
        sigmoid_gate = jax.nn.sigmoid(gate_part)
        hidden_low = (gate_part * sigmoid_gate * up_part).astype(jnp.bfloat16)
        expert_out = apply_experts(hidden_low, down_full, "slcf,lfd->slcd").astype(jnp.bfloat16)
        mlp_slots = collect(mlp_return(expert_out), slots_m, row_count).astype(jnp.float32)
        final_sum = middle + jnp.sum(gates_m[:, :, None] * mlp_slots, axis=1)
        outputs.append(final_sum.astype(jnp.bfloat16))
        grad_out_slots = (
            (gates_m[:, :, None] * upstream[:, None, :])
            .astype(jnp.bfloat16)
            .reshape(row_count * TOP, model_width)
        )
        grad_hidden = apply_experts(
            mlp_send(spread(table_m, grad_out_slots, capacity)), down_full, "slcd,lfd->slcf"
        )
        grad_gate = grad_hidden * up_part * sigmoid_gate * (1.0 + gate_part * (1.0 - sigmoid_gate))
        grad_up_part = grad_hidden * gate_part * sigmoid_gate
        grad_gate_up = jnp.concatenate([grad_gate, grad_up_part], axis=-1).astype(jnp.bfloat16)
        grad_source_two = apply_experts(grad_gate_up, inner_full, "slce,lde->slcd").astype(
            jnp.bfloat16
        )
        grad_normed_two = jnp.sum(
            collect(mlp_return(grad_source_two), slots_m, row_count).astype(jnp.float32), axis=1
        )
        grad_normed_two = grad_normed_two + router_back(
            jnp.sum(upstream[:, None, :] * mlp_slots, axis=-1), gates_m, onehot_m, mlp_router
        )
        grad_middle = upstream + norm_back(middle, scale_two, mlp_gain, grad_normed_two)
        grad_proj_slots = (
            (gates_a[:, :, None] * grad_middle[:, None, :])
            .astype(jnp.bfloat16)
            .reshape(row_count * TOP, model_width)
        )
        grad_attended = apply_experts(
            attn_send(spread(table_a, grad_proj_slots, capacity)), output_full, "slce,lde->slcd"
        ).astype(jnp.bfloat16)
        grad_attended = collect(attn_return(grad_attended), slots_a, row_count).reshape(
            row_count, TOP, HEADS, HDIM
        )
        grad_normed = router_back(
            jnp.sum(grad_middle[:, None, :] * attn_slots, axis=-1), gates_a, onehot_a, attn_router
        )
        again = (
            jnp.einsum("tjhd,khd->hjtk", query_rot, key_rows, preferred_element_type=jnp.float32)
            * scale_qk
        )
        attn_probs = jnp.where(
            visible, jnp.exp(jnp.where(visible, again, MASKED_SCORE) - log_total), 0.0
        )
        grad_probs = jnp.einsum(
            "tjhd,khd->hjtk", grad_attended, value_rows, preferred_element_type=jnp.float32
        )
        row_delta = jnp.sum(attn_probs * grad_probs, axis=-1, keepdims=True)
        grad_scores = (attn_probs * (grad_probs - row_delta)).astype(jnp.bfloat16)
        grad_query_rot = (
            jnp.einsum("hjtk,khd->tjhd", grad_scores, key_rows, preferred_element_type=jnp.float32)
            * scale_qk
        )
        probs_again = attn_probs.astype(jnp.bfloat16)
        grad_key_terms = (
            jnp.einsum("hjtk,tjhd->khd", grad_scores, query_rot, preferred_element_type=jnp.float32)
            * scale_qk
        )
        grad_value_terms = jnp.einsum(
            "hjtk,tjhd->khd", probs_again, grad_attended, preferred_element_type=jnp.float32
        )
        kv_terms = jnp.concatenate(
            [
                grad_key_terms.reshape(seq_len, model_width),
                grad_value_terms.reshape(seq_len, model_width),
            ],
            axis=1,
        )
        kv_own = lax.psum_scatter(
            kv_terms.astype(jnp.bfloat16), "expert", scatter_dimension=0, tiled=True
        )
        grad_key = rotate_back(
            kv_own[:, :model_width].astype(jnp.float32).reshape(row_count, HEADS, HDIM),
            cos_k,
            sin_k,
        )
        kv_grad = jnp.concatenate(
            [
                grad_key.reshape(row_count, model_width).astype(jnp.bfloat16),
                kv_own[:, model_width:],
            ],
            axis=1,
        )
        grad_queries = (
            rotate_back(grad_query_rot, cos_q, sin_q)
            .astype(jnp.bfloat16)
            .reshape(row_count * TOP, model_width)
        )
        grad_source = apply_experts(
            attn_send(spread(table_a, grad_queries, capacity)), query_full, "slce,lde->slcd"
        ).astype(jnp.bfloat16)
        grad_normed = grad_normed + jnp.sum(
            collect(attn_return(grad_source), slots_a, row_count).astype(jnp.float32), axis=1
        )
        grad_low_rank = jnp.dot(kv_grad, up_sel, preferred_element_type=jnp.float32).astype(
            jnp.bfloat16
        )
        grad_normed = grad_normed + jnp.einsum(
            "to,io->ti", kv_grad, kv_full, preferred_element_type=jnp.float32
        )
        grad_normed = grad_normed + jnp.einsum(
            "tr,dr->td", grad_low_rank, down_sel, preferred_element_type=jnp.float32
        )
        input_grads.append(grad_middle + norm_back(tokens, scale_one, attn_gain, grad_normed))
        down_piece = jnp.einsum(
            "td,tr->dr", normed_low, grad_low_rank, preferred_element_type=jnp.float32
        )
        up_piece = jnp.einsum("to,tr->or", kv_grad, low_rank, preferred_element_type=jnp.float32)
        down_total = lax.dynamic_update_slice_in_dim(
            down_total,
            lax.dynamic_slice_in_dim(down_total, adapt_start, RANK, 1) + down_piece,
            adapt_start,
            1,
        )
        up_total = lax.dynamic_update_slice_in_dim(
            up_total,
            lax.dynamic_slice_in_dim(up_total, adapt_start, RANK, 1) + up_piece,
            adapt_start,
            1,
        )
    down_grad, up_grad = (
        lax.psum_scatter(down_total, ("dp", "expert"), scatter_dimension=0, tiled=True),
        lax.psum_scatter(up_total, ("dp", "expert"), scatter_dimension=0, tiled=True),
    )
    return (jnp.stack(outputs), jnp.stack(input_grads), down_grad, up_grad)


def solution(mesh):
    return jax.shard_map(
        per_device,
        mesh=mesh,
        in_specs=(
            P("dp", "expert", None),
            P("dp", "expert", None),
            P("dp", None),
            P("dp", "expert", None),
            P("dp", "expert", None),
            P("dp"),
            P(),
            P(),
            P(),
            P(),
            P("dp", None),
            P("expert", "dp", None),
            P("expert", "dp", None),
            P("expert", "dp", None),
            P("expert", "dp", None),
            P(),
            P(),
        ),
        out_specs=(
            P("dp", "expert", None),
            P("dp", "expert", None),
            P(("dp", "expert"), None),
            P(("dp", "expert"), None),
        ),
        check_vma=False,
    )
```

profile of v0, /device:TPU:9, one launch (start us, length us, event | category | flops | bytes accessed | tf_op | source)
XLA Modules:
  0.0 3478.3 jit_solution(5566482848718046355)
XLA Ops:
  12.8 88.7 %all-gather.8.cloned.1.call-done = bf16[2048,4096]{1,0:T(8,128)(2,1)} async-done(((bf16[256,4096]{1,0:T(8,128)(2,1)}), bf16[2048,4096]{1,0:T(8,128)(2,1)}) %all-gather.8.cloned.1.call-update) | async-done | bytes 16777232 | tf_op jit(solution)/shard_map/all_gather | solution.py:136
  136.0 56.3 %all_to_all.120 = bf16[8,68,2048]{2,1,0:T(8,128)(2,1)} all-to-all(bf16[8,68,2048]{2,1,0:T(8,128)(2,1)} %reshape.668), channel_id=1, replica_groups=mesh['dp'=8,'expert'=4] {'expert'}, dimensions={0} | all-to-all | bytes 4456448 | tf_op jit(solution)/shard_map/all_to_all | solution.py:119
  214.4 107.5 %all-to-all-done.1 = bf16[8,68,2048]{2,1,0:T(8,128)(2,1)} async-done(((bf16[8,68,2048]{2,1,0:T(8,128)(2,1)}), bf16[8,68,2048]{2,1,0:T(8,128)(2,1)}, u32[]{:S(2)}, u32[]{:S(2)}) %all-to-all-start.1) | async-done | bytes 2228256 | tf_op jit(solution)/shard_map/all_to_all | solution.py:123
  344.3 46.6 %all-gather.10.cloned.1.call-done = bf16[1024,4096]{1,0:T(8,128)(2,1)} async-done(((bf16[256,4096]{1,0:T(8,128)(2,1)}), bf16[1024,4096]{1,0:T(8,128)(2,1)}) %all-gather.10.cloned.1.call-update) | async-done | bytes 8388624 | tf_op jit(solution)/shard_map/all_gather | solution.py:213
  485.1 48.9 %all-to-all-done.2 = bf16[8,68,2048]{2,1,0:T(8,128)(2,1)} async-done(((bf16[8,68,2048]{2,1,0:T(8,128)(2,1)}), bf16[8,68,2048]{2,1,0:T(8,128)(2,1)}, u32[]{:S(2)}, u32[]{:S(2)}) %all-to-all-start.2) | async-done | bytes 2228256 | tf_op jit(solution)/shard_map/all_to_all | solution.py:119
  564.8 39.5 %all-to-all-done.3 = bf16[8,68,2048]{2,1,0:T(8,128)(2,1)} async-done(((bf16[8,68,2048]{2,1,0:T(8,128)(2,1)}), bf16[8,68,2048]{2,1,0:T(8,128)(2,1)}, u32[]{:S(2)}, u32[]{:S(2)}) %all-to-all-start.3) | async-done | bytes 2228256 | tf_op jit(solution)/shard_map/all_to_all | solution.py:123
  642.8 60.3 %all_to_all.121 = bf16[8,68,2048]{2,1,0:T(8,128)(2,1)} all-to-all(bf16[8,68,2048]{2,1,0:T(8,128)(2,1)} %reshape.676), channel_id=1, replica_groups=mesh['dp'=8,'expert'=4] {'expert'}, dimensions={0} | all-to-all | bytes 4456448 | tf_op jit(solution)/shard_map/all_to_all | solution.py:127
  703.1 193.8 %all-gather.16.cloned.1.call-done = bf16[2,2048,11264]{2,1,0:T(8,128)(2,1)} async-done(((bf16[2,256,11264]{2,1,0:T(8,128)(2,1)}), bf16[2,2048,11264]{2,1,0:T(8,128)(2,1)}) %all-gather.16.cloned.1.call-update) | async-done | bytes 92274704 | tf_op jit(solution)/shard_map/all_gather | solution.py:141
  896.9 49.4 %fusion.24 = f32[4,2,68,11264]{3,2,0,1:T(8,128)} fusion(bf16[2,2048,11264]{2,1,0:T(8,128)(2,1)} %all-gather.16.cloned.1.call-done, bf16[4,2,68,2048]{3,2,1,0:T(8,128)(2,1)} %bitcast.639), kind=kOutput, calls=%fused_computation.46 | convolution fusion | flops 25098715136 | bytes 119013376 | tf_op jit(solution)/shard_map/slcd,lde->slce/dot_general | solution.py:114
  969.8 143.0 %all-gather.18.cloned.1.call-done = bf16[2,5632,2048]{2,1,0:T(8,128)(2,1)} async-done(((bf16[2,704,2048]{2,1,0:T(8,128)(2,1)}), bf16[2,5632,2048]{2,1,0:T(8,128)(2,1)}) %all-gather.18.cloned.1.call-update) | async-done | bytes 46137360 | tf_op jit(solution)/shard_map/all_gather | solution.py:142
  1217.4 58.8 %all_to_all.122 = bf16[8,68,2048]{2,1,0:T(8,128)(2,1)} all-to-all(bf16[8,68,2048]{2,1,0:T(8,128)(2,1)} %reshape.698), channel_id=1, replica_groups=mesh['dp'=8,'expert'=4] {'expert'}, dimensions={0} | all-to-all | bytes 4456448 | tf_op jit(solution)/shard_map/all_to_all | solution.py:127
  1329.7 41.6 %fusion.152 = bf16[4,2,68,2048]{3,2,0,1:T(8,128)(2,1)} fusion(bf16[2,2048,11264]{2,1,0:T(8,128)(2,1)} %all-gather.16.cloned.1.call-done, bf16[4,2,68,5632]{3,2,1,0:T(8,128)(2,1)} %bitcast.619, bf16[4,2,68,5632]{3,2,1,0:T(8,128)(2,1)} %bitcast.618), kind=kOutput, calls=%fused_computation.175 | convolution fusion | flops 25124339712 | bytes 106758144 | tf_op jit(solution)/shard_map/slce,lde->slcd/dot_general | solution.py:114
  1381.7 48.3 %all-to-all-done.13 = bf16[8,68,2048]{2,1,0:T(8,128)(2,1)} async-done(((bf16[8,68,2048]{2,1,0:T(8,128)(2,1)}), bf16[8,68,2048]{2,1,0:T(8,128)(2,1)}, u32[]{:S(2)}, u32[]{:S(2)}) %all-to-all-start.13) | async-done | bytes 2228256 | tf_op jit(solution)/shard_map/all_to_all | solution.py:131
  1501.4 122.7 %all_to_all.123 = bf16[8,68,2048]{2,1,0:T(8,128)(2,1)S(1)} all-to-all(bf16[8,68,2048]{2,1,0:T(8,128)(2,1)} %reshape.685), channel_id=1, replica_groups=mesh['dp'=8,'expert'=4] {'expert'}, dimensions={0} | all-to-all | bytes 4456448 | tf_op jit(solution)/shard_map/all_to_all | solution.py:119
  1644.4 85.4 %all-to-all-done.7 = bf16[8,68,2048]{2,1,0:T(8,128)(2,1)} async-done(((bf16[8,68,2048]{2,1,0:T(8,128)(2,1)}), bf16[8,68,2048]{2,1,0:T(8,128)(2,1)}, u32[]{:S(2)}, u32[]{:S(2)}) %all-to-all-start.7) | async-done | bytes 2228256 | tf_op jit(solution)/shard_map/all_to_all | solution.py:123
  1833.4 57.7 %all_to_all.124 = bf16[8,68,2048]{2,1,0:T(8,128)(2,1)S(1)} all-to-all(bf16[8,68,2048]{2,1,0:T(8,128)(2,1)} %reshape.689), channel_id=1, replica_groups=mesh['dp'=8,'expert'=4] {'expert'}, dimensions={0} | all-to-all | bytes 4456448 | tf_op jit(solution)/shard_map/all_to_all | solution.py:119
  2066.1 46.4 %fusion.27 = f32[4,2,68,11264]{3,2,0,1:T(8,128)} fusion(bf16[2,2048,11264]{2,1,0:T(8,128)(2,1)} %all-gather.16.cloned.1.call-done, bf16[4,2,68,2048]{3,2,1,0:T(8,128)(2,1)} %bitcast.59), kind=kOutput, calls=%fused_computation.47 | convolution fusion | flops 25098715136 | bytes 119013376 | tf_op jit(solution)/shard_map/slcd,lde->slce/dot_general | solution.py:114
  2411.6 41.4 %fusion.147 = bf16[4,2,68,2048]{3,2,0,1:T(8,128)(2,1)} fusion(bf16[2,2048,11264]{2,1,0:T(8,128)(2,1)} %all-gather.16.cloned.1.call-done, bf16[4,2,68,5632]{3,2,1,0:T(8,128)(2,1)} %bitcast.617, bf16[4,2,68,5632]{3,2,1,0:T(8,128)(2,1)} %bitcast.616), kind=kOutput, calls=%fused_computation.174 | convolution fusion | flops 25124339712 | bytes 106758144 | tf_op jit(solution)/shard_map/slce,lde->slcd/dot_general | solution.py:114
  2492.9 81.9 %all-to-all-done.19 = bf16[8,68,2048]{2,1,0:T(8,128)(2,1)S(1)} async-done(((bf16[8,68,2048]{2,1,0:T(8,128)(2,1)}), bf16[8,68,2048]{2,1,0:T(8,128)(2,1)S(1)}, u32[]{:S(2)}, u32[]{:S(2)}) %all-to-all-start.19) | async-done | bytes 2228256 | tf_op jit(solution)/shard_map/all_to_all | solution.py:131
  2720.2 57.6 %all_to_all.125 = bf16[8,68,2048]{2,1,0:T(8,128)(2,1)S(1)} all-to-all(bf16[8,68,2048]{2,1,0:T(8,128)(2,1)S(1)} %reshape.716), channel_id=1, replica_groups=mesh['dp'=8,'expert'=4] {'expert'}, dimensions={0} | all-to-all | bytes 4456448 | tf_op jit(solution)/shard_map/all_to_all | solution.py:119
  2787.1 56.2 %all_to_all.126 = bf16[8,68,2048]{2,1,0:T(8,128)(2,1)} all-to-all(bf16[8,68,2048]{2,1,0:T(8,128)(2,1)S(1)} %bitcast.611), channel_id=1, replica_groups=mesh['dp'=8,'expert'=4] {'expert'}, dimensions={0} | all-to-all | bytes 4456448 | tf_op jit(solution)/shard_map/all_to_all | solution.py:123
  2977.7 107.5 %all-to-all-done.22 = bf16[8,68,2048]{2,1,0:T(8,128)(2,1)} async-done(((bf16[8,68,2048]{2,1,0:T(8,128)(2,1)}), bf16[8,68,2048]{2,1,0:T(8,128)(2,1)}, u32[]{:S(2)}, u32[]{:S(2)}) %all-to-all-start.22) | async-done | bytes 2228256 | tf_op jit(solution)/shard_map/all_to_all | solution.py:119
  3105.8 83.6 %reduce-scatter.9.cloned.1.call-done = bf16[256,4096]{0,1:T(8,128)(2,1)} async-done(((bf16[1024,4096]{0,1:T(8,128)(2,1)}), bf16[256,4096]{0,1:T(8,128)(2,1)}) %reduce-scatter.9.cloned.1.call-update) | async-done | bytes 2097168 | tf_op jit(solution)/shard_map/reduce_scatter | solution.py:328
  3338.4 132.9 %reduce-scatter.13.cloned.1.call-done = f32[64,128]{1,0:T(8,128)} async-done(((f32[2048,128]{1,0:T(8,128)}), f32[64,128]{1,0:T(8,128)}) %reduce-scatter.13.cloned.1.call-update) | async-done | bytes 32784
  (711 shorter events, 1604.4 us)
Async XLA Ops:
  7.2 94.2 %all-gather.8.cloned.1.call-start = ((), (), s32[]{:S(2)}) async-start(), calls=%async_computation.28 | async-start | bytes 18874368 | tf_op jit(solution)/shard_map/all_gather | solution.py:136
  7.9 185.3 %all-gather.12.cloned.1.call-start = ((), (), s32[]{:S(2)}) async-start(), calls=%async_computation.30 | async-start | bytes 18874368 | tf_op jit(solution)/shard_map/all_gather | solution.py:137
  8.7 382.2 %all-gather.10.cloned.1.call-start = ((), (), s32[]{:S(2)}) async-start(), calls=%async_computation.29 | async-start | bytes 10485760 | tf_op jit(solution)/shard_map/all_gather | solution.py:213
  114.5 370.6 %all-gather.14.cloned.1.call-start = ((), (), s32[]{:S(2)}) async-start(), calls=%async_computation.31 | async-start | bytes 18874368 | tf_op jit(solution)/shard_map/all_gather | solution.py:138
  115.1 781.8 %all-gather.16.cloned.1.call-start = ((), (), s32[]{:S(2)}) async-start(), calls=%async_computation.32 | async-start | bytes 103809024 | tf_op jit(solution)/shard_map/all_gather | solution.py:141
  115.7 997.2 %all-gather.18.cloned.1.call-start = ((), (), s32[]{:S(2)}) async-start(), calls=%async_computation.33 | async-start | bytes 51904512 | tf_op jit(solution)/shard_map/all_gather | solution.py:142
  206.3 115.6 %all-to-all-start.1 = ((bf16[8,68,2048]{2,1,0:T(8,128)(2,1)}), bf16[8,68,2048]{2,1,0:T(8,128)(2,1)}, u32[]{:S(2)}, u32[]{:S(2)}) async-start(bf16[8,68,2048]{2,1,0:T(8,128)(2,1)} %bitcast.605), calls=%async_computation.1 | async-start | bytes 4718592 | tf_op jit(solution)/shard_map/all_to_all | solution.py:123
  474.4 59.6 %all-to-all-start.2 = ((bf16[8,68,2048]{2,1,0:T(8,128)(2,1)}), bf16[8,68,2048]{2,1,0:T(8,128)(2,1)}, u32[]{:S(2)}, u32[]{:S(2)}) async-start(bf16[8,68,2048]{2,1,0:T(8,128)(2,1)} %reshape.672), calls=%async_computation.2 | async-start | bytes 4718592 | tf_op jit(solution)/shard_map/all_to_all | solution.py:119
  547.1 57.2 %all-to-all-start.3 = ((bf16[8,68,2048]{2,1,0:T(8,128)(2,1)}), bf16[8,68,2048]{2,1,0:T(8,128)(2,1)}, u32[]{:S(2)}, u32[]{:S(2)}) async-start(bf16[8,68,2048]{2,1,0:T(8,128)(2,1)} %bitcast.604), calls=%async_computation.3 | async-start | bytes 4718592 | tf_op jit(solution)/shard_map/all_to_all | solution.py:123
  1135.6 55.7 %all-to-all-start.5 = ((bf16[8,68,2048]{2,1,0:T(8,128)(2,1)}), bf16[8,68,2048]{2,1,0:T(8,128)(2,1)}, u32[]{:S(2)}, u32[]{:S(2)}) async-start(bf16[8,68,2048]{2,1,0:T(8,128)(2,1)} %bitcast.606), calls=%async_computation.5 | async-start | bytes 4718592 | tf_op jit(solution)/shard_map/all_to_all | solution.py:131
  1381.0 371.3 %all-gather.20.cloned.1.call-start = ((), (), s32[]{:S(2)}) async-start(), calls=%async_computation.34 | async-start | bytes 10485760 | tf_op jit(solution)/shard_map/all_gather | solution.py:213
  1634.9 94.9 %all-to-all-start.7 = ((bf16[8,68,2048]{2,1,0:T(8,128)(2,1)}), bf16[8,68,2048]{2,1,0:T(8,128)(2,1)}, u32[]{:S(2)}, u32[]{:S(2)}) async-start(bf16[8,68,2048]{2,1,0:T(8,128)(2,1)} %bitcast.608), calls=%async_computation.7 | async-start | bytes 4718592 | tf_op jit(solution)/shard_map/all_to_all | solution.py:123
  1999.4 58.6 %all-to-all-start.10 = ((bf16[8,68,2048]{2,1,0:T(8,128)(2,1)}), bf16[8,68,2048]{2,1,0:T(8,128)(2,1)}, u32[]{:S(2)}, u32[]{:S(2)}) async-start(bf16[8,68,2048]{2,1,0:T(8,128)(2,1)} %reshape.693), calls=%async_computation.10 | async-start | bytes 4718592 | tf_op jit(solution)/shard_map/all_to_all | solution.py:127
  2058.0 71.7 %all-to-all-start.14 = ((bf16[8,68,2048]{2,1,0:T(8,128)(2,1)}), bf16[8,68,2048]{2,1,0:T(8,128)(2,1)S(1)}, u32[]{:S(2)}, u32[]{:S(2)}) async-start(bf16[8,68,2048]{2,1,0:T(8,128)(2,1)} %reshape.702), calls=%async_computation.14 | async-start | bytes 4718592 | tf_op jit(solution)/shard_map/all_to_all | solution.py:119
  2195.1 66.7 %all-to-all-start.11 = ((bf16[8,68,2048]{2,1,0:T(8,128)(2,1)}), bf16[8,68,2048]{2,1,0:T(8,128)(2,1)}, u32[]{:S(2)}, u32[]{:S(2)}) async-start(bf16[8,68,2048]{2,1,0:T(8,128)(2,1)} %bitcast.66), calls=%async_computation.11 | async-start | bytes 4718592 | tf_op jit(solution)/shard_map/all_to_all | solution.py:131
  2279.4 73.9 %all-to-all-start.18 = ((bf16[8,68,2048]{2,1,0:T(8,128)(2,1)}), bf16[8,68,2048]{2,1,0:T(8,128)(2,1)}, u32[]{:S(2)}, u32[]{:S(2)}) async-start(bf16[8,68,2048]{2,1,0:T(8,128)(2,1)} %reshape.712), calls=%async_computation.19 | async-start | bytes 4718592 | tf_op jit(solution)/shard_map/all_to_all | solution.py:127
  2284.0 375.2 %reduce-scatter.7.cloned.1.call-start = ((), (), s32[]{:S(2)}) async-start(), calls=%async_computation.35 | async-start | bytes 10485760 | tf_op jit(solution)/shard_map/reduce_scatter | solution.py:328
  2353.3 116.9 %all-to-all-start.16 = ((bf16[8,68,2048]{2,1,0:T(8,128)(2,1)}), bf16[8,68,2048]{2,1,0:T(8,128)(2,1)S(1)}, u32[]{:S(2)}, u32[]{:S(2)}) async-start(bf16[8,68,2048]{2,1,0:T(8,128)(2,1)} %reshape.705), calls=%async_computation.16 | async-start | bytes 4718592 | tf_op jit(solution)/shard_map/all_to_all | solution.py:119
  2471.5 103.2 %all-to-all-start.19 = ((bf16[8,68,2048]{2,1,0:T(8,128)(2,1)}), bf16[8,68,2048]{2,1,0:T(8,128)(2,1)S(1)}, u32[]{:S(2)}, u32[]{:S(2)}) async-start(bf16[8,68,2048]{2,1,0:T(8,128)(2,1)} %bitcast.609), calls=%async_computation.20 | async-start | bytes 4718592 | tf_op jit(solution)/shard_map/all_to_all | solution.py:131
  2582.2 607.2 %reduce-scatter.9.cloned.1.call-start = ((), (), s32[]{:S(2)}) async-start(), calls=%async_computation.36 | async-start | bytes 10485760 | tf_op jit(solution)/shard_map/reduce_scatter | solution.py:328
  2967.9 117.3 %all-to-all-start.22 = ((bf16[8,68,2048]{2,1,0:T(8,128)(2,1)}), bf16[8,68,2048]{2,1,0:T(8,128)(2,1)}, u32[]{:S(2)}, u32[]{:S(2)}) async-start(bf16[8,68,2048]{2,1,0:T(8,128)(2,1)} %reshape.719), calls=%async_computation.23 | async-start | bytes 4718592 | tf_op jit(solution)/shard_map/all_to_all | solution.py:119
  3096.2 152.4 %all-to-all-start.23 = ((bf16[8,68,2048]{2,1,0:T(8,128)(2,1)}), bf16[8,68,2048]{2,1,0:T(8,128)(2,1)}, u32[]{:S(2)}, u32[]{:S(2)}) async-start(bf16[8,68,2048]{2,1,0:T(8,128)(2,1)} %bitcast.601), calls=%async_computation.24 | async-start | bytes 4718592 | tf_op jit(solution)/shard_map/all_to_all | solution.py:123
  3105.8 231.1 %reduce-scatter.11.cloned.1.call-start = ((), (), s32[]{:S(2)}) async-start(), calls=%async_computation.37 | async-start | bytes 2162688 | tf_op jit(solution)/shard_map/reduce_scatter | solution.py:382
  3206.4 265.0 %reduce-scatter.13.cloned.1.call-start = ((), (), s32[]{:S(2)}) async-start(), calls=%async_computation.38 | async-start | bytes 1081344
  (153 other events, 2677.8 us)
Sparse Core Ops, SparseCore 0:
  9.9 91.4 all-gather.7
  103.3 89.8 all-gather.11
  195.4 195.5 all-gather.9
  392.7 92.3 all-gather.13
  486.9 409.9 all-gather.15
  898.7 214.1 all-gather.17
  1482.3 249.4 all-gather.19
  2331.2 247.8 reduce-scatter.6
  2946.1 243.2 reduce-scatter.8
  3206.5 130.2 reduce-scatter.10
  3339.8 131.5 reduce-scatter.12
where the time goes:
time: 3510 us; the launch traced here: 3480 us
  waiting for transfers between devices  1370 us (39%)
  matrix products  681 us (19%)
  blocking collectives  470 us (13%)
  local copies, waits for them, and re-layouts  455 us (13%)
  other arithmetic  363 us (10%)
  starting transfers between devices  121 us (3%)
    dot_general x16, matrix products, apply_experts(): jnp.einsum(einsum_form, by_expert, weight, preferred_element_type=jnp.flo...  349 us
    all_to_all x7, waiting for transfers between devices, attn_return(): lax.all_to_all(buffer, 'expert', split_axis=0, concat_axis=0, tiled=True)  301 us
    all_to_all x4, blocking collectives, attn_send(): lax.all_to_all(buffer, 'expert', split_axis=0, concat_axis=0, tiled=True)  294 us
    all_gather x1, waiting for transfers between devices, gather_weights(): lax.all_gather(inner_weight, 'dp', axis=1, tiled=True)  194 us
    all_to_all x4, waiting for transfers between devices, attn_send(): lax.all_to_all(buffer, 'expert', split_axis=0, concat_axis=0, tiled=True)  170 us
    all_to_all x4, waiting for transfers between devices, mlp_return(): lax.all_to_all(buffer, 'expert', split_axis=0, concat_axis=0, tiled=True)  164 us
    all_gather x1, waiting for transfers between devices, gather_weights(): lax.all_gather(down_weight, 'dp', axis=1, tiled=True)  143 us
    unnamed x12, waiting for transfers between devices  136 us
  transfers between devices with their start and end apart: 28, of which 22 were waited for; matrix products, arithmetic and copies ran while one was open for 27% of the time, Pallas kernels for 0%

commit v1 on v0

v1 whole, which is shorter than its diff:
```python
import functools
import math

import jax
import jax.numpy as jnp
import numpy as np
from jax import lax
from jax.experimental import pallas as pl
from jax.experimental.pallas import tpu as pltpu
from jax.sharding import PartitionSpec as P

HEADS = 16
HDIM = 128
FF = 5632
EXPERTS = 8
TOP = 2
RANK = 16
NADAPT = 8

PRECISE = lax.Precision.HIGHEST
EPSILON = 1e-06
ROPE_BASE = 10000.0
MASKED_SCORE = -1e30
SCALE_QK = 1.0 / math.sqrt(HDIM)
BF16 = jnp.bfloat16
F32 = jnp.float32
VMEM_LIMIT = 58 * 1024 * 1024

NN = (((1,), (0,)), ((), ()))
NT = (((1,), (1,)), ((), ()))
TN = (((0,), (0,)), ((), ()))


def mm(left, right, dims=NN):
    return lax.dot_general(left, right, dims, preferred_element_type=F32)


def params(*semantics):
    return pltpu.CompilerParams(dimension_semantics=semantics, vmem_limit_bytes=VMEM_LIMIT)


def once(shape, index_map):
    return pl.BlockSpec(shape, index_map, pipeline_mode=pl.Buffered(1))


def rms_scale(values):
    return lax.rsqrt(jnp.mean(values * values, axis=-1, keepdims=True) + EPSILON)


def norm_back(values, scale_rows, norm_gain, grad_rows):
    scaled_grad = norm_gain * grad_rows
    return scale_rows * (
        scaled_grad
        - values * scale_rows * scale_rows * jnp.mean(scaled_grad * values, axis=-1, keepdims=True)
    )


def angle_tables(positions):
    half_dim = HDIM // 2
    frequency = ROPE_BASE ** (-(jnp.arange(half_dim, dtype=F32) * (2.0 / HDIM)))
    frequency = jnp.concatenate([frequency, frequency])
    sign = jnp.concatenate([-jnp.ones((half_dim,), F32), jnp.ones((half_dim,), F32)])
    angles = positions.astype(F32)[..., None] * frequency
    return (jnp.cos(angles), jnp.sin(angles) * sign)


def three_parts(values):
    first = values.astype(BF16)
    rest = values - first.astype(F32)
    second = rest.astype(BF16)
    third = (rest - second.astype(F32)).astype(BF16)
    return first, second, third


def gather_line(block, axis, size, put, start):
    here = lax.axis_index(axis)
    rightward = [(i, i + 1) for i in range(size - 1)]
    leftward = [(i + 1, i) for i in range(size - 1)]
    from_left, from_right = [block], [block]
    for _ in range(size - 1):
        from_left.append(lax.ppermute(from_left[-1], axis, rightward))
        from_right.append(lax.ppermute(from_right[-1], axis, leftward))
    total = put(start, block, here)
    for step in range(1, size):
        piece = jnp.where(here >= step, from_left[step], from_right[size - step])
        total = put(total, piece, lax.rem(here - step + size, size))
    return total


def send(buffer):
    return lax.all_to_all(buffer, "expert", split_axis=0, concat_axis=0, tiled=True)


def kv_body(seqs, seq_len, key_tiles, x_ref, low_ref, w_ref, up_ref, cos_ref, sin_ref, out_ref):
    is_key = pl.program_id(0) < key_tiles
    for s in range(seqs):
        rows = pl.ds(s * seq_len, seq_len)
        made = mm(x_ref[rows, :], w_ref[...]) + mm(low_ref[rows, :], up_ref[...], NT)

        @pl.when(is_key)
        def _(made=made, rows=rows):
            for h in range(made.shape[1] // HDIM):
                cols = slice(h * HDIM, (h + 1) * HDIM)
                part = made[:, cols]
                turned = part * cos_ref[...] + pltpu.roll(part, HDIM // 2, 1) * sin_ref[...]
                out_ref[rows, cols] = turned.astype(BF16)

        @pl.when(jnp.logical_not(is_key))
        def _(made=made, rows=rows):
            out_ref[rows, :] = made.astype(BF16)


def make_key_value(normed_low, low_rank, kv_full, adapt_up, cos_k, sin_k, seqs):
    rows, width = normed_low.shape
    seq_len = rows // seqs
    tile = 512
    return pl.pallas_call(
        functools.partial(kv_body, seqs, seq_len, width // tile),
        grid=(2 * width // tile,),
        in_specs=[
            once((rows, width), lambda i: (0, 0)),
            once((rows, low_rank.shape[1]), lambda i: (0, 0)),
            pl.BlockSpec((width, tile), lambda i: (0, i)),
            pl.BlockSpec((tile, low_rank.shape[1]), lambda i: (i, 0)),
            once((seq_len, HDIM), lambda i: (0, 0)),
            once((seq_len, HDIM), lambda i: (0, 0)),
        ],
        out_specs=pl.BlockSpec((rows, tile), lambda i: (0, i)),
        out_shape=jax.ShapeDtypeStruct((rows, 2 * width), BF16),
        compiler_params=params("arbitrary"),
        name="key_value",
    )(normed_low, low_rank, kv_full, adapt_up, cos_k, sin_k)


def attend_body(q_ref, k_ref, v_ref, cos_ref, sin_ref, qb_ref, kb_ref, rot_ref, out_ref, lse_ref):
    locals_, _, slots, _ = q_ref.shape
    rows = locals_ * slots
    q = q_ref[...].reshape(rows, HDIM).astype(F32)
    cos, sin = cos_ref[...].reshape(rows, HDIM), sin_ref[...].reshape(rows, HDIM)
    rot = (q * cos + pltpu.roll(q, HDIM // 2, 1) * sin).astype(BF16)
    rot_ref[...] = rot.reshape(rot_ref.shape)
    k, v = k_ref[0], v_ref[0]
    kb = kb_ref[0]
    for l in range(locals_):
        part = rot[l * slots : (l + 1) * slots]
        visible = kb <= qb_ref[l, 0]
        masked = jnp.where(visible, mm(part, k, NT), MASKED_SCORE)
        top = jnp.max(masked, axis=-1, keepdims=True)
        terms = jnp.exp((masked - top) * SCALE_QK)
        total = jnp.sum(terms, axis=-1, keepdims=True)
        out = mm(terms.astype(BF16), v) * (1.0 / total)
        out_ref[l, 0] = out.astype(BF16)
        lse_ref[l, 0, 0] = top * SCALE_QK + jnp.log(total)


def attend(queries, key_value, cos_q, sin_q, query_blocks, key_blocks):
    locals_, seqs, slots, width = queries.shape
    seq_len = key_value.shape[1]
    q_spec = pl.BlockSpec((locals_, 1, slots, HDIM), lambda s, h: (0, s, 0, h))
    tab_spec = pl.BlockSpec((locals_, 1, slots, HDIM), lambda s, h: (0, s, 0, 0))
    return pl.pallas_call(
        attend_body,
        grid=(seqs, HEADS),
        in_specs=[
            q_spec,
            pl.BlockSpec((1, seq_len, HDIM), lambda s, h: (s, 0, h)),
            pl.BlockSpec((1, seq_len, HDIM), lambda s, h: (s, 0, HEADS + h)),
            tab_spec,
            tab_spec,
            pl.BlockSpec((locals_, 1, slots, 1), lambda s, h: (0, s, 0, 0)),
            pl.BlockSpec((1, 1, seq_len), lambda s, h: (s, 0, 0)),
        ],
        out_specs=[
            q_spec,
            q_spec,
            pl.BlockSpec((locals_, 1, 1, slots, 1), lambda s, h: (0, s, h, 0, 0)),
        ],
        out_shape=[
            jax.ShapeDtypeStruct(queries.shape, BF16),
            jax.ShapeDtypeStruct(queries.shape, BF16),
            jax.ShapeDtypeStruct((locals_, seqs, HEADS, slots, 1), F32),
        ],
        compiler_params=params("arbitrary", "arbitrary"),
        name="attend",
    )(queries, key_value, key_value, cos_q, sin_q, query_blocks, key_blocks)


def attend_back_body(
    q_ref, k_ref, v_ref, g_ref, lse_ref, cos_ref, sin_ref, qb_ref, kb_ref, ck_ref, sk_ref, dq_ref, dk_ref, dv_ref
):
    locals_, _, slots, _ = q_ref.shape
    k, v = k_ref[0], v_ref[0]
    kb = kb_ref[0]
    dk = dv = None
    for l in range(locals_):
        q, grad = q_ref[l, 0], g_ref[l]
        visible = kb <= qb_ref[l, 0]
        scores = mm(q, k, NT) * SCALE_QK - lse_ref[l, 0, 0]
        probs = jnp.where(visible, jnp.exp(jnp.where(visible, scores, MASKED_SCORE)), 0.0)
        grad_probs = mm(grad, v, NT)
        weighed = probs * grad_probs
        delta = jnp.sum(weighed, axis=-1, keepdims=True)
        grad_scores = (weighed - probs * delta).astype(BF16)
        dq = mm(grad_scores, k) * SCALE_QK
        dq = dq * cos_ref[l, 0] - pltpu.roll(dq, HDIM // 2, 1) * sin_ref[l, 0]
        dq_ref[l] = dq.astype(BF16)
        dk_part = mm(grad_scores, q, TN)
        dv_part = mm(probs.astype(BF16), grad, TN)
        dk = dk_part if dk is None else dk + dk_part
        dv = dv_part if dv is None else dv + dv_part
    dk = dk * SCALE_QK
    dk_ref[...] = (dk * ck_ref[...] - pltpu.roll(dk, HDIM // 2, 1) * sk_ref[...]).astype(BF16)
    dv_ref[...] = dv.astype(BF16)


def attend_back(s, query_rot, key_value, grad, lse, cos_q, sin_q, query_blocks, key_blocks, cos_k, sin_k):
    locals_, _, slots, width = query_rot.shape
    seq_len = key_value.shape[1]
    tab_spec = pl.BlockSpec((locals_, 1, slots, HDIM), lambda h: (0, s, 0, 0))
    key_tab = pl.BlockSpec((seq_len, HDIM), lambda h: (0, 0))
    grad_spec = pl.BlockSpec((locals_, slots, HDIM), lambda h: (0, 0, h))
    key_spec = pl.BlockSpec((seq_len, HDIM), lambda h: (0, h))
    return pl.pallas_call(
        attend_back_body,
        grid=(HEADS,),
        in_specs=[
            pl.BlockSpec((locals_, 1, slots, HDIM), lambda h: (0, s, 0, h)),
            pl.BlockSpec((1, seq_len, HDIM), lambda h: (s, 0, h)),
            pl.BlockSpec((1, seq_len, HDIM), lambda h: (s, 0, HEADS + h)),
            grad_spec,
            pl.BlockSpec((locals_, 1, 1, slots, 1), lambda h: (0, s, h, 0, 0)),
            tab_spec,
            tab_spec,
            pl.BlockSpec((locals_, 1, slots, 1), lambda h: (0, s, 0, 0)),
            pl.BlockSpec((1, 1, seq_len), lambda h: (s, 0, 0)),
            key_tab,
            key_tab,
        ],
        out_specs=[grad_spec, key_spec, key_spec],
        out_shape=[
            jax.ShapeDtypeStruct((locals_, slots, width), BF16),
            jax.ShapeDtypeStruct((seq_len, width), BF16),
            jax.ShapeDtypeStruct((seq_len, width), BF16),
        ],
        compiler_params=params("arbitrary"),
        name="attend_back",
    )(query_rot, key_value, key_value, grad, lse, cos_q, sin_q, query_blocks, key_blocks, cos_k, sin_k)


def expert_body(has_start, x_ref, c_ref, wg_ref, wu_ref, wd_ref, *refs):
    out_ref, gs_ref = refs[-2:]

    @pl.when(pl.program_id(0) == 0)
    def _():
        if has_start:
            out_ref[...] = refs[0][...]
            gs_ref[...] = refs[1][...]
        else:
            out_ref[...] = jnp.zeros_like(out_ref)
            gs_ref[...] = jnp.zeros_like(gs_ref)

    x, c = x_ref[...], c_ref[...]
    wg, wu, wd = wg_ref[...], wu_ref[...], wd_ref[...]
    gate, up = mm(x, wg), mm(x, wu)
    sig = jax.nn.sigmoid(gate)
    silu = gate * sig
    out_ref[...] += mm((silu * up).astype(BF16), wd)
    grad = mm(c, wd, NT)
    grad_gate = (grad * up * sig * (1.0 + gate * (1.0 - sig))).astype(BF16)
    grad_up = (grad * silu).astype(BF16)
    gs_ref[...] += mm(grad_gate, wg, NT) + mm(grad_up, wu, NT)


def expert_pass(rows_in, grad_in, inner, down, down_from, start=None):
    rows, width = rows_in.shape
    units = inner.shape[1] // 2
    tile = 512 if units % 512 == 0 and down_from % 512 == 0 else 256
    whole = once((rows, width), lambda i: (0, 0))
    first = down_from // tile
    more = [] if start is None else list(start)
    return pl.pallas_call(
        functools.partial(expert_body, start is not None),
        grid=(units // tile,),
        in_specs=[
            whole,
            whole,
            pl.BlockSpec((width, tile), lambda i: (0, i)),
            pl.BlockSpec((width, tile), lambda i: (0, units // tile + i)),
            pl.BlockSpec((tile, width), lambda i: (first + i, 0)),
        ]
        + [whole] * len(more),
        out_specs=[pl.BlockSpec((rows, width), lambda i: (0, 0))] * 2,
        out_shape=[jax.ShapeDtypeStruct((rows, width), F32)] * 2,
        compiler_params=params("arbitrary"),
        name="expert",
    )(rows_in, grad_in, inner, inner, down, *more)


def last_body(dk_ref, dv_ref, w_ref, table_ref, gs_ref, low_ref, down_ref, out_ref):
    width = dk_ref.shape[1]
    total = mm(dk_ref[...], w_ref[:, :width], NT) + mm(dv_ref[...], w_ref[:, width:], NT)
    total += mm(table_ref[...], gs_ref[...])
    total += mm(low_ref[...], down_ref[...], NT)
    out_ref[...] = total.astype(BF16)


def last_grad(dk, dv, kv_full, table, grad_source, grad_low, adapt_down):
    seq_len, width = dk.shape
    slots = grad_source.shape[0]
    tile = 512
    return pl.pallas_call(
        last_body,
        grid=(width // tile,),
        in_specs=[
            once((seq_len, width), lambda i: (0, 0)),
            once((seq_len, width), lambda i: (0, 0)),
            pl.BlockSpec((tile, 2 * width), lambda i: (i, 0)),
            once((seq_len, slots), lambda i: (0, 0)),
            pl.BlockSpec((slots, tile), lambda i: (0, i)),
            once((seq_len, grad_low.shape[1]), lambda i: (0, 0)),
            pl.BlockSpec((tile, grad_low.shape[1]), lambda i: (i, 0)),
        ],
        out_specs=pl.BlockSpec((seq_len, tile), lambda i: (0, i)),
        out_shape=jax.ShapeDtypeStruct((seq_len, width), BF16),
        compiler_params=params("arbitrary"),
        name="last_grad",
    )(dk, dv, kv_full, table, grad_source, grad_low, adapt_down)


def per_device(
    hidden_in,
    cotangent,
    block_ids,
    attn_routes,
    mlp_routes,
    adapter_index,
    attn_gain,
    mlp_gain,
    attn_router,
    mlp_router,
    kv_weight,
    query_weight,
    output_weight,
    inner_weight,
    down_weight,
    adapt_down,
    adapt_up,
):
    seqs, row_count, width = hidden_in.shape
    seq_len = block_ids.shape[1]
    ranks = seq_len // row_count
    locals_ = query_weight.shape[0]
    capacity = (17 * row_count * TOP + 16 * EXPERTS - 1) // (16 * EXPERTS)
    slots = ranks * capacity
    here = lax.axis_index("expert")

    kv_full = lax.all_gather(kv_weight, "dp", axis=0, tiled=True)
    query_full = lax.all_gather(query_weight, "dp", axis=1, tiled=True)
    output_full = lax.all_gather(output_weight, "dp", axis=1, tiled=True)
    cut = (FF * 3 // 4) // 256 * 256
    expert_weights = []
    for l in range(locals_):
        down_full = lax.all_gather(down_weight[l], "dp", axis=0, tiled=True)
        if l + 1 < locals_:
            pieces = [(0, lax.all_gather(inner_weight[l], "dp", axis=0, tiled=True))]
        else:
            pieces = []
            for low, high in ((0, cut), (cut, FF)):
                part = jnp.concatenate(
                    [inner_weight[l, :, low:high], inner_weight[l, :, FF + low : FF + high]], axis=1
                )
                pieces.append((low, lax.all_gather(part, "dp", axis=0, tiled=True)))
        expert_weights.append((down_full, pieces))

    routes = lax.all_gather(
        jnp.concatenate([attn_routes, mlp_routes], axis=-1), "expert", axis=1, tiled=True
    ).reshape(seqs, ranks, row_count, 2, TOP)
    adapters = lax.all_gather(adapter_index, "dp", axis=0, tiled=True)
    expert_ids = jnp.arange(EXPERTS, dtype=jnp.int32)
    onehot = (routes[..., None] == expert_ids).astype(F32)
    hits = jnp.sum(onehot, axis=4)
    earlier = (
        jnp.arange(row_count)[:, None] > jnp.arange(row_count)[None, :]
    ).astype(BF16)
    before = jnp.einsum("ut,sptke->spuke", earlier, hits.astype(BF16), preferred_element_type=F32)
    place = jnp.sum(onehot * before[..., None, :], axis=-1).astype(jnp.int32)
    attn_all, mlp_all = routes[:, :, :, 0], routes[:, :, :, 1]
    attn_place, mlp_place = place[:, :, :, 0], place[:, :, :, 1]
    source = jnp.arange(ranks, dtype=jnp.int32)[None, :, None, None]
    which = jnp.arange(seqs, dtype=jnp.int32)[:, None, None, None]

    local_a = attn_all - here * locals_
    is_local = (local_a >= 0) & (local_a < locals_)
    slot_a = jnp.where(is_local, local_a * slots + source * capacity + attn_place, -1)
    slot_a = slot_a.reshape(seqs, seq_len, TOP)
    slot_iota = jnp.arange(locals_ * slots, dtype=jnp.int32)
    spread_a = (
        (slot_iota[None, :, None] == slot_a[:, None, :, 0])
        | (slot_iota[None, :, None] == slot_a[:, None, :, 1])
    ).astype(BF16)
    collect_a = (
        (slot_iota[None, None, :] == slot_a[:, :, 0, None])
        | (slot_iota[None, None, :] == slot_a[:, :, 1, None])
    ).astype(BF16)

    def own(array):
        return lax.dynamic_index_in_dim(array, here, 1, keepdims=False)

    attn_own, attn_own_place = own(attn_all), own(attn_place)
    mlp_own, mlp_own_place = own(mlp_all), own(mlp_place)
    own_slot = attn_own * capacity + attn_own_place
    own_iota = jnp.arange(EXPERTS * capacity, dtype=jnp.int32)
    own_spread_a = (
        (own_iota[None, :, None] == own_slot[:, None, :, 0])
        | (own_iota[None, :, None] == own_slot[:, None, :, 1])
    ).astype(BF16)
    own_collect_a = (
        (own_iota[None, None, :] == own_slot[:, :, 0, None])
        | (own_iota[None, None, :] == own_slot[:, :, 1, None])
    ).astype(BF16)
    mlp_rows = ranks * seqs * capacity
    mlp_iota = jnp.arange(mlp_rows, dtype=jnp.int32)
    own_spread_m, own_collect_m, other_sum = [], [], []
    for l in range(locals_):
        ids = jnp.where(
            mlp_own % locals_ == l,
            (mlp_own // locals_) * (seqs * capacity) + which[:, 0] * capacity + mlp_own_place,
            -1,
        ).reshape(seqs * row_count, TOP)
        own_spread_m.append(
            ((mlp_iota[:, None] == ids[None, :, 0]) | (mlp_iota[:, None] == ids[None, :, 1])).astype(BF16)
        )
        own_collect_m.append(
            ((mlp_iota[None, :] == ids[:, 0, None]) | (mlp_iota[None, :] == ids[:, 1, None])).astype(BF16)
        )
        ids = jnp.where(
            mlp_all == here * locals_ + l,
            source * (seqs * capacity) + which * capacity + mlp_place,
            -1,
        ).reshape(seqs * seq_len, TOP)
        table = (
            (mlp_iota[:, None] == ids[None, :, 0]) | (mlp_iota[:, None] == ids[None, :, 1])
        ).astype(BF16)
        both = jnp.sum(mlp_all, axis=-1).reshape(seqs * seq_len, 1).astype(BF16)
        sums = mm(table, jnp.concatenate([both, jnp.ones_like(both)], axis=1))
        other_sum.append((sums[:, :1], sums[:, 1:]))

    flat_cot = cotangent.reshape(seqs * row_count, width)
    cot_rows = [send(mm(own_spread_m[l], flat_cot).astype(BF16)) for l in range(locals_)]

    everyone = gather_line(
        hidden_in,
        "expert",
        ranks,
        lambda total, piece, at: lax.dynamic_update_slice(total, piece[:, None], (0, at, 0, 0)),
        jnp.zeros((seqs, ranks, row_count, width), BF16),
    ).reshape(seqs, seq_len, width)
    tokens_all = everyone.astype(F32)
    scale_all = rms_scale(tokens_all)
    normed_low = (tokens_all * scale_all * attn_gain).astype(BF16)
    router_parts = jnp.concatenate(three_parts(attn_gain[:, None] * attn_router.astype(F32)), axis=1)
    parts = mm(everyone.reshape(seqs * seq_len, width), router_parts).reshape(seqs, seq_len, 3, EXPERTS)
    logits = scale_all * (parts[:, :, 0] + (parts[:, :, 1] + parts[:, :, 2]))
    onehot_a = onehot[:, :, :, 0].reshape(seqs, seq_len, TOP, EXPERTS)
    gap = jnp.sum((onehot_a[:, :, 0] - onehot_a[:, :, 1]) * logits, axis=-1)

    flat_routes = attn_all.reshape(seqs, seq_len, TOP)
    places = jnp.arange(seq_len, dtype=jnp.int32)
    columns = [
        block_ids,
        jnp.broadcast_to(places // 128, block_ids.shape),
        jnp.broadcast_to(places % 128, block_ids.shape),
        jnp.sum(flat_routes, axis=-1),
        flat_routes[..., 0],
    ]
    known = jnp.stack([c.astype(BF16) for c in columns] + list(three_parts(gap)), axis=-1)
    known = jnp.einsum("srt,stc->src", spread_a, known, preferred_element_type=F32)
    known = known.reshape(seqs, locals_, slots, known.shape[-1]).transpose(1, 0, 2, 3)
    self_id = (here * locals_ + jnp.arange(locals_)).astype(F32)[:, None, None]
    slot_blocks = known[..., 0].astype(jnp.int32)
    slot_place = known[..., 1] * 128.0 + known[..., 2]
    slot_other = known[..., 3] - self_id
    slot_gap = known[..., 5] + (known[..., 6] + known[..., 7])
    slot_gap = jnp.where(known[..., 4] == self_id, slot_gap, -slot_gap)
    gate_a = jax.nn.sigmoid(slot_gap)
    expert_f = expert_ids.astype(F32)
    pick_a = (expert_f == self_id[..., None]).astype(F32) - (expert_f == slot_other[..., None]).astype(F32)
    weigh_a = pick_a * (gate_a * jax.nn.sigmoid(-slot_gap))[..., None]
    cos_q, sin_q = angle_tables(slot_place)
    cos_k, sin_k = angle_tables(places)
    query_blocks = slot_blocks[..., None]
    key_blocks = block_ids[:, None, :]

    flat_low = normed_low.reshape(seqs * seq_len, width)
    own_adapter = (
        jnp.arange(NADAPT * RANK, dtype=jnp.int32)[None, :] // RANK == adapter_index[:, None]
    )
    low_rank = mm(flat_low, adapt_down).reshape(seqs, seq_len, NADAPT * RANK)
    low_rank = jnp.where(own_adapter[:, None, :], low_rank, 0.0).astype(BF16)
    key_value = make_key_value(
        flat_low, low_rank.reshape(seqs * seq_len, -1), kv_full, adapt_up, cos_k, sin_k, seqs
    ).reshape(seqs, seq_len, 2 * width)

    picked = jnp.einsum(
        "slrt,std->lsrd",
        spread_a.reshape(seqs, locals_, slots, seq_len),
        normed_low,
        preferred_element_type=F32,
    ).astype(BF16)
    queries = jnp.stack(
        [mm(picked[l].reshape(seqs * slots, width), query_full[l]).astype(BF16) for l in range(locals_)]
    ).reshape(locals_, seqs, slots, width)
    query_rot, attended, lse = attend(queries, key_value, cos_q, sin_q, query_blocks, key_blocks)
    projected = [
        mm(attended[l].reshape(seqs * slots, width), output_full[l]).reshape(seqs, slots, width)
        for l in range(locals_)
    ]
    order = np.arange(locals_ * slots).reshape(locals_, ranks, capacity).transpose(1, 0, 2).reshape(-1)
    to_send = jnp.asarray(np.eye(locals_ * slots)[order], BF16)
    to_slots = jnp.asarray(np.eye(locals_ * slots)[order].T, BF16)
    tokens = hidden_in.astype(F32)
    upstream = cotangent.astype(F32)
    middles = []
    for s in range(seqs):
        gated = jnp.concatenate(
            [(projected[l][s] * gate_a[l, s][:, None]).astype(BF16) for l in range(locals_)], axis=0
        )
        back = send(mm(to_send, gated).astype(BF16))
        middles.append(tokens[s] + mm(own_collect_a[s], back))
    projected_low = [p.astype(BF16) for p in projected]
    middle = jnp.stack(middles)
    scale_two = rms_scale(middle)
    normed_two_low = (middle * scale_two * mlp_gain).astype(BF16).reshape(seqs * row_count, width)

    final = middle.reshape(seqs * row_count, width)
    grad_normed_two = jnp.zeros((seqs * row_count, width), F32)
    mlp_back = []
    for l in range(locals_):
        rows_in = send(mm(own_spread_m[l], normed_two_low).astype(BF16))
        slot_logits = mm(rows_in, mlp_router)
        me = (here * locals_ + l).astype(F32)
        pick_m = (expert_f[None, :] == me).astype(F32) - (
            expert_f[None, :] == other_sum[l][0] - me
        ).astype(F32)
        gap_m = jnp.sum(pick_m * slot_logits, axis=-1, keepdims=True)
        gate_m = jax.nn.sigmoid(gap_m)
        cot = cot_rows[l].astype(F32)
        grad_rows = (gate_m * cot).astype(BF16)
        down_full, pieces = expert_weights[l]
        made = None
        for low, inner_full in pieces:
            made = expert_pass(rows_in, grad_rows, inner_full, down_full, low, made)
        expert_out, grad_source = made
        dots = jnp.sum(cot * expert_out, axis=-1, keepdims=True)
        weigh_m = pick_m * (dots * gate_m * jax.nn.sigmoid(-gap_m))
        grad_source = grad_source + jnp.dot(weigh_m, mlp_router.astype(F32).T, precision=PRECISE)
        grad_back = send(grad_source.astype(BF16))
        grad_normed_two = grad_normed_two + mm(own_collect_m[l], grad_back)
        mlp_back.append((gate_m * expert_out).astype(BF16))
    for l in range(locals_):
        final = final + mm(own_collect_m[l], send(mlp_back[l]))
    layer_out = final.astype(BF16).reshape(seqs, row_count, width)
    grad_normed_two = grad_normed_two.reshape(seqs, row_count, width)
    grad_middle = upstream + norm_back(middle, scale_two, mlp_gain, grad_normed_two)

    input_grads, down_pieces, up_pieces = [], [], []
    attn_router_f = attn_router.astype(F32)
    for s in range(seqs):
        arrived = send(mm(own_spread_a[s], grad_middle[s].astype(BF16)).astype(BF16))
        grad_rows = mm(to_slots, arrived).reshape(locals_, slots, width)
        grad_attended, extra = [], []
        for l in range(locals_):
            grad_projected = (grad_rows[l] * gate_a[l, s][:, None]).astype(BF16)
            grad_attended.append(mm(grad_projected, output_full[l], NT).astype(BF16))
            dots = jnp.sum(grad_rows[l] * projected_low[l][s].astype(F32), axis=-1, keepdims=True)
            extra.append(weigh_a[l, s] * dots)
        dq, dk, dv = attend_back(
            s, query_rot, key_value, jnp.stack(grad_attended), lse, cos_q, sin_q, query_blocks,
            key_blocks, cos_k, sin_k,
        )
        grad_source = jnp.concatenate(
            [
                (
                    mm(dq[l], query_full[l], NT) + jnp.dot(extra[l], attn_router_f.T, precision=PRECISE)
                ).astype(BF16)
                for l in range(locals_)
            ],
            axis=0,
        )
        grad_low = mm(dk, adapt_up[:width]) + mm(dv, adapt_up[width:])
        grad_low = jnp.where(own_adapter[s][None, :], grad_low, 0.0).astype(BF16)
        part = last_grad(dk, dv, kv_full, collect_a[s], grad_source, grad_low, adapt_down)
        grad_normed = lax.psum_scatter(part, "expert", scatter_dimension=0, tiled=True).astype(F32)
        input_grads.append(
            grad_middle[s] + norm_back(tokens[s], rms_scale(tokens[s]), attn_gain, grad_normed)
        )
        first = adapter_index[s] * RANK
        down_pieces.append(lax.dynamic_slice_in_dim(mm(grad_low, normed_low[s], TN), first, RANK, 0))
        up_piece = jnp.concatenate([mm(low_rank[s], dk, TN), mm(low_rank[s], dv, TN)], axis=1)
        up_pieces.append(lax.dynamic_slice_in_dim(up_piece, first, RANK, 0))

    groups = adapters.shape[0] // seqs
    down_part = width // (groups * ranks)
    pieces = jnp.concatenate(
        [
            jnp.stack(down_pieces).reshape(seqs, RANK, groups, ranks, down_part),
            jnp.stack(up_pieces).reshape(seqs, RANK, groups, ranks, 2 * down_part),
        ],
        axis=-1,
    )
    pieces = pieces.transpose(3, 2, 0, 1, 4).reshape(ranks, groups * seqs * RANK, 3 * down_part)
    pieces = jnp.sum(send(pieces), axis=0).reshape(groups, seqs * RANK, 3 * down_part)
    pieces = lax.all_to_all(pieces, "dp", split_axis=0, concat_axis=0, tiled=True)
    pieces = pieces.reshape(groups * seqs, RANK, 3 * down_part)
    belongs = (adapters[:, None] == jnp.arange(NADAPT, dtype=jnp.int32)[None, :]).astype(F32)
    sums = jnp.einsum("qkf,qa->fak", pieces, belongs, precision=PRECISE).reshape(3 * down_part, NADAPT * RANK)
    return (layer_out, jnp.stack(input_grads), sums[:down_part], sums[down_part:])


def solution(mesh):
    return jax.shard_map(
        per_device,
        mesh=mesh,
        in_specs=(
            P("dp", "expert", None),
            P("dp", "expert", None),
            P("dp", None),
            P("dp", "expert", None),
            P("dp", "expert", None),
            P("dp"),
            P(),
            P(),
            P(),
            P(),
            P("dp", None),
            P("expert", "dp", None),
            P("expert", "dp", None),
            P("expert", "dp", None),
            P("expert", "dp", None),
            P(),
            P(),
        ),
        out_specs=(
            P("dp", "expert", None),
            P("dp", "expert", None),
            P(("dp", "expert"), None),
            P(("dp", "expert"), None),
        ),
        check_vma=False,
    )
```

time: 3510 us -> 1620 us (0.46)
  waiting for transfers between devices: 1370 us -> 586 us
  matrix products: 681 us -> 205 us
  Pallas kernels: 0 us -> 439 us
  local copies, waits for them, and re-layouts: 455 us -> 63.2 us
  blocking collectives: 470 us -> 105 us
  other arithmetic: 363 us -> 91.8 us
    dot_general x64 -> x56, matrix products: 681 us -> 205 us  [the longest x46 181 us: mm(): return lax.dot_general(left, right, dims, preferred_element_type=F32)]
    pallas_call x0 -> x9, Pallas kernels: none -> 439 us  [the longest x3 187 us: expert_pass(): pl.pallas_call(functools.partial(expert_body, start is not None), grid=(u...]
    all_to_all x7 -> x1, blocking collectives: 470 us -> 43 us  [send(): lax.all_to_all(buffer, 'expert', split_axis=0, concat_axis=0, tiled=True)]
    all_gather x7 -> x8, waiting for transfers between devices: 475 us -> 121 us  [the longest x2 121 us: per_device(): pieces.append((low, lax.all_gather(part, 'dp', axis=0, tiled=True)))]
    all_to_all x17 -> x13, waiting for transfers between devices: 647 us -> 341 us  [the longest x12 341 us: send(): lax.all_to_all(buffer, 'expert', split_axis=0, concat_axis=0, tiled=True)]
    unnamed x12 -> x10, waiting for transfers between devices: 136 us -> 2.68 us
    ppermute x0 -> x6, waiting for transfers between devices: none -> 121 us  [the longest x3 121 us: gather_line(): from_right.append(lax.ppermute(from_right[-1], axis, leftward))]
    reduce_scatter x3 -> x2, waiting for transfers between devices: 113 us -> 0.01 us  [per_device(): lax.psum_scatter(part, 'expert', scatter_dimension=0, tiled=True)]
  transfers between devices with their start and end apart: 28 -> 29, of which waited for: 22 -> 12; matrix products, arithmetic and copies ran while one was open for 27% -> 17% of each run, Pallas kernels for 0% -> 23%
where the time goes in v1:
time: 1620 us; the launch traced here: 1610 us
  waiting for transfers between devices  586 us (36%)
  Pallas kernels  439 us (27%)
  matrix products  205 us (13%)
  blocking collectives  105 us (6%)
  starting transfers between devices  99.6 us (6%)
  other arithmetic  91.8 us (6%)
  local copies, waits for them, and re-layouts  63.2 us (4%)
  between operations  18.1 us (1%)
    all_to_all x12, waiting for transfers between devices, send(): lax.all_to_all(buffer, 'expert', split_axis=0, concat_axis=0, tiled=True)  341 us
    pallas_call x3, Pallas kernels, expert_pass(): pl.pallas_call(functools.partial(expert_body, start is not None), grid=(u...  187 us
    dot_general x46, matrix products, mm(): return lax.dot_general(left, right, dims, preferred_element_type=F32)  181 us
    ppermute x3, waiting for transfers between devices, gather_line(): from_right.append(lax.ppermute(from_right[-1], axis, leftward))  121 us
    all_gather x2, waiting for transfers between devices, per_device(): pieces.append((low, lax.all_gather(part, 'dp', axis=0, tiled=True)))  121 us
    pallas_call x2, Pallas kernels, attend_back(): pl.pallas_call(attend_back_body, grid=(HEADS,), in_specs=[pl.BlockSpec((l...  88.3 us
    all_to_all x12, starting transfers between devices, send(): lax.all_to_all(buffer, 'expert', split_axis=0, concat_axis=0, tiled=True)  78.4 us
    pallas_call x2, Pallas kernels, last_grad(): pl.pallas_call(last_body, grid=(width // tile,), in_specs=[once((seq_len,...  58.7 us
  transfers between devices with their start and end apart: 29, of which 12 were waited for; matrix products, arithmetic and copies ran while one was open for 17% of the time, Pallas kernels for 23%

profile of v1, /device:TPU:9, one launch (start us, length us, event | category | flops | bytes accessed | tf_op | source)
XLA Modules:
  0.0 1606.8 jit_solution(2982123618240826344)
XLA Ops:
  34.8 52.4 %all_gather.30 = s32[2,1024,4]{1,2,0:T(4,128)S(1)} all-gather(s32[2,256,4]{1,2,0:T(4,128)S(1)} %pad_add_fusion), channel_id=1, replica_groups=mesh['dp'=8,'expert'=4] {'expert'}, dimensions={1}, use_global_device_ids=true | all-gather | bytes 40960 | tf_op jit(solution)/shard_map/all_gather | solution.py:375
  108.1 84.9 %collective-permute-done.2 = bf16[2,256,2048]{2,1,0:T(8,128)(2,1)} collective-permute-done((bf16[2,256,2048]{2,1,0:T(8,128)(2,1)}, bf16[2,256,2048]{2,1,0:T(8,128)(2,1)}, u32[]{:S(2)}, u32[]{:S(2)}) %collective-permute-start.2) | collective-permute-done | bytes 2097184 | tf_op jit(solution)/shard_map/ppermute | solution.py:82
  204.4 36.5 %collective-permute-done.3 = bf16[2,256,2048]{2,1,0:T(8,128)(2,1)} collective-permute-done((bf16[2,256,2048]{2,1,0:T(8,128)(2,1)}, bf16[2,256,2048]{2,1,0:T(8,128)(2,1)}, u32[]{:S(2)}, u32[]{:S(2)}) %collective-permute-start.3) | collective-permute-done | bytes 2097184 | tf_op jit(solution)/shard_map/ppermute | solution.py:82
  280.4 10.3 convert_bitcast_fusion
  316.9 53.2 %key_value.1 = bf16[2048,4096]{1,0:T(8,128)(2,1)} custom-call(bf16[2048,2048]{1,0:T(8,128)(2,1)} %fusion.1.x_ref, bf16[2048,128]{1,0:T(8,128)(2,1)} %bitcast.451, bf16[2048,4096]{1,0:T(8,128)(2,1)} %all-gather.14.cloned.1.call-done.w_ref, bf16[4096,128]{1,0:T(8,128)(2,1)} %up_ref.1, f32[1024,128]{1,0:T(8,128)} %get-tuple-element.133.cos_ref.ck_ref, ...), custom_call_target="tpu_custom_call" | custom-call | tf_op jit(solution)/shard_map/key_value/pallas_call | solution.py:117
  370.1 51.5 %attend.1 = (bf16[2,2,272,2048]{3,2,1,0:T(8,128)(2,1)}, bf16[2,2,272,2048]{3,2,1,0:T(8,128)(2,1)}, f32[2,2,16,272,1]{4,3,2,1,0:T(8,128)}) custom-call(bf16[2,2,272,2048]{3,2,1,0:T(8,128)(2,1)} %pad_maximum_fusion.q_ref, bf16[2,1024,4096]{2,1,0:T(8,128)(2,1)} %bitcast.423, bf16[2,1024,4096]{2,1,0:T(8,128)(2,1)} %bitcast.424, ...), custom_call_target="tpu_custom_call" | custom-call | tf_op jit(solution)/shard_map/attend/pallas_call | solution.py:161
  426.8 10.3 fusion.244
  460.0 40.7 %all-to-all-done = bf16[4,136,2048]{2,1,0:T(8,128)(2,1)S(1)} async-done(((bf16[4,136,2048]{2,1,0:T(8,128)(2,1)}), bf16[4,136,2048]{2,1,0:T(8,128)(2,1)S(1)}, u32[]{:S(2)}, u32[]{:S(2)}) %all-to-all-start) | async-done | bytes 2228256 | tf_op jit(solution)/shard_map/all_to_all | solution.py:91
  515.0 42.3 %all-to-all-done.1 = bf16[4,136,2048]{2,1,0:T(8,128)(2,1)} async-done(((bf16[4,136,2048]{2,1,0:T(8,128)(2,1)}), bf16[4,136,2048]{2,1,0:T(8,128)(2,1)}, u32[]{:S(2)}, u32[]{:S(2)}) %all-to-all-start.1) | async-done | bytes 2228256 | tf_op jit(solution)/shard_map/all_to_all | solution.py:91
  580.1 31.4 %all-to-all-done.3 = bf16[4,136,2048]{2,1,0:T(8,128)(2,1)S(1)} async-done(((bf16[4,136,2048]{2,1,0:T(8,128)(2,1)}), bf16[4,136,2048]{2,1,0:T(8,128)(2,1)S(1)}, u32[]{:S(2)}, u32[]{:S(2)}) %all-to-all-start.3) | async-done | bytes 2228256 | tf_op jit(solution)/shard_map/all_to_all | solution.py:91
  624.9 42.2 %all-to-all-done.2 = bf16[4,136,2048]{2,1,0:T(8,128)(2,1)S(1)} async-done(((bf16[4,136,2048]{2,1,0:T(8,128)(2,1)}), bf16[4,136,2048]{2,1,0:T(8,128)(2,1)S(1)}, u32[]{:S(2)}, u32[]{:S(2)}) %all-to-all-start.2) | async-done | bytes 2228256 | tf_op jit(solution)/shard_map/all_to_all | solution.py:91
  681.3 88.6 %expert.3 = (f32[544,2048]{1,0:T(8,128)}, f32[544,2048]{1,0:T(8,128)}) custom-call(bf16[544,2048]{1,0:T(8,128)(2,1)} %bitcast.438, bf16[544,2048]{1,0:T(8,128)(2,1)} %fusion.18.c_ref, bf16[2048,11264]{1,0:T(8,128)(2,1)} %bitcast.429, bf16[2048,11264]{1,0:T(8,128)(2,1)} %bitcast.430, bf16[5632,2048]{1,0:T(8,128)(2,1)} %bitcast.442), custom_call_target="tpu_custom_call" | custom-call | tf_op jit(solution)/shard_map/expert/pallas_call | solution.py:281
  788.1 113.1 %all-gather.20.cloned.1.call-done.wg_ref.wu_ref = bf16[2048,8192]{1,0:T(8,128)(2,1)} async-done(((bf16[256,8192]{1,0:T(8,128)(2,1)}), bf16[2048,8192]{1,0:T(8,128)(2,1)}) %all-gather.20.cloned.1.call-update) | async-done | bytes 33554448 | tf_op jit(solution)/shard_map/all_gather | solution.py:372
  901.2 66.4 %expert.4 = (f32[544,2048]{1,0:T(8,128)}, f32[544,2048]{1,0:T(8,128)}) custom-call(bf16[544,2048]{1,0:T(8,128)(2,1)} %bitcast.435, bf16[544,2048]{1,0:T(8,128)(2,1)} %fusion.20.c_ref, bf16[2048,8192]{1,0:T(8,128)(2,1)} %all-gather.20.cloned.1.call-done.wg_ref.wu_ref, bf16[2048,8192]{1,0:T(8,128)(2,1)} %all-gather.20.cloned.1.call-done.wg_ref.wu_ref, ...), custom_call_target="tpu_custom_call" | custom-call | tf_op jit(solution)/shard_map/expert/pallas_call | solution.py:281
  975.3 32.2 %expert.5 = (f32[544,2048]{1,0:T(8,128)}, f32[544,2048]{1,0:T(8,128)}) custom-call(bf16[544,2048]{1,0:T(8,128)(2,1)} %bitcast.436, bf16[544,2048]{1,0:T(8,128)(2,1)} %fusion.20.c_ref, bf16[2048,3072]{1,0:T(8,128)(2,1)} %all-gather.18.cloned.1.call-done.wg_ref.wu_ref, bf16[2048,3072]{1,0:T(8,128)(2,1)} %all-gather.18.cloned.1.call-done.wg_ref.wu_ref, ...), custom_call_target="tpu_custom_call" | custom-call | tf_op jit(solution)/shard_map/expert/pallas_call | solution.py:281
  1026.6 41.9 %all-to-all-done.9 = bf16[4,136,2048]{2,1,0:T(8,128)(2,1)S(1)} async-done(((bf16[4,136,2048]{2,1,0:T(8,128)(2,1)}), bf16[4,136,2048]{2,1,0:T(8,128)(2,1)S(1)}, u32[]{:S(2)}, u32[]{:S(2)}) %all-to-all-start.9) | async-done | bytes 2228256 | tf_op jit(solution)/shard_map/all_to_all | solution.py:91
  1093.7 42.9 %all-to-all-done.10 = bf16[4,136,2048]{2,1,0:T(8,128)(2,1)S(1)} async-done(((bf16[4,136,2048]{2,1,0:T(8,128)(2,1)}), bf16[4,136,2048]{2,1,0:T(8,128)(2,1)S(1)}, u32[]{:S(2)}, u32[]{:S(2)}) %all-to-all-start.10) | async-done | bytes 2228256 | tf_op jit(solution)/shard_map/all_to_all | solution.py:91
  1154.2 38.6 %all-to-all-done.11 = bf16[4,136,2048]{2,1,0:T(8,128)(2,1)} async-done(((bf16[4,136,2048]{2,1,0:T(8,128)(2,1)}), bf16[4,136,2048]{2,1,0:T(8,128)(2,1)}, u32[]{:S(2)}, u32[]{:S(2)}) %all-to-all-start.11) | async-done | bytes 2228256 | tf_op jit(solution)/shard_map/all_to_all | solution.py:91
  1211.4 44.1 %attend_back.3 = (bf16[2,272,2048]{2,1,0:T(8,128)(2,1)}, bf16[1024,2048]{1,0:T(8,128)(2,1)}, bf16[1024,2048]{1,0:T(8,128)(2,1)}) custom-call(bf16[2,2,272,2048]{3,2,1,0:T(8,128)(2,1)} %get-tuple-element.26.q_ref, bf16[2,1024,4096]{2,1,0:T(8,128)(2,1)} %bitcast.425, bf16[2,1024,4096]{2,1,0:T(8,128)(2,1)} %bitcast.426, ...), custom_call_target="tpu_custom_call" | custom-call | tf_op jit(solution)/shard_map/attend_back/pallas_call | solution.py:223
  1280.3 29.2 %last_grad.3 = bf16[1024,2048]{1,0:T(8,128)(2,1)} custom-call(bf16[1024,2048]{1,0:T(8,128)(2,1)} %get-tuple-element.31.dk_ref, bf16[1024,2048]{1,0:T(8,128)(2,1)} %get-tuple-element.32.dv_ref, bf16[2048,4096]{1,0:T(8,128)(2,1)} %all-gather.14.cloned.1.call-done.w_ref, bf16[1024,544]{1,0:T(8,128)(2,1)} %get-tuple-element.102.table_ref, ...), custom_call_target="tpu_custom_call" | custom-call | tf_op jit(solution)/shard_map/last_grad/pallas_call | solution.py:311
  1335.4 44.2 %attend_back.2 = (bf16[2,272,2048]{2,1,0:T(8,128)(2,1)}, bf16[1024,2048]{1,0:T(8,128)(2,1)}, bf16[1024,2048]{1,0:T(8,128)(2,1)}) custom-call(bf16[2,2,272,2048]{3,2,1,0:T(8,128)(2,1)} %get-tuple-element.26.q_ref, bf16[2,1024,4096]{2,1,0:T(8,128)(2,1)} %bitcast.427, bf16[2,1024,4096]{2,1,0:T(8,128)(2,1)} %bitcast.428, ...), custom_call_target="tpu_custom_call" | custom-call | tf_op jit(solution)/shard_map/attend_back/pallas_call | solution.py:223
  1404.3 29.4 %last_grad.2 = bf16[1024,2048]{1,0:T(8,128)(2,1)} custom-call(bf16[1024,2048]{1,0:T(8,128)(2,1)} %get-tuple-element.28.dk_ref, bf16[1024,2048]{1,0:T(8,128)(2,1)} %get-tuple-element.29.dv_ref, bf16[2048,4096]{1,0:T(8,128)(2,1)} %all-gather.14.cloned.1.call-done.w_ref, bf16[1024,544]{1,0:T(8,128)(2,1)} %get-tuple-element.101.table_ref, ...), custom_call_target="tpu_custom_call" | custom-call | tf_op jit(solution)/shard_map/last_grad/pallas_call | solution.py:311
  1449.1 43.0 %all_to_all.146 = f32[4,256,192]{1,2,0:T(8,128)S(1)} all-to-all(f32[4,256,192]{1,2,0:T(8,128)S(1)} %copy.152), channel_id=1, replica_groups=mesh['dp'=8,'expert'=4] {'expert'}, dimensions={0} | all-to-all | bytes 1572864 | tf_op jit(solution)/shard_map/all_to_all | solution.py:91
  1515.0 60.8 %all-to-all-done.7 = bf16[4,136,2048]{2,1,0:T(8,128)(2,1)S(1)} async-done(((bf16[4,136,2048]{2,1,0:T(8,128)(2,1)}), bf16[4,136,2048]{2,1,0:T(8,128)(2,1)S(1)}, u32[]{:S(2)}, u32[]{:S(2)}) %all-to-all-start.7) | async-done | bytes 2228256 | tf_op jit(solution)/shard_map/all_to_all | solution.py:91
  (475 shorter events, 458.4 us)
Async XLA Ops:
  7.2 292.3 %all-gather.12.cloned.1.call-start = ((), (), s32[]{:S(2)}) async-start(), calls=%async_computation.16 | async-start | bytes 18874368 | tf_op jit(solution)/shard_map/all_gather | solution.py:358
  7.9 309.0 %all-gather.14.cloned.1.call-start = ((), (), s32[]{:S(2)}) async-start(), calls=%async_computation.17 | async-start | bytes 18874368 | tf_op jit(solution)/shard_map/all_gather | solution.py:357
  8.7 418.1 %all-gather.16.cloned.1.call-start = ((), (), s32[]{:S(2)}) async-start(), calls=%async_computation.18 | async-start | bytes 18874368 | tf_op jit(solution)/shard_map/all_gather | solution.py:359
  9.4 671.9 %all-gather.24.cloned.1.call-start = ((), (), s32[]{:S(2)}) async-start(), calls=%async_computation.24 | async-start | bytes 25952256 | tf_op jit(solution)/shard_map/all_gather | solution.py:363
  15.6 665.7 %all-gather.22.cloned.1.call-start = ((), (), s32[]{:S(2)}) async-start(), calls=%async_computation.23 | async-start | bytes 51904512 | tf_op jit(solution)/shard_map/all_gather | solution.py:365
  21.6 766.5 %all-gather.26.cloned.1.call-start = ((), (), s32[]{:S(2)}) async-start(), calls=%async_computation.25 | async-start | bytes 25952256 | tf_op jit(solution)/shard_map/all_gather | solution.py:363
  22.1 879.0 %all-gather.20.cloned.1.call-start = ((), (), s32[]{:S(2)}) async-start(), calls=%async_computation.20 | async-start | bytes 37748736 | tf_op jit(solution)/shard_map/all_gather | solution.py:372
  29.4 69.6 %collective-permute-start.1 = (bf16[2,256,2048]{2,1,0:T(8,128)(2,1)S(1)}, bf16[2,256,2048]{2,1,0:T(8,128)(2,1)}, u32[]{:S(2)}, u32[]{:S(2)}) collective-permute-start(bf16[2,256,2048]{2,1,0:T(8,128)(2,1)S(1)} %copy-done.22), channel_id=1, source_target_pairs={{1,0},{2,1},{3,2},{5,4},{6,5},{7,6},{9,8},{10,9},{11,10},{13,12},{... | collective-permute-start | bytes 6291464 | tf_op jit(solution)/shard_map/ppermute | solution.py:82
  31.4 72.6 %collective-permute-start = (bf16[2,256,2048]{2,1,0:T(8,128)(2,1)S(1)}, bf16[2,256,2048]{2,1,0:T(8,128)(2,1)}, u32[]{:S(2)}, u32[]{:S(2)}) collective-permute-start(bf16[2,256,2048]{2,1,0:T(8,128)(2,1)S(1)} %copy-done.22), channel_id=1, source_target_pairs={{0,1},{1,2},{2,3},{4,5},{5,6},{6,7},{8,9},{9,10},{10,11},{12,13},{... | collective-permute-start | bytes 6291464 | tf_op jit(solution)/shard_map/ppermute | solution.py:81
  94.5 356.0 %all-to-all-start.6 = ((bf16[4,136,2048]{2,1,0:T(8,128)(2,1)}), bf16[4,136,2048]{2,1,0:T(8,128)(2,1)}, u32[]{:S(2)}, u32[]{:S(2)}) async-start(bf16[4,136,2048]{2,1,0:T(8,128)(2,1)} %bitcast.459), calls=%async_computation.6 | async-start | bytes 4456448 | tf_op jit(solution)/shard_map/all_to_all | solution.py:91
  99.0 876.3 %all-gather.18.cloned.1.call-start = ((), (), s32[]{:S(2)}) async-start(), calls=%async_computation.19 | async-start | bytes 14155776 | tf_op jit(solution)/shard_map/all_gather | solution.py:372
  99.1 94.0 %collective-permute-start.2 = (bf16[2,256,2048]{2,1,0:T(8,128)(2,1)}, bf16[2,256,2048]{2,1,0:T(8,128)(2,1)}, u32[]{:S(2)}, u32[]{:S(2)}) collective-permute-start(bf16[2,256,2048]{2,1,0:T(8,128)(2,1)} %collective-permute-done.1), channel_id=1, source_target_pairs={{1,0},{2,1},{3,2},{5,4},{6,5},{7,6},{9,8},{10,9},{11,10},{13,12},{... | collective-permute-start | bytes 6291464 | tf_op jit(solution)/shard_map/ppermute | solution.py:82
  104.0 92.0 %collective-permute-start.4 = (bf16[2,256,2048]{2,1,0:T(8,128)(2,1)}, bf16[2,256,2048]{2,1,0:T(8,128)(2,1)}, u32[]{:S(2)}, u32[]{:S(2)}) collective-permute-start(bf16[2,256,2048]{2,1,0:T(8,128)(2,1)} %collective-permute-done), channel_id=1, source_target_pairs={{0,1},{1,2},{2,3},{4,5},{5,6},{6,7},{8,9},{9,10},{10,11},{12,13},{... | collective-permute-start | bytes 6291464 | tf_op jit(solution)/shard_map/ppermute | solution.py:81
  502.1 55.2 %all-to-all-start.1 = ((bf16[4,136,2048]{2,1,0:T(8,128)(2,1)}), bf16[4,136,2048]{2,1,0:T(8,128)(2,1)}, u32[]{:S(2)}, u32[]{:S(2)}) async-start(bf16[4,136,2048]{2,1,0:T(8,128)(2,1)} %bitcast.448), calls=%async_computation.1 | async-start | bytes 4456448 | tf_op jit(solution)/shard_map/all_to_all | solution.py:91
  557.3 54.2 %all-to-all-start.3 = ((bf16[4,136,2048]{2,1,0:T(8,128)(2,1)}), bf16[4,136,2048]{2,1,0:T(8,128)(2,1)S(1)}, u32[]{:S(2)}, u32[]{:S(2)}) async-start(bf16[4,136,2048]{2,1,0:T(8,128)(2,1)} %bitcast.461), calls=%async_computation.3 | async-start | bytes 4456448 | tf_op jit(solution)/shard_map/all_to_all | solution.py:91
  612.8 54.3 %all-to-all-start.2 = ((bf16[4,136,2048]{2,1,0:T(8,128)(2,1)}), bf16[4,136,2048]{2,1,0:T(8,128)(2,1)S(1)}, u32[]{:S(2)}, u32[]{:S(2)}) async-start(bf16[4,136,2048]{2,1,0:T(8,128)(2,1)} %bitcast.463), calls=%async_computation.2 | async-start | bytes 4456448 | tf_op jit(solution)/shard_map/all_to_all | solution.py:91
  668.5 109.4 %all-to-all-start.5 = ((bf16[4,136,2048]{2,1,0:T(8,128)(2,1)}), bf16[4,136,2048]{2,1,0:T(8,128)(2,1)S(1)}, u32[]{:S(2)}, u32[]{:S(2)}) async-start(bf16[4,136,2048]{2,1,0:T(8,128)(2,1)} %bitcast.460), calls=%async_computation.5 | async-start | bytes 4456448 | tf_op jit(solution)/shard_map/all_to_all | solution.py:91
  777.9 238.4 %all-to-all-start.8 = ((bf16[4,136,2048]{2,1,0:T(8,128)(2,1)}), bf16[4,136,2048]{2,1,0:T(8,128)(2,1)}, u32[]{:S(2)}, u32[]{:S(2)}) async-start(bf16[4,136,2048]{2,1,0:T(8,128)(2,1)} %bitcast.445), calls=%async_computation.8 | async-start | bytes 4456448 | tf_op jit(solution)/shard_map/all_to_all | solution.py:91
  1083.3 53.3 %all-to-all-start.10 = ((bf16[4,136,2048]{2,1,0:T(8,128)(2,1)}), bf16[4,136,2048]{2,1,0:T(8,128)(2,1)S(1)}, u32[]{:S(2)}, u32[]{:S(2)}) async-start(bf16[4,136,2048]{2,1,0:T(8,128)(2,1)} %bitcast.95), calls=%async_computation.10 | async-start | bytes 4456448 | tf_op jit(solution)/shard_map/all_to_all | solution.py:91
  1138.0 54.8 %all-to-all-start.11 = ((bf16[4,136,2048]{2,1,0:T(8,128)(2,1)}), bf16[4,136,2048]{2,1,0:T(8,128)(2,1)}, u32[]{:S(2)}, u32[]{:S(2)}) async-start(bf16[4,136,2048]{2,1,0:T(8,128)(2,1)} %bitcast.109), calls=%async_computation.12 | async-start | bytes 4456448 | tf_op jit(solution)/shard_map/all_to_all | solution.py:91
  1146.2 443.3 %reduce-scatter.5.cloned.1.call-start = ((), (), s32[]{:S(2)}) async-start(), calls=%async_computation.22 | async-start | bytes 5242880 | tf_op jit(solution)/shard_map/reduce_scatter | solution.py:593
  1312.1 137.0 %all-to-all-start.4 = ((bf16[4,136,2048]{2,1,0:T(8,128)(2,1)}), bf16[4,136,2048]{2,1,0:T(8,128)(2,1)}, u32[]{:S(2)}, u32[]{:S(2)}) async-start(bf16[4,136,2048]{2,1,0:T(8,128)(2,1)} %bitcast.67), calls=%async_computation.4 | async-start | bytes 4456448 | tf_op jit(solution)/shard_map/all_to_all | solution.py:91
  1320.6 268.9 %reduce-scatter.3.cloned.1.call-start = ((), (), s32[]{:S(2)}) async-start(), calls=%async_computation.21 | async-start | bytes 5242880 | tf_op jit(solution)/shard_map/reduce_scatter | solution.py:593
  1492.1 83.8 %all-to-all-start.7 = ((bf16[4,136,2048]{2,1,0:T(8,128)(2,1)}), bf16[4,136,2048]{2,1,0:T(8,128)(2,1)S(1)}, u32[]{:S(2)}, u32[]{:S(2)}) async-start(bf16[4,136,2048]{2,1,0:T(8,128)(2,1)} %bitcast.82), calls=%async_computation.7 | async-start | bytes 4456448 | tf_op jit(solution)/shard_map/all_to_all | solution.py:91
  (108 other events, 2947.4 us)
Sparse Core Ops, SparseCore 0:
  9.9 91.4 all-gather.11
  103.3 89.8 all-gather.13
  195.1 89.8 all-gather.15
  286.7 116.4 all-gather.23
  405.0 214.6 all-gather.21
  621.4 116.4 all-gather.25
  740.4 160.7 all-gather.19
  903.1 72.1 all-gather.17
  1309.7 127.2 reduce-scatter.4
  1439.2 132.7 reduce-scatter.2

commit v2 on v1

--- a/solution.py
+++ b/solution.py
@@ -110,7 +110,7 @@
             out_ref[rows, :] = made.astype(BF16)
 
 
-def make_key_value(normed_low, low_rank, kv_full, adapt_up, cos_k, sin_k, seqs):
+def make_key_value(normed_low, low_rank, weights, adapt_up, cos_k, sin_k, seqs):
     rows, width = normed_low.shape
     seq_len = rows // seqs
     tile = 512
@@ -129,10 +129,45 @@
         out_shape=jax.ShapeDtypeStruct((rows, 2 * width), BF16),
         compiler_params=params("arbitrary"),
         name="key_value",
-    )(normed_low, low_rank, kv_full, adapt_up, cos_k, sin_k)
-
-
-def attend_body(q_ref, k_ref, v_ref, cos_ref, sin_ref, qb_ref, kb_ref, rot_ref, out_ref, lse_ref):
+    )(normed_low, low_rank, weights, adapt_up, cos_k, sin_k)
+
+
+def project_body(x_ref, w_ref, *refs):
+    made = mm(x_ref[...], w_ref[...])
+    if len(refs) == 1:
+        refs[0][...] = made.astype(BF16)
+    else:
+        gate_ref, out_ref, gated_ref = refs
+        out_ref[...] = made.astype(BF16)
+        gated_ref[...] = (made * gate_ref[...]).astype(BF16)
+
+
+def project(values, weights, from_column, gate=None):
+    locals_, rows, width = values.shape
+    tile = 512
+    first, step = from_column // tile, width // tile
+    out_spec = pl.BlockSpec((None, rows, tile), lambda l, i: (l, 0, i))
+    out_shape = jax.ShapeDtypeStruct(values.shape, BF16)
+    in_specs = [
+        pl.BlockSpec((None, rows, width), lambda l, i: (l, 0, 0)),
+        pl.BlockSpec((width, tile), lambda l, i: (0, first + step * l + i)),
+    ]
+    more = []
+    if gate is not None:
+        in_specs.append(pl.BlockSpec((None, rows, 1), lambda l, i: (l, 0, 0)))
+        more = [gate]
+    return pl.pallas_call(
+        project_body,
+        grid=(locals_, step),
+        in_specs=in_specs,
+        out_specs=out_spec if gate is None else [out_spec] * 2,
+        out_shape=out_shape if gate is None else [out_shape] * 2,
+        compiler_params=params("arbitrary", "arbitrary"),
+        name="project",
+    )(values, weights, *more)
+
+
+def attend_body(q_ref, k_ref, v_ref, cos_ref, sin_ref, qb_ref, kb_ref, rot_ref, out_ref, probs_ref):
     locals_, _, slots, _ = q_ref.shape
     rows = locals_ * slots
     q = q_ref[...].reshape(rows, HDIM).astype(F32)
@@ -148,9 +183,9 @@
         top = jnp.max(masked, axis=-1, keepdims=True)
         terms = jnp.exp((masked - top) * SCALE_QK)
         total = jnp.sum(terms, axis=-1, keepdims=True)
-        out = mm(terms.astype(BF16), v) * (1.0 / total)
-        out_ref[l, 0] = out.astype(BF16)
-        lse_ref[l, 0, 0] = top * SCALE_QK + jnp.log(total)
+        probs = (terms * (1.0 / total)).astype(BF16)
+        probs_ref[l, 0, 0] = probs
+        out_ref[l, 0] = mm(probs, v).astype(BF16)
 
 
 def attend(queries, key_value, cos_q, sin_q, query_blocks, key_blocks):
@@ -173,47 +208,38 @@
         out_specs=[
             q_spec,
             q_spec,
-            pl.BlockSpec((locals_, 1, 1, slots, 1), lambda s, h: (0, s, h, 0, 0)),
+            pl.BlockSpec((locals_, 1, 1, slots, seq_len), lambda s, h: (0, s, h, 0, 0)),
         ],
         out_shape=[
             jax.ShapeDtypeStruct(queries.shape, BF16),
             jax.ShapeDtypeStruct(queries.shape, BF16),
-            jax.ShapeDtypeStruct((locals_, seqs, HEADS, slots, 1), F32),
+            jax.ShapeDtypeStruct((locals_, seqs, HEADS, slots, seq_len), BF16),
         ],
         compiler_params=params("arbitrary", "arbitrary"),
         name="attend",
     )(queries, key_value, key_value, cos_q, sin_q, query_blocks, key_blocks)
 
 
-def attend_back_body(
-    q_ref, k_ref, v_ref, g_ref, lse_ref, cos_ref, sin_ref, qb_ref, kb_ref, ck_ref, sk_ref, dq_ref, dk_ref, dv_ref
-):
+def attend_back_body(q_ref, k_ref, v_ref, g_ref, p_ref, cos_ref, sin_ref, ck_ref, sk_ref, dq_ref, dk_ref, dv_ref):
     locals_, _, slots, _ = q_ref.shape
+    rows = locals_ * slots
     k, v = k_ref[0], v_ref[0]
-    kb = kb_ref[0]
-    dk = dv = None
-    for l in range(locals_):
-        q, grad = q_ref[l, 0], g_ref[l]
-        visible = kb <= qb_ref[l, 0]
-        scores = mm(q, k, NT) * SCALE_QK - lse_ref[l, 0, 0]
-        probs = jnp.where(visible, jnp.exp(jnp.where(visible, scores, MASKED_SCORE)), 0.0)
-        grad_probs = mm(grad, v, NT)
-        weighed = probs * grad_probs
-        delta = jnp.sum(weighed, axis=-1, keepdims=True)
-        grad_scores = (weighed - probs * delta).astype(BF16)
-        dq = mm(grad_scores, k) * SCALE_QK
-        dq = dq * cos_ref[l, 0] - pltpu.roll(dq, HDIM // 2, 1) * sin_ref[l, 0]
-        dq_ref[l] = dq.astype(BF16)
-        dk_part = mm(grad_scores, q, TN)
-        dv_part = mm(probs.astype(BF16), grad, TN)
-        dk = dk_part if dk is None else dk + dk_part
-        dv = dv_part if dv is None else dv + dv_part
-    dk = dk * SCALE_QK
+    q = q_ref[...].reshape(rows, HDIM)
+    grad = g_ref[...].reshape(rows, HDIM)
+    probs = p_ref[...].reshape(rows, k.shape[0])
+    weighed = probs.astype(F32) * mm(grad, v, NT)
+    delta = jnp.sum(weighed, axis=-1, keepdims=True)
+    grad_scores = (weighed - probs.astype(F32) * delta).astype(BF16)
+    dq = mm(grad_scores, k) * SCALE_QK
+    cos, sin = cos_ref[...].reshape(rows, HDIM), sin_ref[...].reshape(rows, HDIM)
+    dq = dq * cos - pltpu.roll(dq, HDIM // 2, 1) * sin
+    dq_ref[...] = dq.astype(BF16).reshape(dq_ref.shape)
+    dk = mm(grad_scores, q, TN) * SCALE_QK
     dk_ref[...] = (dk * ck_ref[...] - pltpu.roll(dk, HDIM // 2, 1) * sk_ref[...]).astype(BF16)
-    dv_ref[...] = dv.astype(BF16)
-
-
-def attend_back(s, query_rot, key_value, grad, lse, cos_q, sin_q, query_blocks, key_blocks, cos_k, sin_k):
+    dv_ref[...] = mm(probs, grad, TN).astype(BF16)
+
+
+def attend_back(s, query_rot, key_value, grad, probs, cos_q, sin_q, cos_k, sin_k):
     locals_, _, slots, width = query_rot.shape
     seq_len = key_value.shape[1]
     tab_spec = pl.BlockSpec((locals_, 1, slots, HDIM), lambda h: (0, s, 0, 0))
@@ -228,11 +254,9 @@
             pl.BlockSpec((1, seq_len, HDIM), lambda h: (s, 0, h)),
             pl.BlockSpec((1, seq_len, HDIM), lambda h: (s, 0, HEADS + h)),
             grad_spec,
-            pl.BlockSpec((locals_, 1, 1, slots, 1), lambda h: (0, s, h, 0, 0)),
+            pl.BlockSpec((locals_, 1, 1, slots, seq_len), lambda h: (0, s, h, 0, 0)),
             tab_spec,
             tab_spec,
-            pl.BlockSpec((locals_, 1, slots, 1), lambda h: (0, s, 0, 0)),
-            pl.BlockSpec((1, 1, seq_len), lambda h: (s, 0, 0)),
             key_tab,
             key_tab,
         ],
@@ -244,17 +268,22 @@
         ],
         compiler_params=params("arbitrary"),
         name="attend_back",
-    )(query_rot, key_value, key_value, grad, lse, cos_q, sin_q, query_blocks, key_blocks, cos_k, sin_k)
-
-
-def expert_body(has_start, x_ref, c_ref, wg_ref, wu_ref, wd_ref, *refs):
-    out_ref, gs_ref = refs[-2:]
+    )(query_rot, key_value, key_value, grad, probs, cos_q, sin_q, cos_k, sin_k)
+
+
+def expert_body(has_start, is_last, x_ref, c_ref, wg_ref, wu_ref, wd_ref, *refs):
+    refs = list(refs)
+    start = [refs.pop(0), refs.pop(0)] if has_start else None
+    if is_last:
+        cot_ref, gate_ref, pick_ref, router_ref, low_ref, back_ref, out_ref, gs_ref = refs
+    else:
+        out_ref, gs_ref = refs
 
     @pl.when(pl.program_id(0) == 0)
     def _():
         if has_start:
-            out_ref[...] = refs[0][...]
-            gs_ref[...] = refs[1][...]
+            out_ref[...] = start[0][...]
+            gs_ref[...] = start[1][...]
         else:
             out_ref[...] = jnp.zeros_like(out_ref)
             gs_ref[...] = jnp.zeros_like(gs_ref)
@@ -270,61 +299,157 @@
     grad_up = (grad * silu).astype(BF16)
     gs_ref[...] += mm(grad_gate, wg, NT) + mm(grad_up, wu, NT)
 
-
-def expert_pass(rows_in, grad_in, inner, down, down_from, start=None):
+    if is_last:
+
+        @pl.when(pl.program_id(0) == pl.num_programs(0) - 1)
+        def _():
+            made = out_ref[...]
+            share = gate_ref[...]
+            dots = jnp.sum(cot_ref[...].astype(F32) * made, axis=-1, keepdims=True)
+            weigh = pick_ref[...] * (dots * share * (1.0 - share))
+            high = weigh.astype(BF16)
+            low = (weigh - high.astype(F32)).astype(BF16)
+            router = router_ref[...]
+            back_ref[...] = (gs_ref[...] + mm(high, router, NT) + mm(low, router, NT)).astype(BF16)
+            low_ref[...] = (share * made).astype(BF16)
+
+
+def expert_pass(rows_in, grad_in, inner, down, l, down_from, start=None, last=None):
     rows, width = rows_in.shape
     units = inner.shape[1] // 2
     tile = 512 if units % 512 == 0 and down_from % 512 == 0 else 256
-    whole = once((rows, width), lambda i: (0, 0))
     first = down_from // tile
-    more = [] if start is None else list(start)
+
+    def whole(array):
+        return once(array.shape, lambda i: (0,) * array.ndim)
+
+    more = ([] if start is None else list(start)) + ([] if last is None else list(last))
+    kind = F32 if last is None else BF16
     return pl.pallas_call(
-        functools.partial(expert_body, start is not None),
+        functools.partial(expert_body, start is not None, last is not None),
         grid=(units // tile,),
         in_specs=[
-            whole,
-            whole,
+            whole(rows_in),
+            whole(grad_in),
             pl.BlockSpec((width, tile), lambda i: (0, i)),
             pl.BlockSpec((width, tile), lambda i: (0, units // tile + i)),
-            pl.BlockSpec((tile, width), lambda i: (first + i, 0)),
+            pl.BlockSpec((None, tile, width), lambda i: (l, first + i, 0)),
         ]
-        + [whole] * len(more),
+        + [whole(m) for m in more],
         out_specs=[pl.BlockSpec((rows, width), lambda i: (0, 0))] * 2,
-        out_shape=[jax.ShapeDtypeStruct((rows, width), F32)] * 2,
+        out_shape=[jax.ShapeDtypeStruct((rows, width), kind)] * 2,
+        scratch_shapes=[] if last is None else [pltpu.VMEM((rows, width), F32)] * 2,
         compiler_params=params("arbitrary"),
         name="expert",
     )(rows_in, grad_in, inner, inner, down, *more)
 
 
-def last_body(dk_ref, dv_ref, w_ref, table_ref, gs_ref, low_ref, down_ref, out_ref):
-    width = dk_ref.shape[1]
-    total = mm(dk_ref[...], w_ref[:, :width], NT) + mm(dv_ref[...], w_ref[:, width:], NT)
-    total += mm(table_ref[...], gs_ref[...])
-    total += mm(low_ref[...], down_ref[...], NT)
-    out_ref[...] = total.astype(BF16)
-
-
-def last_grad(dk, dv, kv_full, table, grad_source, grad_low, adapt_down):
-    seq_len, width = dk.shape
-    slots = grad_source.shape[0]
+def out_back_body(locals_, arrived_ref, order_ref, gate_ref, projected_ref, *refs):
+    w_refs, (out_ref, dots_ref, rows_ref) = refs[:locals_], refs[locals_:]
+    slots = projected_ref.shape[1]
+
+    @pl.when(pl.program_id(0) == 0)
+    def _():
+        for l in range(locals_):
+            rows = mm(order_ref[pl.ds(l * slots, slots), :], arrived_ref[...])
+            dots_ref[l] = jnp.sum(rows * projected_ref[l].astype(F32), axis=-1, keepdims=True)
+            rows_ref[l] = (rows * gate_ref[l]).astype(BF16)
+
+    for l in range(locals_):
+        out_ref[l] = mm(rows_ref[l], w_refs[l][...], NT).astype(BF16)
+
+
+def out_back(s, arrived, order, gate, projected, weights, from_column):
+    locals_, slots = gate.shape[0], gate.shape[2]
+    rows, width = arrived.shape
     tile = 512
     return pl.pallas_call(
-        last_body,
+        functools.partial(out_back_body, locals_),
+        grid=(width // tile,),
+        in_specs=[
+            once((rows, width), lambda i: (0, 0)),
+            once((rows, rows), lambda i: (0, 0)),
+            once((locals_, None, slots, 1), lambda i: (0, s, 0, 0)),
+            once((locals_, None, slots, width), lambda i: (0, s, 0, 0)),
+        ]
+        + [
+            pl.BlockSpec((tile, width), lambda i, l=l: (i, from_column // width + l))
+            for l in range(locals_)
+        ],
+        out_specs=[
+            pl.BlockSpec((locals_, slots, tile), lambda i: (0, 0, i)),
+            pl.BlockSpec((locals_, slots, 1), lambda i: (0, 0, 0)),
+        ],
+        out_shape=[
+            jax.ShapeDtypeStruct((locals_, slots, width), BF16),
+            jax.ShapeDtypeStruct((locals_, slots, 1), F32),
+        ],
+        scratch_shapes=[pltpu.VMEM((locals_, slots, width), BF16)],
+        compiler_params=params("arbitrary"),
+        name="out_back",
+    )(arrived, order, gate, projected, *([weights] * locals_))
+
+
+def last_body(
+    locals_, seq_len, dk_ref, dv_ref, dq_ref, table_ref, dots_ref, weigh_ref, mask_ref, up_ref, router_ref, down_ref, w_ref, *refs
+):
+    wq_refs, (out_ref, low_ref) = refs[:locals_], refs[locals_:]
+    width = dk_ref.shape[1]
+    slots = dq_ref.shape[1]
+
+    @pl.when(pl.program_id(0) == 0)
+    def _():
+        low = mm(dk_ref[...], up_ref[:width, :]) + mm(dv_ref[...], up_ref[width:, :])
+        low_ref[...] = (low * mask_ref[...]).astype(BF16)
+
+    total = mm(dk_ref[...], w_ref[:, :width], NT) + mm(dv_ref[...], w_ref[:, width:], NT)
+    total += mm(low_ref[...], down_ref[...], NT)
+    router = router_ref[...]
+    for l in range(locals_):
+        weigh = weigh_ref[l] * dots_ref[l]
+        high = weigh.astype(BF16)
+        low = (weigh - high.astype(F32)).astype(BF16)
+        source = mm(dq_ref[l], wq_refs[l][...], NT) + mm(high, router, NT) + mm(low, router, NT)
+        total += mm(table_ref[0, :, pl.ds(l * slots, slots)], source.astype(BF16))
+    out_ref[...] = total.astype(BF16)
+
+
+def last_grad(s, dk, dv, dq, table, dots, weigh, mask, adapt_up, router, adapt_down, weights, query_column):
+    seq_len, width = dk.shape
+    locals_, slots, _ = dq.shape
+    tile = 256
+    ranks = adapt_up.shape[1]
+    return pl.pallas_call(
+        functools.partial(last_body, locals_, seq_len),
         grid=(width // tile,),
         in_specs=[
             once((seq_len, width), lambda i: (0, 0)),
             once((seq_len, width), lambda i: (0, 0)),
+            once((locals_, slots, width), lambda i: (0, 0, 0)),
+            once((1, seq_len, locals_ * slots), lambda i: (s, 0, 0)),
+            once((locals_, slots, 1), lambda i: (0, 0, 0)),
+            once((locals_, None, slots, EXPERTS), lambda i: (0, s, 0, 0)),
+            once((None, 1, ranks), lambda i: (s, 0, 0)),
+            once((2 * width, ranks), lambda i: (0, 0)),
+            pl.BlockSpec((tile, EXPERTS), lambda i: (i, 0)),
+            pl.BlockSpec((tile, ranks), lambda i: (i, 0)),
             pl.BlockSpec((tile, 2 * width), lambda i: (i, 0)),
-            once((seq_len, slots), lambda i: (0, 0)),
-            pl.BlockSpec((slots, tile), lambda i: (0, i)),
-            once((seq_len, grad_low.shape[1]), lambda i: (0, 0)),
-            pl.BlockSpec((tile, grad_low.shape[1]), lambda i: (i, 0)),
-        ],
-        out_specs=pl.BlockSpec((seq_len, tile), lambda i: (0, i)),
-        out_shape=jax.ShapeDtypeStruct((seq_len, width), BF16),
+        ]
+        + [
+            pl.BlockSpec((tile, width), lambda i, l=l: (i, query_column // width + l))
+            for l in range(locals_)
+        ],
+        out_specs=[
+            pl.BlockSpec((seq_len, tile), lambda i: (0, i)),
+            pl.BlockSpec((seq_len, ranks), lambda i: (0, 0)),
+        ],
+        out_shape=[
+            jax.ShapeDtypeStruct((seq_len, width), BF16),
+            jax.ShapeDtypeStruct((seq_len, ranks), BF16),
+        ],
         compiler_params=params("arbitrary"),
         name="last_grad",
-    )(dk, dv, kv_full, table, grad_source, grad_low, adapt_down)
+    )(dk, dv, dq, table, dots, weigh, mask, adapt_up, router, adapt_down, weights, *([weights] * locals_))
 
 
 def per_device(
@@ -354,13 +479,19 @@
     slots = ranks * capacity
     here = lax.axis_index("expert")
 
-    kv_full = lax.all_gather(kv_weight, "dp", axis=0, tiled=True)
-    query_full = lax.all_gather(query_weight, "dp", axis=1, tiled=True)
-    output_full = lax.all_gather(output_weight, "dp", axis=1, tiled=True)
-    cut = (FF * 3 // 4) // 256 * 256
-    expert_weights = []
+    query_column = 2 * width
+    output_column = query_column + locals_ * width
+    near = jnp.concatenate(
+        [kv_weight]
+        + [query_weight[l] for l in range(locals_)]
+        + [output_weight[l] for l in range(locals_)],
+        axis=1,
+    )
+    near_full = lax.all_gather(near, "dp", axis=0, tiled=True)
+    down_full = lax.all_gather(down_weight, "dp", axis=1, tiled=True)
+    cut = (FF * 3 // 4) // 512 * 512
+    inner_full = []
     for l in range(locals_):
-        down_full = lax.all_gather(down_weight[l], "dp", axis=0, tiled=True)
         if l + 1 < locals_:
             pieces = [(0, lax.all_gather(inner_weight[l], "dp", axis=0, tiled=True))]
         else:
@@ -370,7 +501,7 @@
                     [inner_weight[l, :, low:high], inner_weight[l, :, FF + low : FF + high]], axis=1
                 )
                 pieces.append((low, lax.all_gather(part, "dp", axis=0, tiled=True)))
-        expert_weights.append((down_full, pieces))
+        inner_full.append(pieces)
 
     routes = lax.all_gather(
         jnp.concatenate([attn_routes, mlp_routes], axis=-1), "expert", axis=1, tiled=True
@@ -445,16 +576,19 @@
         sums = mm(table, jnp.concatenate([both, jnp.ones_like(both)], axis=1))
         other_sum.append((sums[:, :1], sums[:, 1:]))
 
-    flat_cot = cotangent.reshape(seqs * row_count, width)
-    cot_rows = [send(mm(own_spread_m[l], flat_cot).astype(BF16)) for l in range(locals_)]
-
+    hidden_first, routes = lax.optimization_barrier((hidden_in, routes))
     everyone = gather_line(
-        hidden_in,
+        hidden_first,
         "expert",
         ranks,
         lambda total, piece, at: lax.dynamic_update_slice(total, piece[:, None], (0, at, 0, 0)),
         jnp.zeros((seqs, ranks, row_count, width), BF16),
     ).reshape(seqs, seq_len, width)
+
+    flat_cot, everyone = lax.optimization_barrier((cotangent, everyone))
+    flat_cot = flat_cot.reshape(seqs * row_count, width)
+    cot_rows = [send(mm(own_spread_m[l], flat_cot).astype(BF16)) for l in range(locals_)]
+
     tokens_all = everyone.astype(F32)
     scale_all = rms_scale(tokens_all)
     normed_low = (tokens_all * scale_all * attn_gain).astype(BF16)
@@ -498,7 +632,7 @@
     low_rank = mm(flat_low, adapt_down).reshape(seqs, seq_len, NADAPT * RANK)
     low_rank = jnp.where(own_adapter[:, None, :], low_rank, 0.0).astype(BF16)
     key_value = make_key_value(
-        flat_low, low_rank.reshape(seqs * seq_len, -1), kv_full, adapt_up, cos_k, sin_k, seqs
+        flat_low, low_rank.reshape(seqs * seq_len, -1), near_full, adapt_up, cos_k, sin_k, seqs
     ).reshape(seqs, seq_len, 2 * width)
 
     picked = jnp.einsum(
@@ -507,14 +641,19 @@
         normed_low,
         preferred_element_type=F32,
     ).astype(BF16)
-    queries = jnp.stack(
-        [mm(picked[l].reshape(seqs * slots, width), query_full[l]).astype(BF16) for l in range(locals_)]
-    ).reshape(locals_, seqs, slots, width)
-    query_rot, attended, lse = attend(queries, key_value, cos_q, sin_q, query_blocks, key_blocks)
-    projected = [
-        mm(attended[l].reshape(seqs * slots, width), output_full[l]).reshape(seqs, slots, width)
-        for l in range(locals_)
-    ]
+    queries = project(picked.reshape(locals_, seqs * slots, width), near_full, query_column)
+    query_rot, attended, probs = attend(
+        queries.reshape(locals_, seqs, slots, width), key_value, cos_q, sin_q, query_blocks, key_blocks
+    )
+    gate_rows = gate_a[..., None]
+    projected, gated = project(
+        attended.reshape(locals_, seqs * slots, width),
+        near_full,
+        output_column,
+        gate_rows.reshape(locals_, seqs * slots, 1),
+    )
+    projected = projected.reshape(locals_, seqs, slots, width)
+    gated = gated.reshape(locals_, seqs, slots, width)
     order = np.arange(locals_ * slots).reshape(locals_, ranks, capacity).transpose(1, 0, 2).reshape(-1)
     to_send = jnp.asarray(np.eye(locals_ * slots)[order], BF16)
     to_slots = jnp.asarray(np.eye(locals_ * slots)[order].T, BF16)
@@ -522,19 +661,15 @@
     upstream = cotangent.astype(F32)
     middles = []
     for s in range(seqs):
-        gated = jnp.concatenate(
-            [(projected[l][s] * gate_a[l, s][:, None]).astype(BF16) for l in range(locals_)], axis=0
-        )
-        back = send(mm(to_send, gated).astype(BF16))
+        back = send(mm(to_send, gated[:, s].reshape(locals_ * slots, width)).astype(BF16))
         middles.append(tokens[s] + mm(own_collect_a[s], back))
-    projected_low = [p.astype(BF16) for p in projected]
     middle = jnp.stack(middles)
     scale_two = rms_scale(middle)
     normed_two_low = (middle * scale_two * mlp_gain).astype(BF16).reshape(seqs * row_count, width)
 
     final = middle.reshape(seqs * row_count, width)
     grad_normed_two = jnp.zeros((seqs * row_count, width), F32)
-    mlp_back = []
+    held = None
     for l in range(locals_):
         rows_in = send(mm(own_spread_m[l], normed_two_low).astype(BF16))
         slot_logits = mm(rows_in, mlp_router)
@@ -542,54 +677,38 @@
         pick_m = (expert_f[None, :] == me).astype(F32) - (
             expert_f[None, :] == other_sum[l][0] - me
         ).astype(F32)
-        gap_m = jnp.sum(pick_m * slot_logits, axis=-1, keepdims=True)
-        gate_m = jax.nn.sigmoid(gap_m)
-        cot = cot_rows[l].astype(F32)
-        grad_rows = (gate_m * cot).astype(BF16)
-        down_full, pieces = expert_weights[l]
+        gate_m = jax.nn.sigmoid(jnp.sum(pick_m * slot_logits, axis=-1, keepdims=True))
+        grad_rows = (gate_m * cot_rows[l].astype(F32)).astype(BF16)
         made = None
-        for low, inner_full in pieces:
-            made = expert_pass(rows_in, grad_rows, inner_full, down_full, low, made)
-        expert_out, grad_source = made
-        dots = jnp.sum(cot * expert_out, axis=-1, keepdims=True)
-        weigh_m = pick_m * (dots * gate_m * jax.nn.sigmoid(-gap_m))
-        grad_source = grad_source + jnp.dot(weigh_m, mlp_router.astype(F32).T, precision=PRECISE)
-        grad_back = send(grad_source.astype(BF16))
+        for at, (low, inner) in enumerate(inner_full[l]):
+            ends = (cot_rows[l], gate_m, pick_m, mlp_router) if at + 1 == len(inner_full[l]) else None
+            made = expert_pass(rows_in, grad_rows, inner, down_full, l, low, made, ends)
+        gated_out, grad_source = made
+        if held is not None:
+            final = final + mm(own_collect_m[l - 1], held)
+            grad_source, final = lax.optimization_barrier((grad_source, final))
+        grad_back = send(grad_source)
         grad_normed_two = grad_normed_two + mm(own_collect_m[l], grad_back)
-        mlp_back.append((gate_m * expert_out).astype(BF16))
-    for l in range(locals_):
-        final = final + mm(own_collect_m[l], send(mlp_back[l]))
-    layer_out = final.astype(BF16).reshape(seqs, row_count, width)
+        held = send(gated_out) if l + 1 < locals_ else gated_out
     grad_normed_two = grad_normed_two.reshape(seqs, row_count, width)
     grad_middle = upstream + norm_back(middle, scale_two, mlp_gain, grad_normed_two)
 
+    arrived = [send(mm(own_spread_a[s], grad_middle[s].astype(BF16)).astype(BF16)) for s in range(seqs)]
     input_grads, down_pieces, up_pieces = [], [], []
-    attn_router_f = attn_router.astype(F32)
+    mask = own_adapter.astype(F32)[:, None, :]
     for s in range(seqs):
-        arrived = send(mm(own_spread_a[s], grad_middle[s].astype(BF16)).astype(BF16))
-        grad_rows = mm(to_slots, arrived).reshape(locals_, slots, width)
-        grad_attended, extra = [], []
-        for l in range(locals_):
-            grad_projected = (grad_rows[l] * gate_a[l, s][:, None]).astype(BF16)
-            grad_attended.append(mm(grad_projected, output_full[l], NT).astype(BF16))
-            dots = jnp.sum(grad_rows[l] * projected_low[l][s].astype(F32), axis=-1, keepdims=True)
-            extra.append(weigh_a[l, s] * dots)
-        dq, dk, dv = attend_back(
-            s, query_rot, key_value, jnp.stack(grad_attended), lse, cos_q, sin_q, query_blocks,
-            key_blocks, cos_k, sin_k,
+        grad_attended, dots = out_back(
+            s, arrived[s], to_slots, gate_rows, projected, near_full, output_column
         )
-        grad_source = jnp.concatenate(
-            [
-                (
-                    mm(dq[l], query_full[l], NT) + jnp.dot(extra[l], attn_router_f.T, precision=PRECISE)
-                ).astype(BF16)
-                for l in range(locals_)
-            ],
-            axis=0,
+        dq, dk, dv = attend_back(s, query_rot, key_value, grad_attended, probs, cos_q, sin_q, cos_k, sin_k)
+        part, grad_low = last_grad(
+            s, dk, dv, dq, collect_a, dots, weigh_a, mask, adapt_up, attn_router, adapt_down, near_full,
+            query_column,
         )
-        grad_low = mm(dk, adapt_up[:width]) + mm(dv, adapt_up[width:])
-        grad_low = jnp.where(own_adapter[s][None, :], grad_low, 0.0).astype(BF16)
-        part = last_grad(dk, dv, kv_full, collect_a[s], grad_source, grad_low, adapt_down)
+        if s + 1 < seqs:
+            part, arrived[s + 1] = lax.optimization_barrier((part, arrived[s + 1]))
+        if s + 2 == seqs:
+            held, part = lax.optimization_barrier((held, part))
         grad_normed = lax.psum_scatter(part, "expert", scatter_dimension=0, tiled=True).astype(F32)
         input_grads.append(
             grad_middle[s] + norm_back(tokens[s], rms_scale(tokens[s]), attn_gain, grad_normed)
@@ -598,6 +717,8 @@
         down_pieces.append(lax.dynamic_slice_in_dim(mm(grad_low, normed_low[s], TN), first, RANK, 0))
         up_piece = jnp.concatenate([mm(low_rank[s], dk, TN), mm(low_rank[s], dv, TN)], axis=1)
         up_pieces.append(lax.dynamic_slice_in_dim(up_piece, first, RANK, 0))
+    final = final + mm(own_collect_m[locals_ - 1], send(held))
+    layer_out = final.astype(BF16).reshape(seqs, row_count, width)
 
     groups = adapters.shape[0] // seqs
     down_part = width // (groups * ranks)

time: 1620 us -> 1510 us (0.932)
  matrix products: 205 us -> 92.5 us
  Pallas kernels: 439 us -> 520 us
  waiting for transfers between devices: 586 us -> 521 us
  other arithmetic: 91.8 us -> 71.6 us
  blocking collectives: 105 us -> 124 us
    all_gather x2, waiting for transfers between devices: 121 us -> 15.2 us  [per_device(): pieces.append((low, lax.all_gather(part, 'dp', axis=0, tiled=True)))]
    dot_general x46 -> x26, matrix products: 181 us -> 80.9 us  [mm(): return lax.dot_general(left, right, dims, preferred_element_type=F32)]
    pallas_call x5 -> x9, Pallas kernels: 246 us -> 346 us  [the longest x3 193 us: expert_pass(): pl.pallas_call(functools.partial(expert_body, start is not None, last is...]
    all_to_all x1 -> x2, blocking collectives: 43 us -> 95.4 us  [send(): lax.all_to_all(buffer, 'expert', split_axis=0, concat_axis=0, tiled=True)]
    all_gather x1, waiting for transfers between devices: 0.01 us -> 42.3 us  [per_device(): pieces = [(0, lax.all_gather(inner_weight[l], 'dp', axis=0, tiled=True))]]
    all_gather x1, blocking collectives: 52.4 us -> 11.1 us  [per_device(): lax.all_gather(jnp.concatenate([attn_routes, mlp_routes], axis=-1), 'expe...]
    pallas_call x2, Pallas kernels: 88.3 us -> 63.8 us  [attend_back(): pl.pallas_call(attend_back_body, grid=(HEADS,), in_specs=[pl.BlockSpec((l...]
    reduce_scatter x2, waiting for transfers between devices: 0.01 us -> 22.3 us  [per_device(): lax.psum_scatter(part, 'expert', scatter_dimension=0, tiled=True)]
  transfers between devices with their start and end apart: 29 -> 24, of which waited for: 12 -> 15; matrix products, arithmetic and copies ran while one was open for 17% -> 12% of each run, Pallas kernels for 23% -> 29%
where the time goes in v2:
time: 1510 us; the launch traced here: 1500 us
  waiting for transfers between devices  521 us (35%)
  Pallas kernels  520 us (34%)
  blocking collectives  124 us (8%)
  matrix products  92.5 us (6%)
  starting transfers between devices  91.1 us (6%)
  other arithmetic  71.6 us (5%)
  local copies, waits for them, and re-layouts  65.3 us (4%)
  between operations  17.8 us (1%)
    all_to_all x11, waiting for transfers between devices, send(): lax.all_to_all(buffer, 'expert', split_axis=0, concat_axis=0, tiled=True)  331 us
    pallas_call x3, Pallas kernels, expert_pass(): pl.pallas_call(functools.partial(expert_body, start is not None, last is...  193 us
    ppermute x3, waiting for transfers between devices, gather_line(): from_right.append(lax.ppermute(from_right[-1], axis, leftward))  106 us
    all_to_all x2, blocking collectives, send(): lax.all_to_all(buffer, 'expert', split_axis=0, concat_axis=0, tiled=True)  95.4 us
    pallas_call x2, Pallas kernels, last_grad(): pl.pallas_call(functools.partial(last_body, locals_, seq_len), grid=(widt...  90.2 us
    dot_general x26, matrix products, mm(): return lax.dot_general(left, right, dims, preferred_element_type=F32)  80.9 us
    all_to_all x11, starting transfers between devices, send(): lax.all_to_all(buffer, 'expert', split_axis=0, concat_axis=0, tiled=True)  74.8 us
    pallas_call x2, Pallas kernels, attend_back(): pl.pallas_call(attend_back_body, grid=(HEADS,), in_specs=[pl.BlockSpec((l...  63.8 us
  transfers between devices with their start and end apart: 24, of which 15 were waited for; matrix products, arithmetic and copies ran while one was open for 12% of the time, Pallas kernels for 29%

profile of v2, /device:TPU:9, one launch (start us, length us, event | category | flops | bytes accessed | tf_op | source)
XLA Modules:
  0.0 1503.7 jit_solution(843194300226575192)
XLA Ops:
  45.6 39.2 %collective-permute-done.1 = bf16[2,256,2048]{2,1,0:T(8,128)(2,1)} collective-permute-done((bf16[2,256,2048]{2,1,0:T(8,128)(2,1)S(1)}, bf16[2,256,2048]{2,1,0:T(8,128)(2,1)}, u32[]{:S(2)}, u32[]{:S(2)}) %collective-permute-start.1) | collective-permute-done | bytes 2097184 | tf_op jit(solution)/shard_map/ppermute | solution.py:82
  91.2 38.6 %collective-permute-done.2 = bf16[2,256,2048]{2,1,0:T(8,128)(2,1)} collective-permute-done((bf16[2,256,2048]{2,1,0:T(8,128)(2,1)}, bf16[2,256,2048]{2,1,0:T(8,128)(2,1)}, u32[]{:S(2)}, u32[]{:S(2)}) %collective-permute-start.2) | collective-permute-done | bytes 2097184 | tf_op jit(solution)/shard_map/ppermute | solution.py:82
  145.1 28.7 %collective-permute-done.3 = bf16[2,256,2048]{2,1,0:T(8,128)(2,1)} collective-permute-done((bf16[2,256,2048]{2,1,0:T(8,128)(2,1)}, bf16[2,256,2048]{2,1,0:T(8,128)(2,1)}, u32[]{:S(2)}, u32[]{:S(2)}) %collective-permute-start.3) | collective-permute-done | bytes 2097184 | tf_op jit(solution)/shard_map/ppermute | solution.py:82
  266.0 54.6 %key_value.1 = bf16[2048,4096]{1,0:T(8,128)(2,1)} custom-call(bf16[2048,2048]{1,0:T(8,128)(2,1)} %bitcast.311, bf16[2048,128]{1,0:T(8,128)(2,1)} %bitcast.336, bf16[2048,12288]{1,0:T(8,128)(2,1)} %all-gather.7.cloned.1.call-done.w_ref.refs_0_.refs_1_, bf16[4096,128]{1,0:T(8,128)(2,1)} %up_ref.5, f32[1024,128]{1,0:T(8,128)} %get-tuple-element.152.cos_ref.ck_ref, ...), custom_call_target="tpu_custom_call" | custom-call | tf_op jit(solution)/shard_map/key_value/pallas_call | solution.py:117
  320.6 55.9 %attend.1 = (bf16[2,2,272,2048]{3,2,1,0:T(8,128)(2,1)}, bf16[2,2,272,2048]{3,2,1,0:T(8,128)(2,1)}, bf16[2,2,16,272,1024]{4,3,2,1,0:T(8,128)(2,1)}) custom-call(bf16[2,2,272,2048]{3,2,1,0:T(8,128)(2,1)} %bitcast.325, bf16[2,1024,4096]{2,1,0:T(8,128)(2,1)} %bitcast.303, bf16[2,1024,4096]{2,1,0:T(8,128)(2,1)} %bitcast.304, ...), custom_call_target="tpu_custom_call" | custom-call | tf_op jit(solution)/shard_map/attend/pallas_call | solution.py:196
  376.5 17.7 %project.3 = (bf16[2,544,2048]{2,1,0:T(8,128)(2,1)}, bf16[2,544,2048]{2,1,0:T(8,128)(2,1)}) custom-call(bf16[2,544,2048]{2,1,0:T(8,128)(2,1)} %bitcast.337, bf16[2048,12288]{1,0:T(8,128)(2,1)} %all-gather.7.cloned.1.call-done.w_ref.refs_0_.refs_1_, f32[2,544,1]{2,1,0:T(8,128)} %fusion.89.refs_0_), custom_call_target="tpu_custom_call" | custom-call | tf_op jit(solution)/shard_map/project/pallas_call | solution.py:159
  414.3 37.5 %all-to-all-done = bf16[4,136,2048]{2,1,0:T(8,128)(2,1)S(1)} async-done(((bf16[4,136,2048]{2,1,0:T(8,128)(2,1)}), bf16[4,136,2048]{2,1,0:T(8,128)(2,1)S(1)}, u32[]{:S(2)}, u32[]{:S(2)}) %all-to-all-start) | async-done | bytes 2228256 | tf_op jit(solution)/shard_map/all_to_all | solution.py:91
  467.0 42.1 %all-to-all-done.1 = bf16[4,136,2048]{2,1,0:T(8,128)(2,1)} async-done(((bf16[4,136,2048]{2,1,0:T(8,128)(2,1)}), bf16[4,136,2048]{2,1,0:T(8,128)(2,1)}, u32[]{:S(2)}, u32[]{:S(2)}) %all-to-all-start.1) | async-done | bytes 2228256 | tf_op jit(solution)/shard_map/all_to_all | solution.py:91
  531.2 32.3 %all-to-all-done.3 = bf16[4,136,2048]{2,1,0:T(8,128)(2,1)S(1)} async-done(((bf16[4,136,2048]{2,1,0:T(8,128)(2,1)}), bf16[4,136,2048]{2,1,0:T(8,128)(2,1)S(1)}, u32[]{:S(2)}, u32[]{:S(2)}) %all-to-all-start.3) | async-done | bytes 2228256 | tf_op jit(solution)/shard_map/all_to_all | solution.py:91
  577.6 42.3 %all-to-all-done.4 = bf16[4,136,2048]{2,1,0:T(8,128)(2,1)} async-done(((bf16[4,136,2048]{2,1,0:T(8,128)(2,1)}), bf16[4,136,2048]{2,1,0:T(8,128)(2,1)}, u32[]{:S(2)}, u32[]{:S(2)}) %all-to-all-start.4) | async-done | bytes 2228256 | tf_op jit(solution)/shard_map/all_to_all | solution.py:91
  639.1 42.3 %all-gather.15.cloned.1.call-done = bf16[1,2048,11264]{2,1,0:T(8,128)(2,1)} async-done(((bf16[1,256,11264]{2,1,0:T(8,128)(2,1)}), bf16[1,2048,11264]{2,1,0:T(8,128)(2,1)}) %all-gather.15.cloned.1.call-update) | async-done | bytes 46137360 | tf_op jit(solution)/shard_map/all_gather | solution.py:496
  681.4 91.4 %expert.5 = (bf16[544,2048]{1,0:T(8,128)(2,1)}, bf16[544,2048]{1,0:T(8,128)(2,1)}) custom-call(bf16[544,2048]{1,0:T(8,128)(2,1)} %bitcast.72.x_ref, bf16[544,2048]{1,0:T(8,128)(2,1)} %multiply_convert_fusion.c_ref, bf16[2048,11264]{1,0:T(8,128)(2,1)} %bitcast.309, bf16[2048,11264]{1,0:T(8,128)(2,1)} %bitcast.310, ...), custom_call_target="tpu_custom_call" | custom-call | tf_op jit(solution)/shard_map/expert/pallas_call | solution.py:328
  772.8 53.4 %all_to_all.149 = bf16[4,136,2048]{2,1,0:T(8,128)(2,1)} all-to-all(bf16[4,136,2048]{2,1,0:T(8,128)(2,1)} %bitcast.350), channel_id=1, replica_groups=mesh['dp'=8,'expert'=4] {'expert'}, dimensions={0} | all-to-all | bytes 4456448 | tf_op jit(solution)/shard_map/all_to_all | solution.py:91
  843.9 66.3 %expert.3 = (f32[544,2048]{1,0:T(8,128)}, f32[544,2048]{1,0:T(8,128)}) custom-call(bf16[544,2048]{1,0:T(8,128)(2,1)} %bitcast.322, bf16[544,2048]{1,0:T(8,128)(2,1)} %multiply_convert_fusion.1.c_ref, bf16[2048,8192]{1,0:T(8,128)(2,1)} %all-gather.13.cloned.1.call-done.wg_ref.wu_ref, bf16[2048,8192]{1,0:T(8,128)(2,1)} %all-gather.13.cloned.1.call-done.wg_ref.wu_ref, ...), custom_call_target="tpu_custom_call" | custom-call | tf_op jit(solution)/shard_map/expert/pallas_call | solution.py:328
  917.9 35.4 %expert.4 = (bf16[544,2048]{1,0:T(8,128)(2,1)}, bf16[544,2048]{1,0:T(8,128)(2,1)}) custom-call(bf16[544,2048]{1,0:T(8,128)(2,1)} %bitcast.323, bf16[544,2048]{1,0:T(8,128)(2,1)} %multiply_convert_fusion.1.c_ref, bf16[2048,3072]{1,0:T(8,128)(2,1)} %all-gather.9.cloned.1.call-done.wg_ref.wu_ref, bf16[2048,3072]{1,0:T(8,128)(2,1)} %all-gather.9.cloned.1.call-done.wg_ref.wu_ref, ...), custom_call_target="tpu_custom_call" | custom-call | tf_op jit(solution)/shard_map/expert/pallas_call | solution.py:328
  969.5 41.8 %all-to-all-done.8 = bf16[4,136,2048]{2,1,0:T(8,128)(2,1)S(1)} async-done(((bf16[4,136,2048]{2,1,0:T(8,128)(2,1)}), bf16[4,136,2048]{2,1,0:T(8,128)(2,1)S(1)}, u32[]{:S(2)}, u32[]{:S(2)}) %all-to-all-start.8) | async-done | bytes 2228256 | tf_op jit(solution)/shard_map/all_to_all | solution.py:91
  1036.9 42.9 %all-to-all-done.9 = bf16[4,136,2048]{2,1,0:T(8,128)(2,1)S(1)} async-done(((bf16[4,136,2048]{2,1,0:T(8,128)(2,1)}), bf16[4,136,2048]{2,1,0:T(8,128)(2,1)S(1)}, u32[]{:S(2)}, u32[]{:S(2)}) %all-to-all-start.9) | async-done | bytes 2228256 | tf_op jit(solution)/shard_map/all_to_all | solution.py:91
  1107.1 31.9 %attend_back.2 = (bf16[2,272,2048]{2,1,0:T(8,128)(2,1)}, bf16[1024,2048]{1,0:T(8,128)(2,1)}, bf16[1024,2048]{1,0:T(8,128)(2,1)}) custom-call(bf16[2,2,272,2048]{3,2,1,0:T(8,128)(2,1)} %get-tuple-element.49.q_ref, bf16[2,1024,4096]{2,1,0:T(8,128)(2,1)} %bitcast.305, bf16[2,1024,4096]{2,1,0:T(8,128)(2,1)} %bitcast.306, ...), custom_call_target="tpu_custom_call" | custom-call | tf_op jit(solution)/shard_map/attend_back/pallas_call | solution.py:249
  1139.0 45.1 %last_grad.2 = (bf16[1024,2048]{1,0:T(8,128)(2,1)}, bf16[1024,128]{1,0:T(8,128)(2,1)}) custom-call(bf16[1024,2048]{1,0:T(8,128)(2,1)} %get-tuple-element.55.dk_ref, bf16[1024,2048]{1,0:T(8,128)(2,1)} %get-tuple-element.56.dv_ref, bf16[2,272,2048]{2,1,0:T(8,128)(2,1)} %get-tuple-element.57.dq_ref, bf16[2,1024,544]{2,1,0:T(8,128)(2,1)} %fusion.8.table_ref, ...), custom_call_target="tpu_custom_call" | custom-call | tf_op jit(solution)/shard_map/last_grad/pallas_call | solution.py:422
  1199.2 31.9 %attend_back.3 = (bf16[2,272,2048]{2,1,0:T(8,128)(2,1)}, bf16[1024,2048]{1,0:T(8,128)(2,1)}, bf16[1024,2048]{1,0:T(8,128)(2,1)}) custom-call(bf16[2,2,272,2048]{3,2,1,0:T(8,128)(2,1)} %get-tuple-element.49.q_ref, bf16[2,1024,4096]{2,1,0:T(8,128)(2,1)} %bitcast.307, bf16[2,1024,4096]{2,1,0:T(8,128)(2,1)} %bitcast.308, ...), custom_call_target="tpu_custom_call" | custom-call | tf_op jit(solution)/shard_map/attend_back/pallas_call | solution.py:249
  1231.1 45.1 %last_grad.3 = (bf16[1024,2048]{1,0:T(8,128)(2,1)}, bf16[1024,128]{1,0:T(8,128)(2,1)}) custom-call(bf16[1024,2048]{1,0:T(8,128)(2,1)} %get-tuple-element.65.dk_ref, bf16[1024,2048]{1,0:T(8,128)(2,1)} %get-tuple-element.66.dv_ref, bf16[2,272,2048]{2,1,0:T(8,128)(2,1)} %get-tuple-element.67.dq_ref, bf16[2,1024,544]{2,1,0:T(8,128)(2,1)} %fusion.8.table_ref, ...), custom_call_target="tpu_custom_call" | custom-call | tf_op jit(solution)/shard_map/last_grad/pallas_call | solution.py:422
  1297.1 42.0 %all_to_all.150 = f32[4,256,192]{1,2,0:T(8,128)S(1)} all-to-all(f32[4,256,192]{1,2,0:T(8,128)S(1)} %copy.221), channel_id=1, replica_groups=mesh['dp'=8,'expert'=4] {'expert'}, dimensions={0} | all-to-all | bytes 1572864 | tf_op jit(solution)/shard_map/all_to_all | solution.py:91
  1367.0 91.8 %all-to-all-done.11 = bf16[4,136,2048]{2,1,0:T(8,128)(2,1)S(1)} async-done(((bf16[4,136,2048]{2,1,0:T(8,128)(2,1)}), bf16[4,136,2048]{2,1,0:T(8,128)(2,1)S(1)}, u32[]{:S(2)}, u32[]{:S(2)}) %all-to-all-start.11) | async-done | bytes 2228256 | tf_op jit(solution)/shard_map/all_to_all | solution.py:91
  1464.2 22.3 %reduce-scatter.3.cloned.1.call-done = bf16[256,2048]{1,0:T(8,128)(2,1)} async-done(((bf16[1024,2048]{1,0:T(8,128)(2,1)}), bf16[256,2048]{1,0:T(8,128)(2,1)}) %reduce-scatter.3.cloned.1.call-update) | async-done | bytes 1048592 | tf_op jit(solution)/shard_map/reduce_scatter | solution.py:712
  (371 shorter events, 413.5 us)
Async XLA Ops:
  7.2 241.5 %all-gather.7.cloned.1.call-start = ((), (), s32[]{:S(2)}) async-start(), calls=%async_computation.16 | async-start | bytes 56623104 | tf_op jit(solution)/shard_map/all_gather | solution.py:490
  14.8 624.3 %all-gather.11.cloned.1.call-start = ((), (), s32[]{:S(2)}) async-start(), calls=%async_computation.18 | async-start | bytes 51904512 | tf_op jit(solution)/shard_map/all_gather | solution.py:491
  15.5 665.9 %all-gather.15.cloned.1.call-start = ((), (), s32[]{:S(2)}) async-start(), calls=%async_computation.22 | async-start | bytes 51904512 | tf_op jit(solution)/shard_map/all_gather | solution.py:496
  21.1 822.9 %all-gather.13.cloned.1.call-start = ((), (), s32[]{:S(2)}) async-start(), calls=%async_computation.19 | async-start | bytes 37748736 | tf_op jit(solution)/shard_map/all_gather | solution.py:503
  39.2 45.6 %collective-permute-start.1 = (bf16[2,256,2048]{2,1,0:T(8,128)(2,1)S(1)}, bf16[2,256,2048]{2,1,0:T(8,128)(2,1)}, u32[]{:S(2)}, u32[]{:S(2)}) collective-permute-start(bf16[2,256,2048]{2,1,0:T(8,128)(2,1)S(1)} %copy-done.18), channel_id=1, source_target_pairs={{1,0},{2,1},{3,2},{5,4},{6,5},{7,6},{9,8},{10,9},{11,10},{13,12},{... | collective-permute-start | bytes 6291464 | tf_op jit(solution)/shard_map/ppermute | solution.py:82
  41.1 45.9 %collective-permute-start = (bf16[2,256,2048]{2,1,0:T(8,128)(2,1)S(1)}, bf16[2,256,2048]{2,1,0:T(8,128)(2,1)}, u32[]{:S(2)}, u32[]{:S(2)}) collective-permute-start(bf16[2,256,2048]{2,1,0:T(8,128)(2,1)S(1)} %copy-done.18), channel_id=1, source_target_pairs={{0,1},{1,2},{2,3},{4,5},{5,6},{6,7},{8,9},{9,10},{10,11},{12,13},{... | collective-permute-start | bytes 6291464 | tf_op jit(solution)/shard_map/ppermute | solution.py:81
  84.8 44.9 %collective-permute-start.2 = (bf16[2,256,2048]{2,1,0:T(8,128)(2,1)}, bf16[2,256,2048]{2,1,0:T(8,128)(2,1)}, u32[]{:S(2)}, u32[]{:S(2)}) collective-permute-start(bf16[2,256,2048]{2,1,0:T(8,128)(2,1)} %collective-permute-done.1), channel_id=1, source_target_pairs={{1,0},{2,1},{3,2},{5,4},{6,5},{7,6},{9,8},{10,9},{11,10},{13,12},{... | collective-permute-start | bytes 6291464 | tf_op jit(solution)/shard_map/ppermute | solution.py:82
  87.1 45.6 %collective-permute-start.4 = (bf16[2,256,2048]{2,1,0:T(8,128)(2,1)}, bf16[2,256,2048]{2,1,0:T(8,128)(2,1)}, u32[]{:S(2)}, u32[]{:S(2)}) collective-permute-start(bf16[2,256,2048]{2,1,0:T(8,128)(2,1)} %collective-permute-done), channel_id=1, source_target_pairs={{0,1},{1,2},{2,3},{4,5},{5,6},{6,7},{8,9},{9,10},{10,11},{12,13},{... | collective-permute-start | bytes 6291464 | tf_op jit(solution)/shard_map/ppermute | solution.py:81
  129.8 44.1 %collective-permute-start.3 = (bf16[2,256,2048]{2,1,0:T(8,128)(2,1)}, bf16[2,256,2048]{2,1,0:T(8,128)(2,1)}, u32[]{:S(2)}, u32[]{:S(2)}) collective-permute-start(bf16[2,256,2048]{2,1,0:T(8,128)(2,1)} %collective-permute-done.2), channel_id=1, source_target_pairs={{1,0},{2,1},{3,2},{5,4},{6,5},{7,6},{9,8},{10,9},{11,10},{13,12},{... | collective-permute-start | bytes 6291464 | tf_op jit(solution)/shard_map/ppermute | solution.py:82
  132.6 57.4 %collective-permute-start.5 = (bf16[2,256,2048]{2,1,0:T(8,128)(2,1)}, bf16[2,256,2048]{2,1,0:T(8,128)(2,1)S(1)}, u32[]{:S(2)}, u32[]{:S(2)}) collective-permute-start(bf16[2,256,2048]{2,1,0:T(8,128)(2,1)} %collective-permute-done.4), channel_id=1, source_target_pairs={{0,1},{1,2},{2,3},{4,5},{5,6},{6,7},{8,9},{9,10},{10,11},{12,13},{... | collective-permute-start | bytes 6291464 | tf_op jit(solution)/shard_map/ppermute | solution.py:81
  196.6 205.2 %all-to-all-start.5 = ((bf16[4,136,2048]{2,1,0:T(8,128)(2,1)}), bf16[4,136,2048]{2,1,0:T(8,128)(2,1)}, u32[]{:S(2)}, u32[]{:S(2)}) async-start(bf16[4,136,2048]{2,1,0:T(8,128)(2,1)} %bitcast.75), calls=%async_computation.5 | async-start | bytes 4456448 | tf_op jit(solution)/shard_map/all_to_all | solution.py:91
  401.8 50.0 %all-to-all-start = ((bf16[4,136,2048]{2,1,0:T(8,128)(2,1)}), bf16[4,136,2048]{2,1,0:T(8,128)(2,1)S(1)}, u32[]{:S(2)}, u32[]{:S(2)}) async-start(bf16[4,136,2048]{2,1,0:T(8,128)(2,1)} %bitcast.347), calls=%async_computation | async-start | bytes 4456448 | tf_op jit(solution)/shard_map/all_to_all | solution.py:91
  406.4 511.5 %all-gather.9.cloned.1.call-start = ((), (), s32[]{:S(2)}) async-start(), calls=%async_computation.17 | async-start | bytes 14155776 | tf_op jit(solution)/shard_map/all_gather | solution.py:503
  453.1 56.0 %all-to-all-start.1 = ((bf16[4,136,2048]{2,1,0:T(8,128)(2,1)}), bf16[4,136,2048]{2,1,0:T(8,128)(2,1)}, u32[]{:S(2)}, u32[]{:S(2)}) async-start(bf16[4,136,2048]{2,1,0:T(8,128)(2,1)} %bitcast.349), calls=%async_computation.1 | async-start | bytes 4456448 | tf_op jit(solution)/shard_map/all_to_all | solution.py:91
  509.1 54.4 %all-to-all-start.3 = ((bf16[4,136,2048]{2,1,0:T(8,128)(2,1)}), bf16[4,136,2048]{2,1,0:T(8,128)(2,1)S(1)}, u32[]{:S(2)}, u32[]{:S(2)}) async-start(bf16[4,136,2048]{2,1,0:T(8,128)(2,1)} %bitcast.345), calls=%async_computation.3 | async-start | bytes 4456448 | tf_op jit(solution)/shard_map/all_to_all | solution.py:91
  564.9 54.9 %all-to-all-start.4 = ((bf16[4,136,2048]{2,1,0:T(8,128)(2,1)}), bf16[4,136,2048]{2,1,0:T(8,128)(2,1)}, u32[]{:S(2)}, u32[]{:S(2)}) async-start(bf16[4,136,2048]{2,1,0:T(8,128)(2,1)} %bitcast.351), calls=%async_computation.4 | async-start | bytes 4456448 | tf_op jit(solution)/shard_map/all_to_all | solution.py:91
  619.9 152.9 %all-to-all-start.2 = ((bf16[4,136,2048]{2,1,0:T(8,128)(2,1)}), bf16[4,136,2048]{2,1,0:T(8,128)(2,1)S(1)}, u32[]{:S(2)}, u32[]{:S(2)}) async-start(bf16[4,136,2048]{2,1,0:T(8,128)(2,1)} %bitcast.341), calls=%async_computation.2 | async-start | bytes 4456448 | tf_op jit(solution)/shard_map/all_to_all | solution.py:91
  826.2 132.5 %all-to-all-start.7 = ((bf16[4,136,2048]{2,1,0:T(8,128)(2,1)}), bf16[4,136,2048]{2,1,0:T(8,128)(2,1)}, u32[]{:S(2)}, u32[]{:S(2)}) async-start(bf16[4,136,2048]{2,1,0:T(8,128)(2,1)} %bitcast.342), calls=%async_computation.7 | async-start | bytes 4456448 | tf_op jit(solution)/shard_map/all_to_all | solution.py:91
  958.7 52.6 %all-to-all-start.8 = ((bf16[4,136,2048]{2,1,0:T(8,128)(2,1)}), bf16[4,136,2048]{2,1,0:T(8,128)(2,1)S(1)}, u32[]{:S(2)}, u32[]{:S(2)}) async-start(bf16[4,136,2048]{2,1,0:T(8,128)(2,1)} %bitcast.348), calls=%async_computation.8 | async-start | bytes 4456448 | tf_op jit(solution)/shard_map/all_to_all | solution.py:91
  1026.5 53.3 %all-to-all-start.9 = ((bf16[4,136,2048]{2,1,0:T(8,128)(2,1)}), bf16[4,136,2048]{2,1,0:T(8,128)(2,1)S(1)}, u32[]{:S(2)}, u32[]{:S(2)}) async-start(bf16[4,136,2048]{2,1,0:T(8,128)(2,1)} %bitcast.335), calls=%async_computation.9 | async-start | bytes 4456448 | tf_op jit(solution)/shard_map/all_to_all | solution.py:91
  1081.1 103.0 %all-to-all-start.10 = ((bf16[4,136,2048]{2,1,0:T(8,128)(2,1)}), bf16[4,136,2048]{2,1,0:T(8,128)(2,1)S(1)}, u32[]{:S(2)}, u32[]{:S(2)}) async-start(bf16[4,136,2048]{2,1,0:T(8,128)(2,1)} %bitcast.333), calls=%async_computation.10 | async-start | bytes 4456448 | tf_op jit(solution)/shard_map/all_to_all | solution.py:91
  1088.6 375.7 %reduce-scatter.5.cloned.1.call-start = ((), (), s32[]{:S(2)}) async-start(), calls=%async_computation.21 | async-start | bytes 5242880 | tf_op jit(solution)/shard_map/reduce_scatter | solution.py:712
  1276.3 210.2 %reduce-scatter.3.cloned.1.call-start = ((), (), s32[]{:S(2)}) async-start(), calls=%async_computation.20 | async-start | bytes 5242880 | tf_op jit(solution)/shard_map/reduce_scatter | solution.py:712
  1351.1 107.7 %all-to-all-start.11 = ((bf16[4,136,2048]{2,1,0:T(8,128)(2,1)}), bf16[4,136,2048]{2,1,0:T(8,128)(2,1)S(1)}, u32[]{:S(2)}, u32[]{:S(2)}) async-start(bf16[4,136,2048]{2,1,0:T(8,128)(2,1)} %bitcast.340), calls=%async_computation.11 | async-start | bytes 4456448 | tf_op jit(solution)/shard_map/all_to_all | solution.py:91
  (71 other events, 2751.1 us)
Sparse Core Ops, SparseCore 0:
  14.9 233.7 all-gather.6
  250.6 214.1 all-gather.10
  466.7 214.6 all-gather.14
  683.1 160.7 all-gather.12
  845.7 72.1 all-gather.8
  1276.4 112.9 reduce-scatter.4
  1391.7 94.7 reduce-scatter.2

commit v3 on v2

--- a/solution.py
+++ b/solution.py
@@ -85,6 +85,28 @@
         piece = jnp.where(here >= step, from_left[step], from_right[size - step])
         total = put(total, piece, lax.rem(here - step + size, size))
     return total
+
+
+def exchange(total, axis, size, bit):
+    other = lax.ppermute(total, axis, [(i, i ^ bit) for i in range(size)])
+    low = jnp.bitwise_and(lax.axis_index(axis), bit) == 0
+    return jnp.stack([jnp.where(low, total, other), jnp.where(low, other, total)])
+
+
+def halves_bits(size):
+    bits = [1 << k for k in range(1, size.bit_length() - 1)]
+    return [bits + [1], bits[::-1] + [1]]
+
+
+def in_order(halves, orders, size):
+    made = []
+    for total, bits in zip(halves, orders):
+        count = len(bits)
+        order = sorted(range(count), key=lambda d: -bits[count - 1 - d])
+        total = total.transpose(*order, *range(count, total.ndim))
+        made.append(total.reshape(size, *total.shape[count:]))
+    whole = jnp.stack(made, axis=1)
+    return whole.reshape(-1, whole.shape[-1])
 
 
 def send(buffer):
@@ -393,7 +415,7 @@
 def last_body(
     locals_, seq_len, dk_ref, dv_ref, dq_ref, table_ref, dots_ref, weigh_ref, mask_ref, up_ref, router_ref, down_ref, w_ref, *refs
 ):
-    wq_refs, (out_ref, low_ref) = refs[:locals_], refs[locals_:]
+    wq_refs, (out_ref, low_ref, source_ref, weigh_low_ref) = refs[:locals_], refs[locals_:]
     width = dk_ref.shape[1]
     slots = dq_ref.shape[1]
 
@@ -401,16 +423,19 @@
     def _():
         low = mm(dk_ref[...], up_ref[:width, :]) + mm(dv_ref[...], up_ref[width:, :])
         low_ref[...] = (low * mask_ref[...]).astype(BF16)
-
+        for l in range(locals_):
+            weigh = weigh_ref[l] * dots_ref[l]
+            high = weigh.astype(BF16)
+            weigh_low_ref[l, :, :EXPERTS] = high
+            weigh_low_ref[l, :, EXPERTS:] = (weigh - high.astype(F32)).astype(BF16)
+
+    router = jnp.concatenate([router_ref[...]] * 2, axis=1)
+    for l in range(locals_):
+        source = mm(dq_ref[l], wq_refs[l][...], NT) + mm(weigh_low_ref[l], router, NT)
+        source_ref[pl.ds(l * slots, slots), :] = source.astype(BF16)
     total = mm(dk_ref[...], w_ref[:, :width], NT) + mm(dv_ref[...], w_ref[:, width:], NT)
     total += mm(low_ref[...], down_ref[...], NT)
-    router = router_ref[...]
-    for l in range(locals_):
-        weigh = weigh_ref[l] * dots_ref[l]
-        high = weigh.astype(BF16)
-        low = (weigh - high.astype(F32)).astype(BF16)
-        source = mm(dq_ref[l], wq_refs[l][...], NT) + mm(high, router, NT) + mm(low, router, NT)
-        total += mm(table_ref[0, :, pl.ds(l * slots, slots)], source.astype(BF16))
+    total += mm(table_ref[0], source_ref[...])
     out_ref[...] = total.astype(BF16)
 
 
@@ -447,9 +472,76 @@
             jax.ShapeDtypeStruct((seq_len, width), BF16),
             jax.ShapeDtypeStruct((seq_len, ranks), BF16),
         ],
+        scratch_shapes=[
+            pltpu.VMEM((locals_ * slots, tile), BF16),
+            pltpu.VMEM((locals_, slots, 2 * EXPERTS), BF16),
+        ],
         compiler_params=params("arbitrary"),
         name="last_grad",
     )(dk, dv, dq, table, dots, weigh, mask, adapt_up, router, adapt_down, weights, *([weights] * locals_))
+
+
+def middle_back_body(back_ref, table_ref, part_ref, middle_ref, cot_ref, gain_ref, spread_ref, out_ref, rows_ref):
+    middle = middle_ref[...]
+    scale = rms_scale(middle)
+    grad = part_ref[...] + mm(table_ref[...], back_ref[...])
+    out = cot_ref[...].astype(F32) + norm_back(middle, scale, gain_ref[...], grad)
+    out_ref[...] = out
+    rows_ref[...] = mm(spread_ref[...], out.astype(BF16)).astype(BF16)
+
+
+def middle_back(s, back, table, part, middle, cotangent, gain, spread):
+    _, rows, width = middle.shape
+    slots = spread.shape[1]
+
+    def one(array):
+        return once((None, *array.shape[1:]), lambda i: (s, 0, 0))
+
+    return pl.pallas_call(
+        middle_back_body,
+        grid=(1,),
+        in_specs=[
+            once(back.shape, lambda i: (0, 0)),
+            one(table),
+            one(part),
+            one(middle),
+            one(cotangent),
+            once(gain.shape, lambda i: (0, 0)),
+            one(spread),
+        ],
+        out_specs=[once((rows, width), lambda i: (0, 0)), once((slots, width), lambda i: (0, 0))],
+        out_shape=[
+            jax.ShapeDtypeStruct((rows, width), F32),
+            jax.ShapeDtypeStruct((slots, width), BF16),
+        ],
+        compiler_params=params("arbitrary"),
+        name="middle_back",
+    )(back, table, part, middle, cotangent, gain, spread)
+
+
+def input_back_body(grad_ref, middle_ref, tokens_ref, gain_ref, *refs):
+    tokens = tokens_ref[...].astype(F32)
+    refs[-1][...] = middle_ref[...] + norm_back(
+        tokens, rms_scale(tokens), gain_ref[...], grad_ref[...].astype(F32)
+    )
+
+
+def input_back(s, grad, grad_middle, tokens, gain, total):
+    seqs, rows, width = tokens.shape
+    tile = 128
+    flat = pl.BlockSpec((tile, width), lambda i: (i, 0))
+    one = pl.BlockSpec((None, tile, width), lambda i: (s, i, 0))
+    return pl.pallas_call(
+        input_back_body,
+        grid=(rows // tile,),
+        in_specs=[flat, flat, one, pl.BlockSpec((1, width), lambda i: (0, 0))]
+        + ([] if total is None else [pl.BlockSpec(memory_space=pl.ANY)]),
+        out_specs=one,
+        out_shape=jax.ShapeDtypeStruct(tokens.shape, F32),
+        input_output_aliases={} if total is None else {4: 0},
+        compiler_params=params("arbitrary"),
+        name="input_back",
+    )(grad, grad_middle, tokens, gain, *([] if total is None else [total]))
 
 
 def per_device(
@@ -489,18 +581,21 @@
     )
     near_full = lax.all_gather(near, "dp", axis=0, tiled=True)
     down_full = lax.all_gather(down_weight, "dp", axis=1, tiled=True)
-    cut = (FF * 3 // 4) // 512 * 512
-    inner_full = []
+    groups = width // kv_weight.shape[0]
+
+    def stretch(array, l, low, high):
+        return jnp.concatenate([array[l, :, low:high], array[l, :, FF + low : FF + high]], axis=1)
+
+    inner_full, beside = [], []
     for l in range(locals_):
+        pieces = []
+        cut = 3 * 512 if l + 1 < locals_ else FF * 3 // 4 // 512 * 512
         if l + 1 < locals_:
-            pieces = [(0, lax.all_gather(inner_weight[l], "dp", axis=0, tiled=True))]
+            pieces.append((0, None))
+            beside.append(stretch(inner_weight, l, 0, cut))
         else:
-            pieces = []
-            for low, high in ((0, cut), (cut, FF)):
-                part = jnp.concatenate(
-                    [inner_weight[l, :, low:high], inner_weight[l, :, FF + low : FF + high]], axis=1
-                )
-                pieces.append((low, lax.all_gather(part, "dp", axis=0, tiled=True)))
+            pieces.append((0, lax.all_gather(stretch(inner_weight, l, 0, cut), "dp", axis=0, tiled=True)))
+        pieces.append((cut, lax.all_gather(stretch(inner_weight, l, cut, FF), "dp", axis=0, tiled=True)))
         inner_full.append(pieces)
 
     routes = lax.all_gather(
@@ -576,7 +671,7 @@
         sums = mm(table, jnp.concatenate([both, jnp.ones_like(both)], axis=1))
         other_sum.append((sums[:, :1], sums[:, 1:]))
 
-    hidden_first, routes = lax.optimization_barrier((hidden_in, routes))
+    hidden_first, routes, adapters = lax.optimization_barrier((hidden_in, routes, adapters))
     everyone = gather_line(
         hidden_first,
         "expert",
@@ -586,6 +681,15 @@
     ).reshape(seqs, seq_len, width)
 
     flat_cot, everyone = lax.optimization_barrier((cotangent, everyone))
+    orders = halves_bits(groups)
+    beside = [[block[: block.shape[0] // 2], block[block.shape[0] // 2 :]] for block in beside]
+
+    def exchange_all(step):
+        return [
+            [exchange(half, "dp", groups, bits[step]) for half, bits in zip(halves, orders)]
+            for halves in beside
+        ]
+
     flat_cot = flat_cot.reshape(seqs * row_count, width)
     cot_rows = [send(mm(own_spread_m[l], flat_cot).astype(BF16)) for l in range(locals_)]
 
@@ -645,6 +749,11 @@
     query_rot, attended, probs = attend(
         queries.reshape(locals_, seqs, slots, width), key_value, cos_q, sin_q, query_blocks, key_blocks
     )
+    beside, attended = lax.optimization_barrier((beside, attended))
+    for step in range(len(orders[0])):
+        beside = exchange_all(step)
+    for l, halves in enumerate(beside):
+        inner_full[l][0] = (0, in_order(halves, orders, groups))
     gate_rows = gate_a[..., None]
     projected, gated = project(
         attended.reshape(locals_, seqs * slots, width),
@@ -658,7 +767,6 @@
     to_send = jnp.asarray(np.eye(locals_ * slots)[order], BF16)
     to_slots = jnp.asarray(np.eye(locals_ * slots)[order].T, BF16)
     tokens = hidden_in.astype(F32)
-    upstream = cotangent.astype(F32)
     middles = []
     for s in range(seqs):
         back = send(mm(to_send, gated[:, s].reshape(locals_ * slots, width)).astype(BF16))
@@ -681,61 +789,74 @@
         grad_rows = (gate_m * cot_rows[l].astype(F32)).astype(BF16)
         made = None
         for at, (low, inner) in enumerate(inner_full[l]):
+            if held is not None and at + 1 == len(inner_full[l]):
+                held, made = lax.optimization_barrier((held, made))
+                final = final + mm(own_collect_m[l - 1], held)
             ends = (cot_rows[l], gate_m, pick_m, mlp_router) if at + 1 == len(inner_full[l]) else None
             made = expert_pass(rows_in, grad_rows, inner, down_full, l, low, made, ends)
         gated_out, grad_source = made
-        if held is not None:
-            final = final + mm(own_collect_m[l - 1], held)
-            grad_source, final = lax.optimization_barrier((grad_source, final))
         grad_back = send(grad_source)
-        grad_normed_two = grad_normed_two + mm(own_collect_m[l], grad_back)
+        if l + 1 < locals_:
+            grad_normed_two = grad_normed_two + mm(own_collect_m[l], grad_back)
         held = send(gated_out) if l + 1 < locals_ else gated_out
     grad_normed_two = grad_normed_two.reshape(seqs, row_count, width)
-    grad_middle = upstream + norm_back(middle, scale_two, mlp_gain, grad_normed_two)
-
-    arrived = [send(mm(own_spread_a[s], grad_middle[s].astype(BF16)).astype(BF16)) for s in range(seqs)]
-    input_grads, down_pieces, up_pieces = [], [], []
-    mask = own_adapter.astype(F32)[:, None, :]
+    late = (collect_a, own_adapter.astype(F32)[:, None, :], weigh_a, attn_router, to_slots)
+    (collect_a, mask, weigh_a, router_near, to_slots), grad_normed_two = lax.optimization_barrier(
+        (late, grad_normed_two)
+    )
+    back_table = own_collect_m[locals_ - 1].reshape(seqs, row_count, mlp_rows)
+    grad_middle, leaving = [], []
+    for s in range(seqs):
+        grad, rows = middle_back(
+            s, grad_back, back_table, grad_normed_two, middle, cotangent, mlp_gain[None], own_spread_a
+        )
+        grad_middle.append(grad)
+        leaving.append(rows)
+
+    arrived = [send(leaving[0])]
+    arrived[0], held, leaving[1:] = lax.optimization_barrier((arrived[0], held, leaving[1:]))
+    held = send(held)
+    down_pieces, up_pieces = [], []
+    input_grad = None
     for s in range(seqs):
         grad_attended, dots = out_back(
             s, arrived[s], to_slots, gate_rows, projected, near_full, output_column
         )
         dq, dk, dv = attend_back(s, query_rot, key_value, grad_attended, probs, cos_q, sin_q, cos_k, sin_k)
+        if s + 1 < seqs:
+            leaving[s + 1], held, dk = lax.optimization_barrier((leaving[s + 1], held, dk))
+            arrived.append(send(leaving[s + 1]))
         part, grad_low = last_grad(
-            s, dk, dv, dq, collect_a, dots, weigh_a, mask, adapt_up, attn_router, adapt_down, near_full,
+            s, dk, dv, dq, collect_a, dots, weigh_a, mask, adapt_up, router_near, adapt_down, near_full,
             query_column,
         )
         if s + 1 < seqs:
-            part, arrived[s + 1] = lax.optimization_barrier((part, arrived[s + 1]))
-        if s + 2 == seqs:
-            held, part = lax.optimization_barrier((held, part))
-        grad_normed = lax.psum_scatter(part, "expert", scatter_dimension=0, tiled=True).astype(F32)
-        input_grads.append(
-            grad_middle[s] + norm_back(tokens[s], rms_scale(tokens[s]), attn_gain, grad_normed)
-        )
+            arrived[s + 1], part = lax.optimization_barrier((arrived[s + 1], part))
+        grad_normed = lax.psum_scatter(part, "expert", scatter_dimension=0, tiled=True)
+        input_grad = input_back(s, grad_normed, grad_middle[s], hidden_in, attn_gain[None], input_grad)
         first = adapter_index[s] * RANK
         down_pieces.append(lax.dynamic_slice_in_dim(mm(grad_low, normed_low[s], TN), first, RANK, 0))
         up_piece = jnp.concatenate([mm(low_rank[s], dk, TN), mm(low_rank[s], dv, TN)], axis=1)
         up_pieces.append(lax.dynamic_slice_in_dim(up_piece, first, RANK, 0))
-    final = final + mm(own_collect_m[locals_ - 1], send(held))
+    final = final + mm(own_collect_m[locals_ - 1], held)
     layer_out = final.astype(BF16).reshape(seqs, row_count, width)
 
-    groups = adapters.shape[0] // seqs
     down_part = width // (groups * ranks)
     pieces = jnp.concatenate(
         [
-            jnp.stack(down_pieces).reshape(seqs, RANK, groups, ranks, down_part),
-            jnp.stack(up_pieces).reshape(seqs, RANK, groups, ranks, 2 * down_part),
+            jnp.stack(down_pieces).reshape(seqs * RANK, groups, ranks, down_part),
+            jnp.stack(up_pieces).reshape(seqs * RANK, groups, ranks, 2 * down_part),
         ],
         axis=-1,
     )
-    pieces = pieces.transpose(3, 2, 0, 1, 4).reshape(ranks, groups * seqs * RANK, 3 * down_part)
-    pieces = jnp.sum(send(pieces), axis=0).reshape(groups, seqs * RANK, 3 * down_part)
+    pieces = pieces.transpose(1, 0, 2, 3).reshape(groups, seqs * RANK, 3 * ranks * down_part)
     pieces = lax.all_to_all(pieces, "dp", split_axis=0, concat_axis=0, tiled=True)
-    pieces = pieces.reshape(groups * seqs, RANK, 3 * down_part)
+    pieces = pieces.reshape(groups * seqs, RANK, 3 * ranks * down_part)
     belongs = (adapters[:, None] == jnp.arange(NADAPT, dtype=jnp.int32)[None, :]).astype(F32)
-    sums = jnp.einsum("qkf,qa->fak", pieces, belongs, precision=PRECISE).reshape(3 * down_part, NADAPT * RANK)
-    return (layer_out, jnp.stack(input_grads), sums[:down_part], sums[down_part:])
+    sums = jnp.einsum("qkf,qa->akf", pieces, belongs, precision=PRECISE)
+    sums = sums.reshape(NADAPT * RANK, ranks, 3 * down_part).transpose(1, 0, 2)
+    sums = jnp.sum(send(sums), axis=0).T
+    return (layer_out, input_grad, sums[:down_part], sums[down_part:])
 
 
 def solution(mesh):

time: 1510 us -> 1360 us (0.901)
  waiting for transfers between devices: 521 us -> 349 us
  blocking collectives: 124 us -> 71.4 us
  other arithmetic: 71.6 us -> 103 us
  starting transfers between devices: 91.1 us -> 116 us
  Pallas kernels: 520 us -> 540 us
  matrix products: 92.5 us -> 77.1 us
    all_to_all x11 -> x12, waiting for transfers between devices: 331 us -> 169 us  [send(): lax.all_to_all(buffer, 'expert', split_axis=0, concat_axis=0, tiled=True)]
    ppermute x0 -> x6, waiting for transfers between devices: none -> 59.3 us  [exchange(): other = lax.ppermute(total, axis, [(i, i ^ bit) for i in range(size)])]
    all_gather x3, waiting for transfers between devices: 57.5 us -> 0.67 us  [the longest x2 0.67 us: per_device(): lax.all_gather(stretch(inner_weight, l, cut, FF), 'dp', axis=0, tiled=True)]
    all_to_all x2 -> x1, blocking collectives: 95.4 us -> 52.8 us  [send(): lax.all_to_all(buffer, 'expert', split_axis=0, concat_axis=0, tiled=True)]
    pallas_call x0 -> x4, Pallas kernels: none -> 21.9 us  [the longest x2 14.1 us: middle_back(): pl.pallas_call(middle_back_body, grid=(1,), in_specs=[once(back.shape, la...]
    another operation x2 -> x16, other arithmetic: 5.51 us -> 27.2 us  [the longest x11 25.8 us: exchange(): jnp.stack([jnp.where(low, total, other), jnp.where(low, other, total)])]
    dot_general x26 -> x23, matrix products: 80.9 us -> 65 us  [mm(): return lax.dot_general(left, right, dims, preferred_element_type=F32)]
    pallas_call x3 -> x4, Pallas kernels: 193 us -> 204 us  [expert_pass(): pl.pallas_call(functools.partial(expert_body, start is not None, last is...]
  transfers between devices with their start and end apart: 24 -> 32, of which waited for: 15 -> 16; matrix products, arithmetic and copies ran while one was open for 12% -> 17% of each run, Pallas kernels for 29% -> 39%
where the time goes in v3:
time: 1360 us; the launch traced here: 1350 us
  Pallas kernels  540 us (40%)
  waiting for transfers between devices  349 us (26%)
  starting transfers between devices  116 us (9%)
  other arithmetic  103 us (8%)
  matrix products  77.1 us (6%)
  local copies, waits for them, and re-layouts  76 us (6%)
  blocking collectives  71.4 us (5%)
  between operations  18.1 us (1%)
    pallas_call x4, Pallas kernels, expert_pass(): pl.pallas_call(functools.partial(expert_body, start is not None, last is...  204 us
    all_to_all x12, waiting for transfers between devices, send(): lax.all_to_all(buffer, 'expert', split_axis=0, concat_axis=0, tiled=True)  169 us
    ppermute x3, waiting for transfers between devices, gather_line(): from_right.append(lax.ppermute(from_right[-1], axis, leftward))  96.6 us
    all_to_all x12, starting transfers between devices, send(): lax.all_to_all(buffer, 'expert', split_axis=0, concat_axis=0, tiled=True)  86 us
    pallas_call x2, Pallas kernels, last_grad(): pl.pallas_call(functools.partial(last_body, locals_, seq_len), grid=(widt...  77.3 us
    dot_general x23, matrix products, mm(): return lax.dot_general(left, right, dims, preferred_element_type=F32)  65 us
    pallas_call x2, Pallas kernels, attend_back(): pl.pallas_call(attend_back_body, grid=(HEADS,), in_specs=[pl.BlockSpec((l...  63.8 us
    ppermute x6, waiting for transfers between devices, exchange(): other = lax.ppermute(total, axis, [(i, i ^ bit) for i in range(size)])  59.3 us
  transfers between devices with their start and end apart: 32, of which 16 were waited for; matrix products, arithmetic and copies ran while one was open for 17% of the time, Pallas kernels for 39%

profile of v3, /device:TPU:9, one launch (start us, length us, event | category | flops | bytes accessed | tf_op | source)
XLA Modules:
  0.0 1350.5 jit_solution(882986424690734957)
XLA Ops:
  58.3 36.3 %collective-permute-done.1 = bf16[2,256,2048]{2,1,0:T(8,128)(2,1)} collective-permute-done((bf16[2,256,2048]{2,1,0:T(8,128)(2,1)S(1)}, bf16[2,256,2048]{2,1,0:T(8,128)(2,1)}, u32[]{:S(2)}, u32[]{:S(2)}) %collective-permute-start.1) | collective-permute-done | bytes 2097184 | tf_op jit(solution)/shard_map/ppermute | solution.py:82
  104.6 34.4 %collective-permute-done.2 = bf16[2,256,2048]{2,1,0:T(8,128)(2,1)} collective-permute-done((bf16[2,256,2048]{2,1,0:T(8,128)(2,1)}, bf16[2,256,2048]{2,1,0:T(8,128)(2,1)}, u32[]{:S(2)}, u32[]{:S(2)}) %collective-permute-start.2) | collective-permute-done | bytes 2097184 | tf_op jit(solution)/shard_map/ppermute | solution.py:82
  157.2 25.9 %collective-permute-done.3 = bf16[2,256,2048]{2,1,0:T(8,128)(2,1)} collective-permute-done((bf16[2,256,2048]{2,1,0:T(8,128)(2,1)}, bf16[2,256,2048]{2,1,0:T(8,128)(2,1)}, u32[]{:S(2)}, u32[]{:S(2)}) %collective-permute-start.3) | collective-permute-done | bytes 2097184 | tf_op jit(solution)/shard_map/ppermute | solution.py:82
  255.5 18.1 %project.2 = bf16[2,544,2048]{2,1,0:T(8,128)(2,1)} custom-call(bf16[2,544,2048]{2,1,0:T(8,128)(2,1)} %bitcast.348, bf16[2048,12288]{1,0:T(8,128)(2,1)} %all-gather.6.cloned.1.call-done.w_ref.refs_0_.refs_1_), custom_call_target="tpu_custom_call" | custom-call | tf_op jit(solution)/shard_map/project/pallas_call | solution.py:181
  273.6 53.0 %key_value.1 = bf16[2048,4096]{1,0:T(8,128)(2,1)} custom-call(bf16[2048,2048]{1,0:T(8,128)(2,1)} %bitcast.327, bf16[2048,128]{1,0:T(8,128)(2,1)} %bitcast.356, bf16[2048,12288]{1,0:T(8,128)(2,1)} %all-gather.6.cloned.1.call-done.w_ref.refs_0_.refs_1_, bf16[4096,128]{1,0:T(8,128)(2,1)} %up_ref.5, f32[1024,128]{1,0:T(8,128)} %get-tuple-element.192.cos_ref.ck_ref, ...), custom_call_target="tpu_custom_call" | custom-call | tf_op jit(solution)/shard_map/key_value/pallas_call | solution.py:139
  326.6 55.9 %attend.1 = (bf16[2,2,272,2048]{3,2,1,0:T(8,128)(2,1)}, bf16[2,2,272,2048]{3,2,1,0:T(8,128)(2,1)}, bf16[2,2,16,272,1024]{4,3,2,1,0:T(8,128)(2,1)}) custom-call(bf16[2,2,272,2048]{3,2,1,0:T(8,128)(2,1)} %bitcast.347, bf16[2,1024,4096]{2,1,0:T(8,128)(2,1)} %bitcast.319, bf16[2,1024,4096]{2,1,0:T(8,128)(2,1)} %bitcast.320, ...), custom_call_target="tpu_custom_call" | custom-call | tf_op jit(solution)/shard_map/attend/pallas_call | solution.py:218
  382.5 17.7 %project.3 = (bf16[2,544,2048]{2,1,0:T(8,128)(2,1)}, bf16[2,544,2048]{2,1,0:T(8,128)(2,1)}) custom-call(bf16[2,544,2048]{2,1,0:T(8,128)(2,1)} %bitcast.357, bf16[2048,12288]{1,0:T(8,128)(2,1)} %all-gather.6.cloned.1.call-done.w_ref.refs_0_.refs_1_, f32[2,544,1]{2,1,0:T(8,128)} %fusion.88.refs_0_), custom_call_target="tpu_custom_call" | custom-call | tf_op jit(solution)/shard_map/project/pallas_call | solution.py:181
  422.8 32.3 %all-to-all-done = bf16[4,136,2048]{2,1,0:T(8,128)(2,1)} async-done(((bf16[4,136,2048]{2,1,0:T(8,128)(2,1)}), bf16[4,136,2048]{2,1,0:T(8,128)(2,1)}, u32[]{:S(2)}, u32[]{:S(2)}) %all-to-all-start) | async-done | bytes 2228256 | tf_op jit(solution)/shard_map/all_to_all | solution.py:113
  470.4 20.7 %collective-permute-done.9 = bf16[128,3072]{1,0:T(8,128)(2,1)S(1)} collective-permute-done((bf16[128,3072]{1,0:T(8,128)(2,1)}, bf16[128,3072]{1,0:T(8,128)(2,1)S(1)}, u32[]{:S(2)}, u32[]{:S(2)}) %collective-permute-start.9) | collective-permute-done | bytes 786464 | tf_op jit(solution)/shard_map/ppermute | solution.py:91
  498.7 14.8 %all-to-all-done.1 = bf16[4,136,2048]{2,1,0:T(8,128)(2,1)S(1)} async-done(((bf16[4,136,2048]{2,1,0:T(8,128)(2,1)}), bf16[4,136,2048]{2,1,0:T(8,128)(2,1)S(1)}, u32[]{:S(2)}, u32[]{:S(2)}) %all-to-all-start.1) | async-done | bytes 2228256 | tf_op jit(solution)/shard_map/all_to_all | solution.py:113
  525.6 38.6 %collective-permute-done.10 = bf16[2,128,3072]{2,1,0:T(8,128)(2,1)} collective-permute-done((bf16[2,128,3072]{2,1,0:T(8,128)(2,1)}, bf16[2,128,3072]{2,1,0:T(8,128)(2,1)}, u32[]{:S(2)}, u32[]{:S(2)}) %collective-permute-start.10) | collective-permute-done | bytes 1572896 | tf_op jit(solution)/shard_map/ppermute | solution.py:91
  608.5 29.0 %all-to-all-done.2 = bf16[4,136,2048]{2,1,0:T(8,128)(2,1)} async-done(((bf16[4,136,2048]{2,1,0:T(8,128)(2,1)}), bf16[4,136,2048]{2,1,0:T(8,128)(2,1)}, u32[]{:S(2)}, u32[]{:S(2)}) %all-to-all-start.2) | async-done | bytes 2228256 | tf_op jit(solution)/shard_map/all_to_all | solution.py:113
  672.4 29.5 %expert.4 = (f32[544,2048]{1,0:T(8,128)}, f32[544,2048]{1,0:T(8,128)}) custom-call(bf16[544,2048]{1,0:T(8,128)(2,1)} %bitcast.62.x_ref, bf16[544,2048]{1,0:T(8,128)(2,1)} %multiply_convert_fusion.1.c_ref, bf16[2048,3072]{1,0:T(8,128)(2,1)} %bitcast.325, bf16[2048,3072]{1,0:T(8,128)(2,1)} %bitcast.326, bf16[2,5632,2048]{2,1,0:T(8,128)(2,1)} %all-gather.10.cloned.1.call-done.wd_ref), custom_call_target="tpu_custom_call" | custom-call | tf_op jit(solution)/shard_map/expert/pallas_call | solution.py:350
  702.0 72.2 %expert.5 = (bf16[544,2048]{1,0:T(8,128)(2,1)}, bf16[544,2048]{1,0:T(8,128)(2,1)}) custom-call(bf16[544,2048]{1,0:T(8,128)(2,1)} %bitcast.62.x_ref, bf16[544,2048]{1,0:T(8,128)(2,1)} %multiply_convert_fusion.1.c_ref, bf16[2048,8192]{1,0:T(8,128)(2,1)} %all-gather.8.cloned.1.call-done.wg_ref.wu_ref, ...), custom_call_target="tpu_custom_call" | custom-call | tf_op jit(solution)/shard_map/expert/pallas_call | solution.py:350
  774.1 52.8 %all_to_all.149 = bf16[4,136,2048]{2,1,0:T(8,128)(2,1)} all-to-all(bf16[4,136,2048]{2,1,0:T(8,128)(2,1)} %bitcast.370), channel_id=1, replica_groups=mesh['dp'=8,'expert'=4] {'expert'}, dimensions={0} | all-to-all | bytes 4456448 | tf_op jit(solution)/shard_map/all_to_all | solution.py:113
  837.1 67.4 %expert.6 = (f32[544,2048]{1,0:T(8,128)}, f32[544,2048]{1,0:T(8,128)}) custom-call(bf16[544,2048]{1,0:T(8,128)(2,1)} %bitcast.342, bf16[544,2048]{1,0:T(8,128)(2,1)} %multiply_convert_fusion.c_ref, bf16[2048,8192]{1,0:T(8,128)(2,1)} %all-gather.12.cloned.1.call-done.wg_ref.wu_ref, bf16[2048,8192]{1,0:T(8,128)(2,1)} %all-gather.12.cloned.1.call-done.wg_ref.wu_ref, ...), custom_call_target="tpu_custom_call" | custom-call | tf_op jit(solution)/shard_map/expert/pallas_call | solution.py:350
  905.2 35.2 %expert.7 = (bf16[544,2048]{1,0:T(8,128)(2,1)}, bf16[544,2048]{1,0:T(8,128)(2,1)}) custom-call(bf16[544,2048]{1,0:T(8,128)(2,1)} %bitcast.343, bf16[544,2048]{1,0:T(8,128)(2,1)} %multiply_convert_fusion.c_ref, bf16[2048,3072]{1,0:T(8,128)(2,1)} %all-gather.14.cloned.1.call-done.wg_ref.wu_ref, bf16[2048,3072]{1,0:T(8,128)(2,1)} %all-gather.14.cloned.1.call-done.wg_ref.wu_ref, ...), custom_call_target="tpu_custom_call" | custom-call | tf_op jit(solution)/shard_map/expert/pallas_call | solution.py:350
  957.4 33.9 %all-to-all-done.7 = bf16[4,136,2048]{2,1,0:T(8,128)(2,1)S(1)} async-done(((bf16[4,136,2048]{2,1,0:T(8,128)(2,1)}), bf16[4,136,2048]{2,1,0:T(8,128)(2,1)S(1)}, u32[]{:S(2)}, u32[]{:S(2)}) %all-to-all-start.7) | async-done | bytes 2228256 | tf_op jit(solution)/shard_map/all_to_all | solution.py:113
  1015.4 39.5 %all-to-all-done.9 = bf16[4,136,2048]{2,1,0:T(8,128)(2,1)S(1)} async-done(((bf16[4,136,2048]{2,1,0:T(8,128)(2,1)}), bf16[4,136,2048]{2,1,0:T(8,128)(2,1)S(1)}, u32[]{:S(2)}, u32[]{:S(2)}) %all-to-all-start.9) | async-done | bytes 2228256 | tf_op jit(solution)/shard_map/all_to_all | solution.py:113
  1078.2 31.9 %attend_back.2 = (bf16[2,272,2048]{2,1,0:T(8,128)(2,1)}, bf16[1024,2048]{1,0:T(8,128)(2,1)}, bf16[1024,2048]{1,0:T(8,128)(2,1)}) custom-call(bf16[2,2,272,2048]{3,2,1,0:T(8,128)(2,1)} %get-tuple-element.83.q_ref, bf16[2,1024,4096]{2,1,0:T(8,128)(2,1)} %bitcast.321, bf16[2,1024,4096]{2,1,0:T(8,128)(2,1)} %bitcast.322, ...), custom_call_target="tpu_custom_call" | custom-call | tf_op jit(solution)/shard_map/attend_back/pallas_call | solution.py:271
  1120.2 38.4 %last_grad.2 = (bf16[1024,2048]{1,0:T(8,128)(2,1)}, bf16[1024,128]{1,0:T(8,128)(2,1)}) custom-call(bf16[1024,2048]{1,0:T(8,128)(2,1)} %get-tuple-element.92.dk_ref, bf16[1024,2048]{1,0:T(8,128)(2,1)} %get-tuple-element.93.dv_ref, bf16[2,272,2048]{2,1,0:T(8,128)(2,1)} %get-tuple-element.94.dq_ref, bf16[2,1024,544]{2,1,0:T(8,128)(2,1)} %fusion.8.table_ref, ...), custom_call_target="tpu_custom_call" | custom-call | tf_op jit(solution)/shard_map/last_grad/pallas_call | solution.py:447
  1181.1 31.9 %attend_back.3 = (bf16[2,272,2048]{2,1,0:T(8,128)(2,1)}, bf16[1024,2048]{1,0:T(8,128)(2,1)}, bf16[1024,2048]{1,0:T(8,128)(2,1)}) custom-call(bf16[2,2,272,2048]{3,2,1,0:T(8,128)(2,1)} %get-tuple-element.83.q_ref, bf16[2,1024,4096]{2,1,0:T(8,128)(2,1)} %bitcast.323, bf16[2,1024,4096]{2,1,0:T(8,128)(2,1)} %bitcast.324, ...), custom_call_target="tpu_custom_call" | custom-call | tf_op jit(solution)/shard_map/attend_back/pallas_call | solution.py:271
  1213.0 38.9 %last_grad.3 = (bf16[1024,2048]{1,0:T(8,128)(2,1)}, bf16[1024,128]{1,0:T(8,128)(2,1)}) custom-call(bf16[1024,2048]{1,0:T(8,128)(2,1)} %get-tuple-element.103.dk_ref, bf16[1024,2048]{1,0:T(8,128)(2,1)} %get-tuple-element.104.dv_ref, bf16[2,272,2048]{2,1,0:T(8,128)(2,1)} %get-tuple-element.105.dq_ref, bf16[2,1024,544]{2,1,0:T(8,128)(2,1)} %fusion.8.table_ref, ...), custom_call_target="tpu_custom_call" | custom-call | tf_op jit(solution)/shard_map/last_grad/pallas_call | solution.py:447
  1320.2 19.3 %reduce-scatter.3.cloned.1.call-done.grad_ref = bf16[256,2048]{1,0:T(8,128)(2,1)} async-done(((bf16[1024,2048]{1,0:T(8,128)(2,1)}), bf16[256,2048]{1,0:T(8,128)(2,1)}) %reduce-scatter.3.cloned.1.call-update) | async-done | bytes 1048592 | tf_op jit(solution)/shard_map/reduce_scatter | solution.py:835
  (462 shorter events, 464.7 us)
Async XLA Ops:
  7.2 248.3 %all-gather.6.cloned.1.call-start = ((), (), s32[]{:S(2)}) async-start(), calls=%async_computation.16 | async-start | bytes 56623104 | tf_op jit(solution)/shard_map/all_gather | solution.py:582
  14.9 657.6 %all-gather.10.cloned.1.call-start = ((), (), s32[]{:S(2)}) async-start(), calls=%async_computation.18 | async-start | bytes 51904512 | tf_op jit(solution)/shard_map/all_gather | solution.py:583
  15.6 686.4 %all-gather.8.cloned.1.call-start = ((), (), s32[]{:S(2)}) async-start(), calls=%async_computation.17 | async-start | bytes 37748736 | tf_op jit(solution)/shard_map/all_gather | solution.py:598
  23.0 814.1 %all-gather.12.cloned.1.call-start = ((), (), s32[]{:S(2)}) async-start(), calls=%async_computation.19 | async-start | bytes 37748736 | tf_op jit(solution)/shard_map/all_gather | solution.py:597
  51.3 46.6 %collective-permute-start = (bf16[2,256,2048]{2,1,0:T(8,128)(2,1)S(1)}, bf16[2,256,2048]{2,1,0:T(8,128)(2,1)}, u32[]{:S(2)}, u32[]{:S(2)}) collective-permute-start(bf16[2,256,2048]{2,1,0:T(8,128)(2,1)S(1)} %copy-done.1), channel_id=1, source_target_pairs={{0,1},{1,2},{2,3},{4,5},{5,6},{6,7},{8,9},{9,10},{10,11},{12,13},{... | collective-permute-start | bytes 6291464 | tf_op jit(solution)/shard_map/ppermute | solution.py:81
  97.9 48.9 %collective-permute-start.4 = (bf16[2,256,2048]{2,1,0:T(8,128)(2,1)}, bf16[2,256,2048]{2,1,0:T(8,128)(2,1)}, u32[]{:S(2)}, u32[]{:S(2)}) collective-permute-start(bf16[2,256,2048]{2,1,0:T(8,128)(2,1)} %collective-permute-done), channel_id=1, source_target_pairs={{0,1},{1,2},{2,3},{4,5},{5,6},{6,7},{8,9},{9,10},{10,11},{12,13},{... | collective-permute-start | bytes 6291464 | tf_op jit(solution)/shard_map/ppermute | solution.py:81
  146.8 52.3 %collective-permute-start.5 = (bf16[2,256,2048]{2,1,0:T(8,128)(2,1)}, bf16[2,256,2048]{2,1,0:T(8,128)(2,1)S(1)}, u32[]{:S(2)}, u32[]{:S(2)}) collective-permute-start(bf16[2,256,2048]{2,1,0:T(8,128)(2,1)} %collective-permute-done.4), channel_id=1, source_target_pairs={{0,1},{1,2},{2,3},{4,5},{5,6},{6,7},{8,9},{9,10},{10,11},{12,13},{... | collective-permute-start | bytes 6291464 | tf_op jit(solution)/shard_map/ppermute | solution.py:81
  205.7 202.2 %all-to-all-start.3 = ((bf16[4,136,2048]{2,1,0:T(8,128)(2,1)}), bf16[4,136,2048]{2,1,0:T(8,128)(2,1)}, u32[]{:S(2)}, u32[]{:S(2)}) async-start(bf16[4,136,2048]{2,1,0:T(8,128)(2,1)} %bitcast.66), calls=%async_computation.3 | async-start | bytes 4456448 | tf_op jit(solution)/shard_map/all_to_all | solution.py:113
  407.9 47.2 %all-to-all-start = ((bf16[4,136,2048]{2,1,0:T(8,128)(2,1)}), bf16[4,136,2048]{2,1,0:T(8,128)(2,1)}, u32[]{:S(2)}, u32[]{:S(2)}) async-start(bf16[4,136,2048]{2,1,0:T(8,128)(2,1)} %bitcast.48), calls=%async_computation | async-start | bytes 4456448 | tf_op jit(solution)/shard_map/all_to_all | solution.py:113
  412.5 492.7 %all-gather.14.cloned.1.call-start = ((), (), s32[]{:S(2)}) async-start(), calls=%async_computation.20 | async-start | bytes 14155776 | tf_op jit(solution)/shard_map/all_gather | solution.py:598
  455.1 58.4 %all-to-all-start.1 = ((bf16[4,136,2048]{2,1,0:T(8,128)(2,1)}), bf16[4,136,2048]{2,1,0:T(8,128)(2,1)S(1)}, u32[]{:S(2)}, u32[]{:S(2)}) async-start(bf16[4,136,2048]{2,1,0:T(8,128)(2,1)} %bitcast.362), calls=%async_computation.1 | async-start | bytes 4456448 | tf_op jit(solution)/shard_map/all_to_all | solution.py:113
  494.5 69.6 %collective-permute-start.10 = (bf16[2,128,3072]{2,1,0:T(8,128)(2,1)}, bf16[2,128,3072]{2,1,0:T(8,128)(2,1)}, u32[]{:S(2)}, u32[]{:S(2)}) collective-permute-start(bf16[2,128,3072]{2,1,0:T(8,128)(2,1)} %pad_maximum_fusion.8), channel_id=1, source_target_pairs={{0,8},{4,12},{8,0},{12,4},{16,24},{20,28},{24,16},{28,20},{1,9},{5... | collective-permute-start | bytes 4718600 | tf_op jit(solution)/shard_map/ppermute | solution.py:91
  514.9 70.2 %all-to-all-start.6 = ((bf16[4,136,2048]{2,1,0:T(8,128)(2,1)}), bf16[4,136,2048]{2,1,0:T(8,128)(2,1)S(1)}, u32[]{:S(2)}, u32[]{:S(2)}) async-start(bf16[4,136,2048]{2,1,0:T(8,128)(2,1)} %bitcast.366), calls=%async_computation.6 | async-start | bytes 4456448 | tf_op jit(solution)/shard_map/all_to_all | solution.py:113
  525.0 66.4 %collective-permute-start.7 = (bf16[2,128,3072]{2,1,0:T(8,128)(2,1)}, bf16[2,128,3072]{2,1,0:T(8,128)(2,1)}, u32[]{:S(2)}, u32[]{:S(2)}) collective-permute-start(bf16[2,128,3072]{2,1,0:T(8,128)(2,1)} %pad_maximum_fusion.7), channel_id=1, source_target_pairs={{0,16},{4,20},{8,24},{12,28},{16,0},{20,4},{24,8},{28,12},{1,17},{... | collective-permute-start | bytes 4718600 | tf_op jit(solution)/shard_map/ppermute | solution.py:91
  586.5 51.0 %all-to-all-start.2 = ((bf16[4,136,2048]{2,1,0:T(8,128)(2,1)}), bf16[4,136,2048]{2,1,0:T(8,128)(2,1)}, u32[]{:S(2)}, u32[]{:S(2)}) async-start(bf16[4,136,2048]{2,1,0:T(8,128)(2,1)} %bitcast.364), calls=%async_computation.2 | async-start | bytes 4456448 | tf_op jit(solution)/shard_map/all_to_all | solution.py:113
  595.9 53.5 %collective-permute-start.8 = (bf16[2,2,128,3072]{3,2,1,0:T(8,128)(2,1)}, bf16[2,2,128,3072]{3,2,1,0:T(8,128)(2,1)}, u32[]{:S(2)}, u32[]{:S(2)}) collective-permute-start(bf16[2,2,128,3072]{3,2,1,0:T(8,128)(2,1)} %pad_maximum_fusion.5), channel_id=1, source_target_pairs={{0,4},{4,0},{8,12},{12,8},{16,20},{20,16},{24,28},{28,24},{1,5},{5... | collective-permute-start | bytes 9437192 | tf_op jit(solution)/shard_map/ppermute | solution.py:91
  637.5 136.6 %all-to-all-start.5 = ((bf16[4,136,2048]{2,1,0:T(8,128)(2,1)}), bf16[4,136,2048]{2,1,0:T(8,128)(2,1)S(1)}, u32[]{:S(2)}, u32[]{:S(2)}) async-start(bf16[4,136,2048]{2,1,0:T(8,128)(2,1)} %bitcast.363), calls=%async_computation.5 | async-start | bytes 4456448 | tf_op jit(solution)/shard_map/all_to_all | solution.py:113
  826.9 113.5 %all-to-all-start.8 = ((bf16[4,136,2048]{2,1,0:T(8,128)(2,1)}), bf16[4,136,2048]{2,1,0:T(8,128)(2,1)}, u32[]{:S(2)}, u32[]{:S(2)}) async-start(bf16[4,136,2048]{2,1,0:T(8,128)(2,1)} %bitcast.367), calls=%async_computation.8 | async-start | bytes 4456448 | tf_op jit(solution)/shard_map/all_to_all | solution.py:113
  940.5 50.8 %all-to-all-start.7 = ((bf16[4,136,2048]{2,1,0:T(8,128)(2,1)}), bf16[4,136,2048]{2,1,0:T(8,128)(2,1)S(1)}, u32[]{:S(2)}, u32[]{:S(2)}) async-start(bf16[4,136,2048]{2,1,0:T(8,128)(2,1)} %bitcast.368), calls=%async_computation.7 | async-start | bytes 4456448 | tf_op jit(solution)/shard_map/all_to_all | solution.py:113
  999.8 55.0 %all-to-all-start.9 = ((bf16[4,136,2048]{2,1,0:T(8,128)(2,1)}), bf16[4,136,2048]{2,1,0:T(8,128)(2,1)S(1)}, u32[]{:S(2)}, u32[]{:S(2)}) async-start(bf16[4,136,2048]{2,1,0:T(8,128)(2,1)} %bitcast.371), calls=%async_computation.9 | async-start | bytes 4456448 | tf_op jit(solution)/shard_map/all_to_all | solution.py:113
  1056.2 55.0 %all-to-all-start.10 = ((bf16[4,136,2048]{2,1,0:T(8,128)(2,1)}), bf16[4,136,2048]{2,1,0:T(8,128)(2,1)}, u32[]{:S(2)}, u32[]{:S(2)}) async-start(bf16[4,136,2048]{2,1,0:T(8,128)(2,1)} %bitcast.361), calls=%async_computation.10 | async-start | bytes 4456448 | tf_op jit(solution)/shard_map/all_to_all | solution.py:113
  1111.2 54.5 %all-to-all-start.11 = ((bf16[4,136,2048]{2,1,0:T(8,128)(2,1)}), bf16[4,136,2048]{2,1,0:T(8,128)(2,1)S(1)}, u32[]{:S(2)}, u32[]{:S(2)}) async-start(bf16[4,136,2048]{2,1,0:T(8,128)(2,1)} %bitcast.369), calls=%async_computation.11 | async-start | bytes 4456448 | tf_op jit(solution)/shard_map/all_to_all | solution.py:113
  1119.1 197.2 %reduce-scatter.5.cloned.1.call-start = ((), (), s32[]{:S(2)}) async-start(), calls=%async_computation.22 | async-start | bytes 5242880 | tf_op jit(solution)/shard_map/reduce_scatter | solution.py:835
  1165.7 173.8 %reduce-scatter.3.cloned.1.call-start = ((), (), s32[]{:S(2)}) async-start(), calls=%async_computation.21 | async-start | bytes 5242880 | tf_op jit(solution)/shard_map/reduce_scatter | solution.py:835
  (110 other events, 2052.1 us)
Sparse Core Ops, SparseCore 0:
  15.0 233.8 all-gather.5
  250.8 214.0 all-gather.9
  466.8 201.8 all-gather.7
  670.5 160.7 all-gather.11
  833.1 72.1 all-gather.13
  1165.8 79.3 reduce-scatter.4
  1252.1 87.3 reduce-scatter.2

commit v4 on v3

--- a/solution.py
+++ b/solution.py
@@ -295,20 +295,23 @@
 
 def expert_body(has_start, is_last, x_ref, c_ref, wg_ref, wu_ref, wd_ref, *refs):
     refs = list(refs)
-    start = [refs.pop(0), refs.pop(0)] if has_start else None
+    start = [refs.pop(0), refs.pop(0)] if has_start else []
     if is_last:
-        cot_ref, gate_ref, pick_ref, router_ref, low_ref, back_ref, out_ref, gs_ref = refs
+        cot_ref, gate_ref, pick_ref, router_ref, low_ref, back_ref, out_ref, gs_ref = refs[:8]
+        late = start + [cot_ref]
     else:
-        out_ref, gs_ref = refs
+        out_ref, gs_ref = refs[:2]
+        late = start
+    count = len(late)
+    held, sem = (refs[-count - 1 : -1], refs[-1]) if count else ([], None)
+    copies = [pltpu.make_async_copy(late[i], held[i], sem.at[i]) for i in range(count)]
 
     @pl.when(pl.program_id(0) == 0)
     def _():
-        if has_start:
-            out_ref[...] = start[0][...]
-            gs_ref[...] = start[1][...]
-        else:
-            out_ref[...] = jnp.zeros_like(out_ref)
-            gs_ref[...] = jnp.zeros_like(gs_ref)
+        for copy in copies:
+            copy.start()
+        out_ref[...] = jnp.zeros_like(out_ref)
+        gs_ref[...] = jnp.zeros_like(gs_ref)
 
     x, c = x_ref[...], c_ref[...]
     wg, wu, wd = wg_ref[...], wu_ref[...], wd_ref[...]
@@ -321,18 +324,24 @@
     grad_up = (grad * silu).astype(BF16)
     gs_ref[...] += mm(grad_gate, wg, NT) + mm(grad_up, wu, NT)
 
-    if is_last:
-
-        @pl.when(pl.program_id(0) == pl.num_programs(0) - 1)
-        def _():
-            made = out_ref[...]
+    @pl.when(pl.program_id(0) == pl.num_programs(0) - 1)
+    def _():
+        for copy in copies:
+            copy.wait()
+        made, back = out_ref[...], gs_ref[...]
+        if has_start:
+            made, back = made + held[0][...], back + held[1][...]
+        if has_start and not is_last:
+            out_ref[...] = made
+            gs_ref[...] = back
+        if is_last:
             share = gate_ref[...]
-            dots = jnp.sum(cot_ref[...].astype(F32) * made, axis=-1, keepdims=True)
+            dots = jnp.sum(held[-1][...].astype(F32) * made, axis=-1, keepdims=True)
             weigh = pick_ref[...] * (dots * share * (1.0 - share))
             high = weigh.astype(BF16)
             low = (weigh - high.astype(F32)).astype(BF16)
             router = router_ref[...]
-            back_ref[...] = (gs_ref[...] + mm(high, router, NT) + mm(low, router, NT)).astype(BF16)
+            back_ref[...] = (back + mm(high, router, NT) + mm(low, router, NT)).astype(BF16)
             low_ref[...] = (share * made).astype(BF16)
 
 
@@ -347,6 +356,11 @@
 
     more = ([] if start is None else list(start)) + ([] if last is None else list(last))
     kind = F32 if last is None else BF16
+    late = ([] if start is None else [F32, F32]) + ([] if last is None else [BF16])
+    away = len(late)
+    scratch = [] if last is None else [pltpu.VMEM((rows, width), F32)] * 2
+    if away:
+        scratch += [pltpu.VMEM((rows, width), t) for t in late] + [pltpu.SemaphoreType.DMA((away,))]
     return pl.pallas_call(
         functools.partial(expert_body, start is not None, last is not None),
         grid=(units // tile,),
@@ -357,10 +371,10 @@
             pl.BlockSpec((width, tile), lambda i: (0, units // tile + i)),
             pl.BlockSpec((None, tile, width), lambda i: (l, first + i, 0)),
         ]
-        + [whole(m) for m in more],
+        + [pl.BlockSpec(memory_space=pl.ANY) if i < away else whole(m) for i, m in enumerate(more)],
         out_specs=[pl.BlockSpec((rows, width), lambda i: (0, 0))] * 2,
         out_shape=[jax.ShapeDtypeStruct((rows, width), kind)] * 2,
-        scratch_shapes=[] if last is None else [pltpu.VMEM((rows, width), F32)] * 2,
+        scratch_shapes=scratch,
         compiler_params=params("arbitrary"),
         name="expert",
     )(rows_in, grad_in, inner, inner, down, *more)
@@ -745,15 +759,12 @@
         normed_low,
         preferred_element_type=F32,
     ).astype(BF16)
+    beside, picked = lax.optimization_barrier((beside, picked))
+    beside = exchange_all(0)
     queries = project(picked.reshape(locals_, seqs * slots, width), near_full, query_column)
     query_rot, attended, probs = attend(
         queries.reshape(locals_, seqs, slots, width), key_value, cos_q, sin_q, query_blocks, key_blocks
     )
-    beside, attended = lax.optimization_barrier((beside, attended))
-    for step in range(len(orders[0])):
-        beside = exchange_all(step)
-    for l, halves in enumerate(beside):
-        inner_full[l][0] = (0, in_order(halves, orders, groups))
     gate_rows = gate_a[..., None]
     projected, gated = project(
         attended.reshape(locals_, seqs * slots, width),
@@ -761,6 +772,11 @@
         output_column,
         gate_rows.reshape(locals_, seqs * slots, 1),
     )
+    beside, projected = lax.optimization_barrier((beside, projected))
+    for step in range(1, len(orders[0])):
+        beside = exchange_all(step)
+    for l, halves in enumerate(beside):
+        inner_full[l][0] = (0, in_order(halves, orders, groups))
     projected = projected.reshape(locals_, seqs, slots, width)
     gated = gated.reshape(locals_, seqs, slots, width)
     order = np.arange(locals_ * slots).reshape(locals_, ranks, capacity).transpose(1, 0, 2).reshape(-1)

time: 1360 us -> 1350 us (level)
    ppermute x6, waiting for transfers between devices: 59.3 us -> 0.02 us  [exchange(): other = lax.ppermute(total, axis, [(i, i ^ bit) for i in range(size)])]
    all_to_all x12, waiting for transfers between devices: 169 us -> 219 us  [send(): lax.all_to_all(buffer, 'expert', split_axis=0, concat_axis=0, tiled=True)]
    unnamed x224 -> x210, local copies, waits for them, and re-layouts: 27.3 us -> 26 us
where the time goes in v4:
time: 1350 us; the launch traced here: 1340 us
  Pallas kernels  533 us (39%)
  waiting for transfers between devices  350 us (26%)
  starting transfers between devices  114 us (8%)
  other arithmetic  102 us (8%)
  matrix products  78.1 us (6%)
  local copies, waits for them, and re-layouts  74.6 us (6%)
  blocking collectives  71.2 us (5%)
  between operations  18.1 us (1%)
    all_to_all x12, waiting for transfers between devices, send(): lax.all_to_all(buffer, 'expert', split_axis=0, concat_axis=0, tiled=True)  219 us
    pallas_call x4, Pallas kernels, expert_pass(): pl.pallas_call(functools.partial(expert_body, start is not None, last is...  197 us
    ppermute x3, waiting for transfers between devices, gather_line(): from_right.append(lax.ppermute(from_right[-1], axis, leftward))  96.5 us
    all_to_all x12, starting transfers between devices, send(): lax.all_to_all(buffer, 'expert', split_axis=0, concat_axis=0, tiled=True)  87.1 us
    pallas_call x2, Pallas kernels, last_grad(): pl.pallas_call(functools.partial(last_body, locals_, seq_len), grid=(widt...  77.3 us
    dot_general x23, matrix products, mm(): return lax.dot_general(left, right, dims, preferred_element_type=F32)  65.9 us
    pallas_call x2, Pallas kernels, attend_back(): pl.pallas_call(attend_back_body, grid=(HEADS,), in_specs=[pl.BlockSpec((l...  63.8 us
    pallas_call x1, Pallas kernels, attend(): pl.pallas_call(attend_body, grid=(seqs, HEADS), in_specs=[q_spec, pl.Bloc...  55.9 us
  transfers between devices with their start and end apart: 32, of which 16 were waited for; matrix products, arithmetic and copies ran while one was open for 17% of the time, Pallas kernels for 39%

profile of v4, /device:TPU:9, one launch (start us, length us, event | category | flops | bytes accessed | tf_op | source)
XLA Modules:
  0.0 1340.0 jit_solution(1437404769917348827)
XLA Ops:
  58.5 36.2 %collective-permute-done.1 = bf16[2,256,2048]{2,1,0:T(8,128)(2,1)} collective-permute-done((bf16[2,256,2048]{2,1,0:T(8,128)(2,1)S(1)}, bf16[2,256,2048]{2,1,0:T(8,128)(2,1)}, u32[]{:S(2)}, u32[]{:S(2)}) %collective-permute-start.1) | collective-permute-done | bytes 2097184 | tf_op jit(solution)/shard_map/ppermute | solution.py:82
  104.7 34.4 %collective-permute-done.2 = bf16[2,256,2048]{2,1,0:T(8,128)(2,1)} collective-permute-done((bf16[2,256,2048]{2,1,0:T(8,128)(2,1)}, bf16[2,256,2048]{2,1,0:T(8,128)(2,1)}, u32[]{:S(2)}, u32[]{:S(2)}) %collective-permute-start.2) | collective-permute-done | bytes 2097184 | tf_op jit(solution)/shard_map/ppermute | solution.py:82
  157.4 25.9 %collective-permute-done.3 = bf16[2,256,2048]{2,1,0:T(8,128)(2,1)} collective-permute-done((bf16[2,256,2048]{2,1,0:T(8,128)(2,1)}, bf16[2,256,2048]{2,1,0:T(8,128)(2,1)}, u32[]{:S(2)}, u32[]{:S(2)}) %collective-permute-start.3) | collective-permute-done | bytes 2097184 | tf_op jit(solution)/shard_map/ppermute | solution.py:82
  255.5 18.1 %project.2 = bf16[2,544,2048]{2,1,0:T(8,128)(2,1)} custom-call(bf16[2,544,2048]{2,1,0:T(8,128)(2,1)} %bitcast.348, bf16[2048,12288]{1,0:T(8,128)(2,1)} %all-gather.6.cloned.1.call-done.w_ref.refs_0_.refs_1_), custom_call_target="tpu_custom_call" | custom-call | tf_op jit(solution)/shard_map/project/pallas_call | solution.py:181
  273.7 53.1 %key_value.1 = bf16[2048,4096]{1,0:T(8,128)(2,1)} custom-call(bf16[2048,2048]{1,0:T(8,128)(2,1)} %bitcast.327, bf16[2048,128]{1,0:T(8,128)(2,1)} %bitcast.356, bf16[2048,12288]{1,0:T(8,128)(2,1)} %all-gather.6.cloned.1.call-done.w_ref.refs_0_.refs_1_, bf16[4096,128]{1,0:T(8,128)(2,1)} %up_ref.5, f32[1024,128]{1,0:T(8,128)} %get-tuple-element.198.cos_ref.ck_ref, ...), custom_call_target="tpu_custom_call" | custom-call | tf_op jit(solution)/shard_map/key_value/pallas_call | solution.py:139
  326.8 55.9 %attend.1 = (bf16[2,2,272,2048]{3,2,1,0:T(8,128)(2,1)}, bf16[2,2,272,2048]{3,2,1,0:T(8,128)(2,1)}, bf16[2,2,16,272,1024]{4,3,2,1,0:T(8,128)(2,1)}) custom-call(bf16[2,2,272,2048]{3,2,1,0:T(8,128)(2,1)} %bitcast.347, bf16[2,1024,4096]{2,1,0:T(8,128)(2,1)} %bitcast.319, bf16[2,1024,4096]{2,1,0:T(8,128)(2,1)} %bitcast.320, ...), custom_call_target="tpu_custom_call" | custom-call | tf_op jit(solution)/shard_map/attend/pallas_call | solution.py:218
  382.7 17.7 %project.3 = (bf16[2,544,2048]{2,1,0:T(8,128)(2,1)}, bf16[2,544,2048]{2,1,0:T(8,128)(2,1)}) custom-call(bf16[2,544,2048]{2,1,0:T(8,128)(2,1)} %bitcast.357, bf16[2048,12288]{1,0:T(8,128)(2,1)} %all-gather.6.cloned.1.call-done.w_ref.refs_0_.refs_1_, f32[2,544,1]{2,1,0:T(8,128)} %fusion.88.refs_0_), custom_call_target="tpu_custom_call" | custom-call | tf_op jit(solution)/shard_map/project/pallas_call | solution.py:181
  424.4 30.6 %all-to-all-done = bf16[4,136,2048]{2,1,0:T(8,128)(2,1)} async-done(((bf16[4,136,2048]{2,1,0:T(8,128)(2,1)}), bf16[4,136,2048]{2,1,0:T(8,128)(2,1)}, u32[]{:S(2)}, u32[]{:S(2)}) %all-to-all-start) | async-done | bytes 2228256 | tf_op jit(solution)/shard_map/all_to_all | solution.py:113
  478.4 34.9 %all-to-all-done.1 = bf16[4,136,2048]{2,1,0:T(8,128)(2,1)S(1)} async-done(((bf16[4,136,2048]{2,1,0:T(8,128)(2,1)}), bf16[4,136,2048]{2,1,0:T(8,128)(2,1)S(1)}, u32[]{:S(2)}, u32[]{:S(2)}) %all-to-all-start.1) | async-done | bytes 2228256 | tf_op jit(solution)/shard_map/all_to_all | solution.py:113
  539.5 29.2 %all-to-all-done.6 = bf16[4,136,2048]{2,1,0:T(8,128)(2,1)S(1)} async-done(((bf16[4,136,2048]{2,1,0:T(8,128)(2,1)}), bf16[4,136,2048]{2,1,0:T(8,128)(2,1)S(1)}, u32[]{:S(2)}, u32[]{:S(2)}) %all-to-all-start.6) | async-done | bytes 2228256 | tf_op jit(solution)/shard_map/all_to_all | solution.py:113
  595.8 29.6 %all-to-all-done.2 = bf16[4,136,2048]{2,1,0:T(8,128)(2,1)} async-done(((bf16[4,136,2048]{2,1,0:T(8,128)(2,1)}), bf16[4,136,2048]{2,1,0:T(8,128)(2,1)}, u32[]{:S(2)}, u32[]{:S(2)}) %all-to-all-start.2) | async-done | bytes 2228256 | tf_op jit(solution)/shard_map/all_to_all | solution.py:113
  659.7 29.5 %expert.4 = (f32[544,2048]{1,0:T(8,128)}, f32[544,2048]{1,0:T(8,128)}) custom-call(bf16[544,2048]{1,0:T(8,128)(2,1)} %bitcast.62.x_ref, bf16[544,2048]{1,0:T(8,128)(2,1)} %multiply_convert_fusion.1.c_ref, bf16[2048,3072]{1,0:T(8,128)(2,1)} %bitcast.325, bf16[2048,3072]{1,0:T(8,128)(2,1)} %bitcast.326, bf16[2,5632,2048]{2,1,0:T(8,128)(2,1)} %all-gather.10.cloned.1.call-done.wd_ref), custom_call_target="tpu_custom_call" | custom-call | tf_op jit(solution)/shard_map/expert/pallas_call | solution.py:364
  689.2 69.0 %expert.5 = (bf16[544,2048]{1,0:T(8,128)(2,1)}, bf16[544,2048]{1,0:T(8,128)(2,1)}) custom-call(bf16[544,2048]{1,0:T(8,128)(2,1)} %bitcast.62.x_ref, bf16[544,2048]{1,0:T(8,128)(2,1)} %multiply_convert_fusion.1.c_ref, bf16[2048,8192]{1,0:T(8,128)(2,1)} %all-gather.8.cloned.1.call-done.wg_ref.wu_ref, ...), custom_call_target="tpu_custom_call" | custom-call | tf_op jit(solution)/shard_map/expert/pallas_call | solution.py:364
  758.3 52.6 %all_to_all.149 = bf16[4,136,2048]{2,1,0:T(8,128)(2,1)} all-to-all(bf16[4,136,2048]{2,1,0:T(8,128)(2,1)} %bitcast.370), channel_id=1, replica_groups=mesh['dp'=8,'expert'=4] {'expert'}, dimensions={0} | all-to-all | bytes 4456448 | tf_op jit(solution)/shard_map/all_to_all | solution.py:113
  823.9 66.4 %expert.6 = (f32[544,2048]{1,0:T(8,128)}, f32[544,2048]{1,0:T(8,128)}) custom-call(bf16[544,2048]{1,0:T(8,128)(2,1)} %bitcast.342, bf16[544,2048]{1,0:T(8,128)(2,1)} %multiply_convert_fusion.c_ref, bf16[2048,8192]{1,0:T(8,128)(2,1)} %all-gather.12.cloned.1.call-done.wg_ref.wu_ref, bf16[2048,8192]{1,0:T(8,128)(2,1)} %all-gather.12.cloned.1.call-done.wg_ref.wu_ref, ...), custom_call_target="tpu_custom_call" | custom-call | tf_op jit(solution)/shard_map/expert/pallas_call | solution.py:364
  897.8 32.2 %expert.7 = (bf16[544,2048]{1,0:T(8,128)(2,1)}, bf16[544,2048]{1,0:T(8,128)(2,1)}) custom-call(bf16[544,2048]{1,0:T(8,128)(2,1)} %bitcast.343, bf16[544,2048]{1,0:T(8,128)(2,1)} %multiply_convert_fusion.c_ref, bf16[2048,3072]{1,0:T(8,128)(2,1)} %all-gather.14.cloned.1.call-done.wg_ref.wu_ref, bf16[2048,3072]{1,0:T(8,128)(2,1)} %all-gather.14.cloned.1.call-done.wg_ref.wu_ref, ...), custom_call_target="tpu_custom_call" | custom-call | tf_op jit(solution)/shard_map/expert/pallas_call | solution.py:364
  946.9 35.9 %all-to-all-done.7 = bf16[4,136,2048]{2,1,0:T(8,128)(2,1)S(1)} async-done(((bf16[4,136,2048]{2,1,0:T(8,128)(2,1)}), bf16[4,136,2048]{2,1,0:T(8,128)(2,1)S(1)}, u32[]{:S(2)}, u32[]{:S(2)}) %all-to-all-start.7) | async-done | bytes 2228256 | tf_op jit(solution)/shard_map/all_to_all | solution.py:113
  1004.9 39.6 %all-to-all-done.9 = bf16[4,136,2048]{2,1,0:T(8,128)(2,1)S(1)} async-done(((bf16[4,136,2048]{2,1,0:T(8,128)(2,1)}), bf16[4,136,2048]{2,1,0:T(8,128)(2,1)S(1)}, u32[]{:S(2)}, u32[]{:S(2)}) %all-to-all-start.9) | async-done | bytes 2228256 | tf_op jit(solution)/shard_map/all_to_all | solution.py:113
  1067.8 31.9 %attend_back.2 = (bf16[2,272,2048]{2,1,0:T(8,128)(2,1)}, bf16[1024,2048]{1,0:T(8,128)(2,1)}, bf16[1024,2048]{1,0:T(8,128)(2,1)}) custom-call(bf16[2,2,272,2048]{3,2,1,0:T(8,128)(2,1)} %get-tuple-element.89.q_ref, bf16[2,1024,4096]{2,1,0:T(8,128)(2,1)} %bitcast.321, bf16[2,1024,4096]{2,1,0:T(8,128)(2,1)} %bitcast.322, ...), custom_call_target="tpu_custom_call" | custom-call | tf_op jit(solution)/shard_map/attend_back/pallas_call | solution.py:271
  1109.8 38.4 %last_grad.2 = (bf16[1024,2048]{1,0:T(8,128)(2,1)}, bf16[1024,128]{1,0:T(8,128)(2,1)}) custom-call(bf16[1024,2048]{1,0:T(8,128)(2,1)} %get-tuple-element.98.dk_ref, bf16[1024,2048]{1,0:T(8,128)(2,1)} %get-tuple-element.99.dv_ref, bf16[2,272,2048]{2,1,0:T(8,128)(2,1)} %get-tuple-element.100.dq_ref, bf16[2,1024,544]{2,1,0:T(8,128)(2,1)} %fusion.8.table_ref, ...), custom_call_target="tpu_custom_call" | custom-call | tf_op jit(solution)/shard_map/last_grad/pallas_call | solution.py:461
  1156.6 14.0 %out_back.3 = (bf16[2,272,2048]{2,1,0:T(8,128)(2,1)}, f32[2,272,1]{2,1,0:T(8,128)}) custom-call(bf16[544,2048]{1,0:T(8,128)(2,1)} %bitcast.351, bf16[544,544]{1,0:T(8,128)(2,1)} %constant.168.clone.order_ref, f32[2,2,272,1]{3,2,1,0:T(8,128)} %get-tuple-element.169.gate_ref, bf16[2,2,272,2048]{3,2,1,0:T(8,128)(2,1)} %bitcast.350, ...), custom_call_target="tpu_custom_call" | custom-call | tf_op jit(solution)/shard_map/out_back/pallas_call | solution.py:402
  1170.7 31.9 %attend_back.3 = (bf16[2,272,2048]{2,1,0:T(8,128)(2,1)}, bf16[1024,2048]{1,0:T(8,128)(2,1)}, bf16[1024,2048]{1,0:T(8,128)(2,1)}) custom-call(bf16[2,2,272,2048]{3,2,1,0:T(8,128)(2,1)} %get-tuple-element.89.q_ref, bf16[2,1024,4096]{2,1,0:T(8,128)(2,1)} %bitcast.323, bf16[2,1024,4096]{2,1,0:T(8,128)(2,1)} %bitcast.324, ...), custom_call_target="tpu_custom_call" | custom-call | tf_op jit(solution)/shard_map/attend_back/pallas_call | solution.py:271
  1202.6 38.9 %last_grad.3 = (bf16[1024,2048]{1,0:T(8,128)(2,1)}, bf16[1024,128]{1,0:T(8,128)(2,1)}) custom-call(bf16[1024,2048]{1,0:T(8,128)(2,1)} %get-tuple-element.109.dk_ref, bf16[1024,2048]{1,0:T(8,128)(2,1)} %get-tuple-element.110.dv_ref, bf16[2,272,2048]{2,1,0:T(8,128)(2,1)} %get-tuple-element.111.dq_ref, bf16[2,1024,544]{2,1,0:T(8,128)(2,1)} %fusion.8.table_ref, ...), custom_call_target="tpu_custom_call" | custom-call | tf_op jit(solution)/shard_map/last_grad/pallas_call | solution.py:461
  1309.8 19.2 %reduce-scatter.3.cloned.1.call-done.grad_ref = bf16[256,2048]{1,0:T(8,128)(2,1)} async-done(((bf16[1024,2048]{1,0:T(8,128)(2,1)}), bf16[256,2048]{1,0:T(8,128)(2,1)}) %reduce-scatter.3.cloned.1.call-update) | async-done | bytes 1048592 | tf_op jit(solution)/shard_map/reduce_scatter | solution.py:851
  (447 shorter events, 456.6 us)
Async XLA Ops:
  7.2 248.4 %all-gather.6.cloned.1.call-start = ((), (), s32[]{:S(2)}) async-start(), calls=%async_computation.16 | async-start | bytes 56623104 | tf_op jit(solution)/shard_map/all_gather | solution.py:596
  15.0 644.7 %all-gather.10.cloned.1.call-start = ((), (), s32[]{:S(2)}) async-start(), calls=%async_computation.18 | async-start | bytes 51904512 | tf_op jit(solution)/shard_map/all_gather | solution.py:597
  15.7 673.5 %all-gather.8.cloned.1.call-start = ((), (), s32[]{:S(2)}) async-start(), calls=%async_computation.17 | async-start | bytes 37748736 | tf_op jit(solution)/shard_map/all_gather | solution.py:612
  23.1 800.8 %all-gather.12.cloned.1.call-start = ((), (), s32[]{:S(2)}) async-start(), calls=%async_computation.19 | async-start | bytes 37748736 | tf_op jit(solution)/shard_map/all_gather | solution.py:611
  146.9 52.3 %collective-permute-start.5 = (bf16[2,256,2048]{2,1,0:T(8,128)(2,1)}, bf16[2,256,2048]{2,1,0:T(8,128)(2,1)S(1)}, u32[]{:S(2)}, u32[]{:S(2)}) collective-permute-start(bf16[2,256,2048]{2,1,0:T(8,128)(2,1)} %collective-permute-done.4), channel_id=1, source_target_pairs={{0,1},{1,2},{2,3},{4,5},{5,6},{6,7},{8,9},{9,10},{10,11},{12,13},{... | collective-permute-start | bytes 6291464 | tf_op jit(solution)/shard_map/ppermute | solution.py:81
  205.8 202.1 %all-to-all-start.3 = ((bf16[4,136,2048]{2,1,0:T(8,128)(2,1)}), bf16[4,136,2048]{2,1,0:T(8,128)(2,1)}, u32[]{:S(2)}, u32[]{:S(2)}) async-start(bf16[4,136,2048]{2,1,0:T(8,128)(2,1)} %bitcast.66), calls=%async_computation.3 | async-start | bytes 4456448 | tf_op jit(solution)/shard_map/all_to_all | solution.py:113
  412.5 485.3 %all-gather.14.cloned.1.call-start = ((), (), s32[]{:S(2)}) async-start(), calls=%async_computation.20 | async-start | bytes 14155776 | tf_op jit(solution)/shard_map/all_gather | solution.py:612
  415.1 51.6 %collective-permute-start.7 = (bf16[128,3072]{1,0:T(8,128)(2,1)}, bf16[128,3072]{1,0:T(8,128)(2,1)}, u32[]{:S(2)}, u32[]{:S(2)}) collective-permute-start(bf16[128,3072]{1,0:T(8,128)(2,1)} %get-tuple-element.69), channel_id=1, source_target_pairs={{0,16},{4,20},{8,24},{12,28},{16,0},{20,4},{24,8},{28,12},{1,17},{... | collective-permute-start | bytes 2359304 | tf_op jit(solution)/shard_map/ppermute | solution.py:91
  419.3 48.9 %collective-permute-start.6 = (bf16[128,3072]{1,0:T(8,128)(2,1)S(1)}, bf16[128,3072]{1,0:T(8,128)(2,1)}, u32[]{:S(2)}, u32[]{:S(2)}) collective-permute-start(bf16[128,3072]{1,0:T(8,128)(2,1)S(1)} %copy-done.24), channel_id=1, source_target_pairs={{0,8},{4,12},{8,0},{12,4},{16,24},{20,28},{24,16},{28,20},{1,9},{5... | collective-permute-start | bytes 2359304 | tf_op jit(solution)/shard_map/ppermute | solution.py:91
  455.1 58.2 %all-to-all-start.1 = ((bf16[4,136,2048]{2,1,0:T(8,128)(2,1)}), bf16[4,136,2048]{2,1,0:T(8,128)(2,1)S(1)}, u32[]{:S(2)}, u32[]{:S(2)}) async-start(bf16[4,136,2048]{2,1,0:T(8,128)(2,1)} %bitcast.364), calls=%async_computation.1 | async-start | bytes 4456448 | tf_op jit(solution)/shard_map/all_to_all | solution.py:113
  471.4 50.8 %collective-permute-start.10 = (bf16[2,128,3072]{2,1,0:T(8,128)(2,1)}, bf16[2,128,3072]{2,1,0:T(8,128)(2,1)}, u32[]{:S(2)}, u32[]{:S(2)}) collective-permute-start(bf16[2,128,3072]{2,1,0:T(8,128)(2,1)} %get-tuple-element.72), channel_id=1, source_target_pairs={{0,8},{4,12},{8,0},{12,4},{16,24},{20,28},{24,16},{28,20},{1,9},{5... | collective-permute-start | bytes 4718600 | tf_op jit(solution)/shard_map/ppermute | solution.py:91
  477.8 101.1 %collective-permute-start.8 = (bf16[2,128,3072]{2,1,0:T(8,128)(2,1)}, bf16[2,128,3072]{2,1,0:T(8,128)(2,1)}, u32[]{:S(2)}, u32[]{:S(2)}) collective-permute-start(bf16[2,128,3072]{2,1,0:T(8,128)(2,1)} %get-tuple-element.71), channel_id=1, source_target_pairs={{0,16},{4,20},{8,24},{12,28},{16,0},{20,4},{24,8},{28,12},{1,17},{... | collective-permute-start | bytes 4718600 | tf_op jit(solution)/shard_map/ppermute | solution.py:91
  514.7 54.1 %all-to-all-start.6 = ((bf16[4,136,2048]{2,1,0:T(8,128)(2,1)}), bf16[4,136,2048]{2,1,0:T(8,128)(2,1)S(1)}, u32[]{:S(2)}, u32[]{:S(2)}) async-start(bf16[4,136,2048]{2,1,0:T(8,128)(2,1)} %bitcast.368), calls=%async_computation.6 | async-start | bytes 4456448 | tf_op jit(solution)/shard_map/all_to_all | solution.py:113
  527.4 64.0 %collective-permute-start.11 = (bf16[2,2,128,3072]{3,2,1,0:T(8,128)(2,1)}, bf16[2,2,128,3072]{3,2,1,0:T(8,128)(2,1)}, u32[]{:S(2)}, u32[]{:S(2)}) collective-permute-start(bf16[2,2,128,3072]{3,2,1,0:T(8,128)(2,1)} %pad_maximum_fusion.6), channel_id=1, source_target_pairs={{0,4},{4,0},{8,12},{12,8},{16,20},{20,16},{24,28},{28,24},{1,5},{5... | collective-permute-start | bytes 9437192 | tf_op jit(solution)/shard_map/ppermute | solution.py:91
  570.2 55.2 %all-to-all-start.2 = ((bf16[4,136,2048]{2,1,0:T(8,128)(2,1)}), bf16[4,136,2048]{2,1,0:T(8,128)(2,1)}, u32[]{:S(2)}, u32[]{:S(2)}) async-start(bf16[4,136,2048]{2,1,0:T(8,128)(2,1)} %bitcast.365), calls=%async_computation.2 | async-start | bytes 4456448 | tf_op jit(solution)/shard_map/all_to_all | solution.py:113
  583.9 53.1 %collective-permute-start.9 = (bf16[2,2,128,3072]{3,2,1,0:T(8,128)(2,1)}, bf16[2,2,128,3072]{3,2,1,0:T(8,128)(2,1)}, u32[]{:S(2)}, u32[]{:S(2)}) collective-permute-start(bf16[2,2,128,3072]{3,2,1,0:T(8,128)(2,1)} %pad_maximum_fusion.5), channel_id=1, source_target_pairs={{0,4},{4,0},{8,12},{12,8},{16,20},{20,16},{24,28},{28,24},{1,5},{5... | collective-permute-start | bytes 9437192 | tf_op jit(solution)/shard_map/ppermute | solution.py:91
  625.5 132.8 %all-to-all-start.5 = ((bf16[4,136,2048]{2,1,0:T(8,128)(2,1)}), bf16[4,136,2048]{2,1,0:T(8,128)(2,1)S(1)}, u32[]{:S(2)}, u32[]{:S(2)}) async-start(bf16[4,136,2048]{2,1,0:T(8,128)(2,1)} %bitcast.363), calls=%async_computation.5 | async-start | bytes 4456448 | tf_op jit(solution)/shard_map/all_to_all | solution.py:113
  810.9 119.1 %all-to-all-start.8 = ((bf16[4,136,2048]{2,1,0:T(8,128)(2,1)}), bf16[4,136,2048]{2,1,0:T(8,128)(2,1)}, u32[]{:S(2)}, u32[]{:S(2)}) async-start(bf16[4,136,2048]{2,1,0:T(8,128)(2,1)} %bitcast.366), calls=%async_computation.8 | async-start | bytes 4456448 | tf_op jit(solution)/shard_map/all_to_all | solution.py:113
  930.1 52.8 %all-to-all-start.7 = ((bf16[4,136,2048]{2,1,0:T(8,128)(2,1)}), bf16[4,136,2048]{2,1,0:T(8,128)(2,1)S(1)}, u32[]{:S(2)}, u32[]{:S(2)}) async-start(bf16[4,136,2048]{2,1,0:T(8,128)(2,1)} %bitcast.367), calls=%async_computation.7 | async-start | bytes 4456448 | tf_op jit(solution)/shard_map/all_to_all | solution.py:113
  991.3 53.3 %all-to-all-start.9 = ((bf16[4,136,2048]{2,1,0:T(8,128)(2,1)}), bf16[4,136,2048]{2,1,0:T(8,128)(2,1)S(1)}, u32[]{:S(2)}, u32[]{:S(2)}) async-start(bf16[4,136,2048]{2,1,0:T(8,128)(2,1)} %bitcast.371), calls=%async_computation.9 | async-start | bytes 4456448 | tf_op jit(solution)/shard_map/all_to_all | solution.py:113
  1045.9 54.9 %all-to-all-start.10 = ((bf16[4,136,2048]{2,1,0:T(8,128)(2,1)}), bf16[4,136,2048]{2,1,0:T(8,128)(2,1)}, u32[]{:S(2)}, u32[]{:S(2)}) async-start(bf16[4,136,2048]{2,1,0:T(8,128)(2,1)} %bitcast.361), calls=%async_computation.10 | async-start | bytes 4456448 | tf_op jit(solution)/shard_map/all_to_all | solution.py:113
  1100.8 54.5 %all-to-all-start.11 = ((bf16[4,136,2048]{2,1,0:T(8,128)(2,1)}), bf16[4,136,2048]{2,1,0:T(8,128)(2,1)S(1)}, u32[]{:S(2)}, u32[]{:S(2)}) async-start(bf16[4,136,2048]{2,1,0:T(8,128)(2,1)} %bitcast.369), calls=%async_computation.11 | async-start | bytes 4456448 | tf_op jit(solution)/shard_map/all_to_all | solution.py:113
  1108.7 197.3 %reduce-scatter.5.cloned.1.call-start = ((), (), s32[]{:S(2)}) async-start(), calls=%async_computation.22 | async-start | bytes 5242880 | tf_op jit(solution)/shard_map/reduce_scatter | solution.py:851
  1155.3 173.8 %reduce-scatter.3.cloned.1.call-start = ((), (), s32[]{:S(2)}) async-start(), calls=%async_computation.21 | async-start | bytes 5242880 | tf_op jit(solution)/shard_map/reduce_scatter | solution.py:851
  (103 other events, 1934.4 us)
Sparse Core Ops, SparseCore 0:
  15.1 233.9 all-gather.5
  251.0 231.3 all-gather.9
  484.2 177.0 all-gather.7
  663.0 160.7 all-gather.11
  825.6 72.1 all-gather.13
  1155.4 79.3 reduce-scatter.4
  1241.7 87.3 reduce-scatter.2

commit v5 on v4

--- a/solution.py
+++ b/solution.py
@@ -830,8 +830,8 @@
         leaving.append(rows)
 
     arrived = [send(leaving[0])]
-    arrived[0], held, leaving[1:] = lax.optimization_barrier((arrived[0], held, leaving[1:]))
-    held = send(held)
+    arrived[0], leaving[1:] = lax.optimization_barrier((arrived[0], leaving[1:]))
+    arrived += [send(rows) for rows in leaving[1:]]
     down_pieces, up_pieces = [], []
     input_grad = None
     for s in range(seqs):
@@ -839,15 +839,15 @@
             s, arrived[s], to_slots, gate_rows, projected, near_full, output_column
         )
         dq, dk, dv = attend_back(s, query_rot, key_value, grad_attended, probs, cos_q, sin_q, cos_k, sin_k)
-        if s + 1 < seqs:
-            leaving[s + 1], held, dk = lax.optimization_barrier((leaving[s + 1], held, dk))
-            arrived.append(send(leaving[s + 1]))
+        if s == 0:
+            arrived[1:], held, dk = lax.optimization_barrier((arrived[1:], held, dk))
+            held = send(held)
         part, grad_low = last_grad(
             s, dk, dv, dq, collect_a, dots, weigh_a, mask, adapt_up, router_near, adapt_down, near_full,
             query_column,
         )
         if s + 1 < seqs:
-            arrived[s + 1], part = lax.optimization_barrier((arrived[s + 1], part))
+            arrived[s + 1], held, part = lax.optimization_barrier((arrived[s + 1], held, part))
         grad_normed = lax.psum_scatter(part, "expert", scatter_dimension=0, tiled=True)
         input_grad = input_back(s, grad_normed, grad_middle[s], hidden_in, attn_gain[None], input_grad)
         first = adapter_index[s] * RANK

time: 1350 us -> 1350 us (level)
  no operation moved by 1% of the time
where the time goes in v5:
time: 1350 us; the launch traced here: 1340 us
  Pallas kernels  533 us (39%)
  waiting for transfers between devices  351 us (26%)
  starting transfers between devices  113 us (8%)
  other arithmetic  102 us (8%)
  matrix products  78 us (6%)
  local copies, waits for them, and re-layouts  74.5 us (6%)
  blocking collectives  71.2 us (5%)
  between operations  18.1 us (1%)
    all_to_all x12, waiting for transfers between devices, send(): lax.all_to_all(buffer, 'expert', split_axis=0, concat_axis=0, tiled=True)  219 us
    pallas_call x4, Pallas kernels, expert_pass(): pl.pallas_call(functools.partial(expert_body, start is not None, last is...  197 us
    ppermute x3, waiting for transfers between devices, gather_line(): from_right.append(lax.ppermute(from_right[-1], axis, leftward))  96.5 us
    all_to_all x12, starting transfers between devices, send(): lax.all_to_all(buffer, 'expert', split_axis=0, concat_axis=0, tiled=True)  85.9 us
    pallas_call x2, Pallas kernels, last_grad(): pl.pallas_call(functools.partial(last_body, locals_, seq_len), grid=(widt...  77.2 us
    dot_general x23, matrix products, mm(): return lax.dot_general(left, right, dims, preferred_element_type=F32)  65.8 us
    pallas_call x2, Pallas kernels, attend_back(): pl.pallas_call(attend_back_body, grid=(HEADS,), in_specs=[pl.BlockSpec((l...  63.8 us
    pallas_call x1, Pallas kernels, attend(): pl.pallas_call(attend_body, grid=(seqs, HEADS), in_specs=[q_spec, pl.Bloc...  55.9 us
  transfers between devices with their start and end apart: 32, of which 16 were waited for; matrix products, arithmetic and copies ran while one was open for 17% of the time, Pallas kernels for 39%

profile of v5, /device:TPU:9, one launch (start us, length us, event | category | flops | bytes accessed | tf_op | source)
XLA Modules:
  0.0 1339.9 jit_solution(456367060611830965)
XLA Ops:
  58.2 36.2 %collective-permute-done.1 = bf16[2,256,2048]{2,1,0:T(8,128)(2,1)} collective-permute-done((bf16[2,256,2048]{2,1,0:T(8,128)(2,1)S(1)}, bf16[2,256,2048]{2,1,0:T(8,128)(2,1)}, u32[]{:S(2)}, u32[]{:S(2)}) %collective-permute-start.1) | collective-permute-done | bytes 2097184 | tf_op jit(solution)/shard_map/ppermute | solution.py:82
  104.4 34.4 %collective-permute-done.2 = bf16[2,256,2048]{2,1,0:T(8,128)(2,1)} collective-permute-done((bf16[2,256,2048]{2,1,0:T(8,128)(2,1)}, bf16[2,256,2048]{2,1,0:T(8,128)(2,1)}, u32[]{:S(2)}, u32[]{:S(2)}) %collective-permute-start.2) | collective-permute-done | bytes 2097184 | tf_op jit(solution)/shard_map/ppermute | solution.py:82
  157.0 25.9 %collective-permute-done.3 = bf16[2,256,2048]{2,1,0:T(8,128)(2,1)} collective-permute-done((bf16[2,256,2048]{2,1,0:T(8,128)(2,1)}, bf16[2,256,2048]{2,1,0:T(8,128)(2,1)}, u32[]{:S(2)}, u32[]{:S(2)}) %collective-permute-start.3) | collective-permute-done | bytes 2097184 | tf_op jit(solution)/shard_map/ppermute | solution.py:82
  255.2 18.1 %project.2 = bf16[2,544,2048]{2,1,0:T(8,128)(2,1)} custom-call(bf16[2,544,2048]{2,1,0:T(8,128)(2,1)} %bitcast.348, bf16[2048,12288]{1,0:T(8,128)(2,1)} %all-gather.6.cloned.1.call-done.w_ref.refs_0_.refs_1_), custom_call_target="tpu_custom_call" | custom-call | tf_op jit(solution)/shard_map/project/pallas_call | solution.py:181
  273.4 53.1 %key_value.1 = bf16[2048,4096]{1,0:T(8,128)(2,1)} custom-call(bf16[2048,2048]{1,0:T(8,128)(2,1)} %bitcast.327, bf16[2048,128]{1,0:T(8,128)(2,1)} %bitcast.356, bf16[2048,12288]{1,0:T(8,128)(2,1)} %all-gather.6.cloned.1.call-done.w_ref.refs_0_.refs_1_, bf16[4096,128]{1,0:T(8,128)(2,1)} %up_ref.5, f32[1024,128]{1,0:T(8,128)} %get-tuple-element.198.cos_ref.ck_ref, ...), custom_call_target="tpu_custom_call" | custom-call | tf_op jit(solution)/shard_map/key_value/pallas_call | solution.py:139
  326.5 55.9 %attend.1 = (bf16[2,2,272,2048]{3,2,1,0:T(8,128)(2,1)}, bf16[2,2,272,2048]{3,2,1,0:T(8,128)(2,1)}, bf16[2,2,16,272,1024]{4,3,2,1,0:T(8,128)(2,1)}) custom-call(bf16[2,2,272,2048]{3,2,1,0:T(8,128)(2,1)} %bitcast.347, bf16[2,1024,4096]{2,1,0:T(8,128)(2,1)} %bitcast.319, bf16[2,1024,4096]{2,1,0:T(8,128)(2,1)} %bitcast.320, ...), custom_call_target="tpu_custom_call" | custom-call | tf_op jit(solution)/shard_map/attend/pallas_call | solution.py:218
  382.4 17.7 %project.3 = (bf16[2,544,2048]{2,1,0:T(8,128)(2,1)}, bf16[2,544,2048]{2,1,0:T(8,128)(2,1)}) custom-call(bf16[2,544,2048]{2,1,0:T(8,128)(2,1)} %bitcast.357, bf16[2048,12288]{1,0:T(8,128)(2,1)} %all-gather.6.cloned.1.call-done.w_ref.refs_0_.refs_1_, f32[2,544,1]{2,1,0:T(8,128)} %fusion.88.refs_0_), custom_call_target="tpu_custom_call" | custom-call | tf_op jit(solution)/shard_map/project/pallas_call | solution.py:181
  424.1 30.6 %all-to-all-done = bf16[4,136,2048]{2,1,0:T(8,128)(2,1)} async-done(((bf16[4,136,2048]{2,1,0:T(8,128)(2,1)}), bf16[4,136,2048]{2,1,0:T(8,128)(2,1)}, u32[]{:S(2)}, u32[]{:S(2)}) %all-to-all-start) | async-done | bytes 2228256 | tf_op jit(solution)/shard_map/all_to_all | solution.py:113
  478.1 34.9 %all-to-all-done.1 = bf16[4,136,2048]{2,1,0:T(8,128)(2,1)S(1)} async-done(((bf16[4,136,2048]{2,1,0:T(8,128)(2,1)}), bf16[4,136,2048]{2,1,0:T(8,128)(2,1)S(1)}, u32[]{:S(2)}, u32[]{:S(2)}) %all-to-all-start.1) | async-done | bytes 2228256 | tf_op jit(solution)/shard_map/all_to_all | solution.py:113
  539.2 29.2 %all-to-all-done.6 = bf16[4,136,2048]{2,1,0:T(8,128)(2,1)S(1)} async-done(((bf16[4,136,2048]{2,1,0:T(8,128)(2,1)}), bf16[4,136,2048]{2,1,0:T(8,128)(2,1)S(1)}, u32[]{:S(2)}, u32[]{:S(2)}) %all-to-all-start.6) | async-done | bytes 2228256 | tf_op jit(solution)/shard_map/all_to_all | solution.py:113
  595.5 29.6 %all-to-all-done.2 = bf16[4,136,2048]{2,1,0:T(8,128)(2,1)} async-done(((bf16[4,136,2048]{2,1,0:T(8,128)(2,1)}), bf16[4,136,2048]{2,1,0:T(8,128)(2,1)}, u32[]{:S(2)}, u32[]{:S(2)}) %all-to-all-start.2) | async-done | bytes 2228256 | tf_op jit(solution)/shard_map/all_to_all | solution.py:113
  659.4 29.5 %expert.4 = (f32[544,2048]{1,0:T(8,128)}, f32[544,2048]{1,0:T(8,128)}) custom-call(bf16[544,2048]{1,0:T(8,128)(2,1)} %bitcast.62.x_ref, bf16[544,2048]{1,0:T(8,128)(2,1)} %multiply_convert_fusion.1.c_ref, bf16[2048,3072]{1,0:T(8,128)(2,1)} %bitcast.325, bf16[2048,3072]{1,0:T(8,128)(2,1)} %bitcast.326, bf16[2,5632,2048]{2,1,0:T(8,128)(2,1)} %all-gather.10.cloned.1.call-done.wd_ref), custom_call_target="tpu_custom_call" | custom-call | tf_op jit(solution)/shard_map/expert/pallas_call | solution.py:364
  688.9 69.0 %expert.5 = (bf16[544,2048]{1,0:T(8,128)(2,1)}, bf16[544,2048]{1,0:T(8,128)(2,1)}) custom-call(bf16[544,2048]{1,0:T(8,128)(2,1)} %bitcast.62.x_ref, bf16[544,2048]{1,0:T(8,128)(2,1)} %multiply_convert_fusion.1.c_ref, bf16[2048,8192]{1,0:T(8,128)(2,1)} %all-gather.8.cloned.1.call-done.wg_ref.wu_ref, ...), custom_call_target="tpu_custom_call" | custom-call | tf_op jit(solution)/shard_map/expert/pallas_call | solution.py:364
  757.9 52.6 %all_to_all.149 = bf16[4,136,2048]{2,1,0:T(8,128)(2,1)} all-to-all(bf16[4,136,2048]{2,1,0:T(8,128)(2,1)} %bitcast.370), channel_id=1, replica_groups=mesh['dp'=8,'expert'=4] {'expert'}, dimensions={0} | all-to-all | bytes 4456448 | tf_op jit(solution)/shard_map/all_to_all | solution.py:113
  823.6 66.4 %expert.6 = (f32[544,2048]{1,0:T(8,128)}, f32[544,2048]{1,0:T(8,128)}) custom-call(bf16[544,2048]{1,0:T(8,128)(2,1)} %bitcast.342, bf16[544,2048]{1,0:T(8,128)(2,1)} %multiply_convert_fusion.c_ref, bf16[2048,8192]{1,0:T(8,128)(2,1)} %all-gather.12.cloned.1.call-done.wg_ref.wu_ref, bf16[2048,8192]{1,0:T(8,128)(2,1)} %all-gather.12.cloned.1.call-done.wg_ref.wu_ref, ...), custom_call_target="tpu_custom_call" | custom-call | tf_op jit(solution)/shard_map/expert/pallas_call | solution.py:364
  897.5 32.1 %expert.7 = (bf16[544,2048]{1,0:T(8,128)(2,1)}, bf16[544,2048]{1,0:T(8,128)(2,1)}) custom-call(bf16[544,2048]{1,0:T(8,128)(2,1)} %bitcast.343, bf16[544,2048]{1,0:T(8,128)(2,1)} %multiply_convert_fusion.c_ref, bf16[2048,3072]{1,0:T(8,128)(2,1)} %all-gather.14.cloned.1.call-done.wg_ref.wu_ref, bf16[2048,3072]{1,0:T(8,128)(2,1)} %all-gather.14.cloned.1.call-done.wg_ref.wu_ref, ...), custom_call_target="tpu_custom_call" | custom-call | tf_op jit(solution)/shard_map/expert/pallas_call | solution.py:364
  946.5 36.0 %all-to-all-done.7 = bf16[4,136,2048]{2,1,0:T(8,128)(2,1)S(1)} async-done(((bf16[4,136,2048]{2,1,0:T(8,128)(2,1)}), bf16[4,136,2048]{2,1,0:T(8,128)(2,1)S(1)}, u32[]{:S(2)}, u32[]{:S(2)}) %all-to-all-start.7) | async-done | bytes 2228256 | tf_op jit(solution)/shard_map/all_to_all | solution.py:113
  1004.8 39.6 %all-to-all-done.9 = bf16[4,136,2048]{2,1,0:T(8,128)(2,1)S(1)} async-done(((bf16[4,136,2048]{2,1,0:T(8,128)(2,1)}), bf16[4,136,2048]{2,1,0:T(8,128)(2,1)S(1)}, u32[]{:S(2)}, u32[]{:S(2)}) %all-to-all-start.9) | async-done | bytes 2228256 | tf_op jit(solution)/shard_map/all_to_all | solution.py:113
  1066.7 31.9 %attend_back.2 = (bf16[2,272,2048]{2,1,0:T(8,128)(2,1)}, bf16[1024,2048]{1,0:T(8,128)(2,1)}, bf16[1024,2048]{1,0:T(8,128)(2,1)}) custom-call(bf16[2,2,272,2048]{3,2,1,0:T(8,128)(2,1)} %get-tuple-element.88.q_ref, bf16[2,1024,4096]{2,1,0:T(8,128)(2,1)} %bitcast.321, bf16[2,1024,4096]{2,1,0:T(8,128)(2,1)} %bitcast.322, ...), custom_call_target="tpu_custom_call" | custom-call | tf_op jit(solution)/shard_map/attend_back/pallas_call | solution.py:271
  1110.7 38.4 %last_grad.2 = (bf16[1024,2048]{1,0:T(8,128)(2,1)}, bf16[1024,128]{1,0:T(8,128)(2,1)}) custom-call(bf16[1024,2048]{1,0:T(8,128)(2,1)} %get-tuple-element.97.dk_ref, bf16[1024,2048]{1,0:T(8,128)(2,1)} %get-tuple-element.98.dv_ref, bf16[2,272,2048]{2,1,0:T(8,128)(2,1)} %get-tuple-element.99.dq_ref, bf16[2,1024,544]{2,1,0:T(8,128)(2,1)} %fusion.8.table_ref, ...), custom_call_target="tpu_custom_call" | custom-call | tf_op jit(solution)/shard_map/last_grad/pallas_call | solution.py:461
  1156.3 14.2 %out_back.3 = (bf16[2,272,2048]{2,1,0:T(8,128)(2,1)}, f32[2,272,1]{2,1,0:T(8,128)}) custom-call(bf16[544,2048]{1,0:T(8,128)(2,1)} %bitcast.351, bf16[544,544]{1,0:T(8,128)(2,1)} %constant.168.clone.order_ref, f32[2,2,272,1]{3,2,1,0:T(8,128)} %get-tuple-element.169.gate_ref, bf16[2,2,272,2048]{3,2,1,0:T(8,128)(2,1)} %bitcast.350, ...), custom_call_target="tpu_custom_call" | custom-call | tf_op jit(solution)/shard_map/out_back/pallas_call | solution.py:402
  1170.5 31.9 %attend_back.3 = (bf16[2,272,2048]{2,1,0:T(8,128)(2,1)}, bf16[1024,2048]{1,0:T(8,128)(2,1)}, bf16[1024,2048]{1,0:T(8,128)(2,1)}) custom-call(bf16[2,2,272,2048]{3,2,1,0:T(8,128)(2,1)} %get-tuple-element.88.q_ref, bf16[2,1024,4096]{2,1,0:T(8,128)(2,1)} %bitcast.323, bf16[2,1024,4096]{2,1,0:T(8,128)(2,1)} %bitcast.324, ...), custom_call_target="tpu_custom_call" | custom-call | tf_op jit(solution)/shard_map/attend_back/pallas_call | solution.py:271
  1202.4 38.8 %last_grad.3 = (bf16[1024,2048]{1,0:T(8,128)(2,1)}, bf16[1024,128]{1,0:T(8,128)(2,1)}) custom-call(bf16[1024,2048]{1,0:T(8,128)(2,1)} %get-tuple-element.109.dk_ref, bf16[1024,2048]{1,0:T(8,128)(2,1)} %get-tuple-element.110.dv_ref, bf16[2,272,2048]{2,1,0:T(8,128)(2,1)} %get-tuple-element.111.dq_ref, bf16[2,1024,544]{2,1,0:T(8,128)(2,1)} %fusion.8.table_ref, ...), custom_call_target="tpu_custom_call" | custom-call | tf_op jit(solution)/shard_map/last_grad/pallas_call | solution.py:461
  1308.6 20.3 %reduce-scatter.3.cloned.1.call-done.grad_ref = bf16[256,2048]{1,0:T(8,128)(2,1)} async-done(((bf16[1024,2048]{1,0:T(8,128)(2,1)}), bf16[256,2048]{1,0:T(8,128)(2,1)}) %reduce-scatter.3.cloned.1.call-update) | async-done | bytes 1048592 | tf_op jit(solution)/shard_map/reduce_scatter | solution.py:851
  (447 shorter events, 455.5 us)
Async XLA Ops:
  7.2 248.1 %all-gather.6.cloned.1.call-start = ((), (), s32[]{:S(2)}) async-start(), calls=%async_computation.16 | async-start | bytes 56623104 | tf_op jit(solution)/shard_map/all_gather | solution.py:596
  14.7 644.7 %all-gather.10.cloned.1.call-start = ((), (), s32[]{:S(2)}) async-start(), calls=%async_computation.18 | async-start | bytes 51904512 | tf_op jit(solution)/shard_map/all_gather | solution.py:597
  15.4 673.5 %all-gather.8.cloned.1.call-start = ((), (), s32[]{:S(2)}) async-start(), calls=%async_computation.17 | async-start | bytes 37748736 | tf_op jit(solution)/shard_map/all_gather | solution.py:612
  22.8 800.8 %all-gather.12.cloned.1.call-start = ((), (), s32[]{:S(2)}) async-start(), calls=%async_computation.19 | async-start | bytes 37748736 | tf_op jit(solution)/shard_map/all_gather | solution.py:611
  146.6 52.4 %collective-permute-start.5 = (bf16[2,256,2048]{2,1,0:T(8,128)(2,1)}, bf16[2,256,2048]{2,1,0:T(8,128)(2,1)S(1)}, u32[]{:S(2)}, u32[]{:S(2)}) collective-permute-start(bf16[2,256,2048]{2,1,0:T(8,128)(2,1)} %collective-permute-done.4), channel_id=1, source_target_pairs={{0,1},{1,2},{2,3},{4,5},{5,6},{6,7},{8,9},{9,10},{10,11},{12,13},{... | collective-permute-start | bytes 6291464 | tf_op jit(solution)/shard_map/ppermute | solution.py:81
  205.6 202.0 %all-to-all-start.3 = ((bf16[4,136,2048]{2,1,0:T(8,128)(2,1)}), bf16[4,136,2048]{2,1,0:T(8,128)(2,1)}, u32[]{:S(2)}, u32[]{:S(2)}) async-start(bf16[4,136,2048]{2,1,0:T(8,128)(2,1)} %bitcast.66), calls=%async_computation.3 | async-start | bytes 4456448 | tf_op jit(solution)/shard_map/all_to_all | solution.py:113
  412.2 485.3 %all-gather.14.cloned.1.call-start = ((), (), s32[]{:S(2)}) async-start(), calls=%async_computation.20 | async-start | bytes 14155776 | tf_op jit(solution)/shard_map/all_gather | solution.py:612
  414.8 51.6 %collective-permute-start.7 = (bf16[128,3072]{1,0:T(8,128)(2,1)}, bf16[128,3072]{1,0:T(8,128)(2,1)}, u32[]{:S(2)}, u32[]{:S(2)}) collective-permute-start(bf16[128,3072]{1,0:T(8,128)(2,1)} %get-tuple-element.69), channel_id=1, source_target_pairs={{0,16},{4,20},{8,24},{12,28},{16,0},{20,4},{24,8},{28,12},{1,17},{... | collective-permute-start | bytes 2359304 | tf_op jit(solution)/shard_map/ppermute | solution.py:91
  419.0 48.9 %collective-permute-start.6 = (bf16[128,3072]{1,0:T(8,128)(2,1)S(1)}, bf16[128,3072]{1,0:T(8,128)(2,1)}, u32[]{:S(2)}, u32[]{:S(2)}) collective-permute-start(bf16[128,3072]{1,0:T(8,128)(2,1)S(1)} %copy-done.24), channel_id=1, source_target_pairs={{0,8},{4,12},{8,0},{12,4},{16,24},{20,28},{24,16},{28,20},{1,9},{5... | collective-permute-start | bytes 2359304 | tf_op jit(solution)/shard_map/ppermute | solution.py:91
  454.7 58.2 %all-to-all-start.1 = ((bf16[4,136,2048]{2,1,0:T(8,128)(2,1)}), bf16[4,136,2048]{2,1,0:T(8,128)(2,1)S(1)}, u32[]{:S(2)}, u32[]{:S(2)}) async-start(bf16[4,136,2048]{2,1,0:T(8,128)(2,1)} %bitcast.364), calls=%async_computation.1 | async-start | bytes 4456448 | tf_op jit(solution)/shard_map/all_to_all | solution.py:113
  471.1 50.8 %collective-permute-start.10 = (bf16[2,128,3072]{2,1,0:T(8,128)(2,1)}, bf16[2,128,3072]{2,1,0:T(8,128)(2,1)}, u32[]{:S(2)}, u32[]{:S(2)}) collective-permute-start(bf16[2,128,3072]{2,1,0:T(8,128)(2,1)} %get-tuple-element.72), channel_id=1, source_target_pairs={{0,8},{4,12},{8,0},{12,4},{16,24},{20,28},{24,16},{28,20},{1,9},{5... | collective-permute-start | bytes 4718600 | tf_op jit(solution)/shard_map/ppermute | solution.py:91
  477.6 101.0 %collective-permute-start.8 = (bf16[2,128,3072]{2,1,0:T(8,128)(2,1)}, bf16[2,128,3072]{2,1,0:T(8,128)(2,1)}, u32[]{:S(2)}, u32[]{:S(2)}) collective-permute-start(bf16[2,128,3072]{2,1,0:T(8,128)(2,1)} %get-tuple-element.71), channel_id=1, source_target_pairs={{0,16},{4,20},{8,24},{12,28},{16,0},{20,4},{24,8},{28,12},{1,17},{... | collective-permute-start | bytes 4718600 | tf_op jit(solution)/shard_map/ppermute | solution.py:91
  514.3 54.1 %all-to-all-start.6 = ((bf16[4,136,2048]{2,1,0:T(8,128)(2,1)}), bf16[4,136,2048]{2,1,0:T(8,128)(2,1)S(1)}, u32[]{:S(2)}, u32[]{:S(2)}) async-start(bf16[4,136,2048]{2,1,0:T(8,128)(2,1)} %bitcast.368), calls=%async_computation.6 | async-start | bytes 4456448 | tf_op jit(solution)/shard_map/all_to_all | solution.py:113
  527.1 64.0 %collective-permute-start.11 = (bf16[2,2,128,3072]{3,2,1,0:T(8,128)(2,1)}, bf16[2,2,128,3072]{3,2,1,0:T(8,128)(2,1)}, u32[]{:S(2)}, u32[]{:S(2)}) collective-permute-start(bf16[2,2,128,3072]{3,2,1,0:T(8,128)(2,1)} %pad_maximum_fusion.6), channel_id=1, source_target_pairs={{0,4},{4,0},{8,12},{12,8},{16,20},{20,16},{24,28},{28,24},{1,5},{5... | collective-permute-start | bytes 9437192 | tf_op jit(solution)/shard_map/ppermute | solution.py:91
  569.9 55.2 %all-to-all-start.2 = ((bf16[4,136,2048]{2,1,0:T(8,128)(2,1)}), bf16[4,136,2048]{2,1,0:T(8,128)(2,1)}, u32[]{:S(2)}, u32[]{:S(2)}) async-start(bf16[4,136,2048]{2,1,0:T(8,128)(2,1)} %bitcast.365), calls=%async_computation.2 | async-start | bytes 4456448 | tf_op jit(solution)/shard_map/all_to_all | solution.py:113
  583.6 53.1 %collective-permute-start.9 = (bf16[2,2,128,3072]{3,2,1,0:T(8,128)(2,1)}, bf16[2,2,128,3072]{3,2,1,0:T(8,128)(2,1)}, u32[]{:S(2)}, u32[]{:S(2)}) collective-permute-start(bf16[2,2,128,3072]{3,2,1,0:T(8,128)(2,1)} %pad_maximum_fusion.5), channel_id=1, source_target_pairs={{0,4},{4,0},{8,12},{12,8},{16,20},{20,16},{24,28},{28,24},{1,5},{5... | collective-permute-start | bytes 9437192 | tf_op jit(solution)/shard_map/ppermute | solution.py:91
  625.1 132.8 %all-to-all-start.5 = ((bf16[4,136,2048]{2,1,0:T(8,128)(2,1)}), bf16[4,136,2048]{2,1,0:T(8,128)(2,1)S(1)}, u32[]{:S(2)}, u32[]{:S(2)}) async-start(bf16[4,136,2048]{2,1,0:T(8,128)(2,1)} %bitcast.363), calls=%async_computation.5 | async-start | bytes 4456448 | tf_op jit(solution)/shard_map/all_to_all | solution.py:113
  810.6 119.0 %all-to-all-start.8 = ((bf16[4,136,2048]{2,1,0:T(8,128)(2,1)}), bf16[4,136,2048]{2,1,0:T(8,128)(2,1)}, u32[]{:S(2)}, u32[]{:S(2)}) async-start(bf16[4,136,2048]{2,1,0:T(8,128)(2,1)} %bitcast.366), calls=%async_computation.8 | async-start | bytes 4456448 | tf_op jit(solution)/shard_map/all_to_all | solution.py:113
  929.7 52.8 %all-to-all-start.7 = ((bf16[4,136,2048]{2,1,0:T(8,128)(2,1)}), bf16[4,136,2048]{2,1,0:T(8,128)(2,1)S(1)}, u32[]{:S(2)}, u32[]{:S(2)}) async-start(bf16[4,136,2048]{2,1,0:T(8,128)(2,1)} %bitcast.367), calls=%async_computation.7 | async-start | bytes 4456448 | tf_op jit(solution)/shard_map/all_to_all | solution.py:113
  991.1 53.3 %all-to-all-start.9 = ((bf16[4,136,2048]{2,1,0:T(8,128)(2,1)}), bf16[4,136,2048]{2,1,0:T(8,128)(2,1)S(1)}, u32[]{:S(2)}, u32[]{:S(2)}) async-start(bf16[4,136,2048]{2,1,0:T(8,128)(2,1)} %bitcast.371), calls=%async_computation.9 | async-start | bytes 4456448 | tf_op jit(solution)/shard_map/all_to_all | solution.py:113
  1045.8 54.0 %all-to-all-start.10 = ((bf16[4,136,2048]{2,1,0:T(8,128)(2,1)}), bf16[4,136,2048]{2,1,0:T(8,128)(2,1)S(1)}, u32[]{:S(2)}, u32[]{:S(2)}) async-start(bf16[4,136,2048]{2,1,0:T(8,128)(2,1)} %bitcast.369), calls=%async_computation.10 | async-start | bytes 4456448 | tf_op jit(solution)/shard_map/all_to_all | solution.py:113
  1101.1 55.1 %all-to-all-start.11 = ((bf16[4,136,2048]{2,1,0:T(8,128)(2,1)}), bf16[4,136,2048]{2,1,0:T(8,128)(2,1)}, u32[]{:S(2)}, u32[]{:S(2)}) async-start(bf16[4,136,2048]{2,1,0:T(8,128)(2,1)} %bitcast.361), calls=%async_computation.11 | async-start | bytes 4456448 | tf_op jit(solution)/shard_map/all_to_all | solution.py:113
  1109.7 195.0 %reduce-scatter.5.cloned.1.call-start = ((), (), s32[]{:S(2)}) async-start(), calls=%async_computation.22 | async-start | bytes 5242880 | tf_op jit(solution)/shard_map/reduce_scatter | solution.py:851
  1156.3 172.7 %reduce-scatter.3.cloned.1.call-start = ((), (), s32[]{:S(2)}) async-start(), calls=%async_computation.21 | async-start | bytes 5242880 | tf_op jit(solution)/shard_map/reduce_scatter | solution.py:851
  (103 other events, 1934.2 us)
Sparse Core Ops, SparseCore 0:
  14.8 233.9 all-gather.5
  250.7 231.3 all-gather.9
  483.9 177.0 all-gather.7
  662.7 160.7 all-gather.11
  825.3 72.1 all-gather.13
  1156.4 79.4 reduce-scatter.4
  1241.4 87.5 reduce-scatter.2

commit v6 on v5

--- a/solution.py
+++ b/solution.py
@@ -72,17 +72,18 @@
     return first, second, third
 
 
-def gather_line(block, axis, size, put, start):
-    here = lax.axis_index(axis)
+def hop(from_left, from_right, axis, size):
     rightward = [(i, i + 1) for i in range(size - 1)]
     leftward = [(i + 1, i) for i in range(size - 1)]
-    from_left, from_right = [block], [block]
-    for _ in range(size - 1):
-        from_left.append(lax.ppermute(from_left[-1], axis, rightward))
-        from_right.append(lax.ppermute(from_right[-1], axis, leftward))
-    total = put(start, block, here)
+    return lax.ppermute(from_left, axis, rightward), lax.ppermute(from_right, axis, leftward)
+
+
+def put_line(hops, axis, put, start):
+    size = len(hops)
+    here = lax.axis_index(axis)
+    total = put(start, hops[0][0], here)
     for step in range(1, size):
-        piece = jnp.where(here >= step, from_left[step], from_right[size - step])
+        piece = jnp.where(here >= step, hops[step][0], hops[size - step][1])
         total = put(total, piece, lax.rem(here - step + size, size))
     return total
 
@@ -95,7 +96,7 @@
 
 def halves_bits(size):
     bits = [1 << k for k in range(1, size.bit_length() - 1)]
-    return [bits + [1], bits[::-1] + [1]]
+    return [bits, bits[::-1]]
 
 
 def in_order(halves, orders, size):
@@ -113,36 +114,63 @@
     return lax.all_to_all(buffer, "expert", split_axis=0, concat_axis=0, tiled=True)
 
 
-def kv_body(seqs, seq_len, key_tiles, x_ref, low_ref, w_ref, up_ref, cos_ref, sin_ref, out_ref):
+def merge_body(core_ref, mine_ref, other_ref, out_ref):
+    rows = mine_ref.shape[0]
+    low = core_ref[0] == 0
+    mine, other = mine_ref[...], other_ref[...]
+    out_ref[:rows, :] = jnp.where(low, mine, other)
+    out_ref[rows:, :] = jnp.where(low, other, mine)
+
+
+def merge_halves(mine, other, core, block_rows):
+    parts, rows, part = mine.shape
+    half = pl.BlockSpec((None, block_rows, part), lambda q, g: (q, g, 0))
+    return pl.pallas_call(
+        merge_body,
+        grid=(parts, rows // block_rows),
+        in_specs=[pl.BlockSpec(memory_space=pltpu.SMEM), half, half],
+        out_specs=pl.BlockSpec((2 * block_rows, part), lambda q, g: (g, q)),
+        out_shape=jax.ShapeDtypeStruct((2 * rows, parts * part), BF16),
+        compiler_params=params("arbitrary", "arbitrary"),
+        name="merge_halves",
+    )(core, mine, other)
+
+
+def kv_body(seqs, seq_len, key_tiles, x_ref, low_ref, wk_ref, wv_ref, up_ref, cos_ref, sin_ref, out_ref):
     is_key = pl.program_id(0) < key_tiles
-    for s in range(seqs):
-        rows = pl.ds(s * seq_len, seq_len)
-        made = mm(x_ref[rows, :], w_ref[...]) + mm(low_ref[rows, :], up_ref[...], NT)
-
-        @pl.when(is_key)
-        def _(made=made, rows=rows):
+
+    @pl.when(is_key)
+    def _():
+        for s in range(seqs):
+            rows = pl.ds(s * seq_len, seq_len)
+            made = mm(x_ref[rows, :], wk_ref[...]) + mm(low_ref[rows, :], up_ref[...], NT)
             for h in range(made.shape[1] // HDIM):
                 cols = slice(h * HDIM, (h + 1) * HDIM)
                 part = made[:, cols]
                 turned = part * cos_ref[...] + pltpu.roll(part, HDIM // 2, 1) * sin_ref[...]
                 out_ref[rows, cols] = turned.astype(BF16)
 
-        @pl.when(jnp.logical_not(is_key))
-        def _(made=made, rows=rows):
+    @pl.when(jnp.logical_not(is_key))
+    def _():
+        for s in range(seqs):
+            rows = pl.ds(s * seq_len, seq_len)
+            made = mm(x_ref[rows, :], wv_ref[...]) + mm(low_ref[rows, :], up_ref[...], NT)
             out_ref[rows, :] = made.astype(BF16)
 
 
-def make_key_value(normed_low, low_rank, weights, adapt_up, cos_k, sin_k, seqs):
+def make_key_value(normed_low, low_rank, weights, value_weights, adapt_up, cos_k, sin_k, seqs):
     rows, width = normed_low.shape
     seq_len = rows // seqs
     tile = 512
+    count = width // tile
     return pl.pallas_call(
-        functools.partial(kv_body, seqs, seq_len, width // tile),
-        grid=(2 * width // tile,),
+        functools.partial(kv_body, seqs, seq_len, count),
+        grid=(2 * count,),
         in_specs=[
             once((rows, width), lambda i: (0, 0)),
             once((rows, low_rank.shape[1]), lambda i: (0, 0)),
-            pl.BlockSpec((width, tile), lambda i: (0, i)),
+            pl.BlockSpec((width, tile), lambda i: (0, jnp.minimum(i, count - 1))),
+            pl.BlockSpec((width, tile), lambda i: (0, jnp.maximum(i - count, 0))),
             pl.BlockSpec((tile, low_rank.shape[1]), lambda i: (i, 0)),
             once((seq_len, HDIM), lambda i: (0, 0)),
             once((seq_len, HDIM), lambda i: (0, 0)),
@@ -151,7 +179,7 @@
         out_shape=jax.ShapeDtypeStruct((rows, 2 * width), BF16),
         compiler_params=params("arbitrary"),
         name="key_value",
-    )(normed_low, low_rank, weights, adapt_up, cos_k, sin_k)
+    )(normed_low, low_rank, weights, value_weights, adapt_up, cos_k, sin_k)
 
 
 def project_body(x_ref, w_ref, *refs):
@@ -293,11 +321,12 @@
     )(query_rot, key_value, key_value, grad, probs, cos_q, sin_q, cos_k, sin_k)
 
 
-def expert_body(has_start, is_last, x_ref, c_ref, wg_ref, wu_ref, wd_ref, *refs):
+def expert_body(has_start, is_last, joint, x_ref, c_ref, wg_ref, wu_ref, wd_ref, *refs):
     refs = list(refs)
     start = [refs.pop(0), refs.pop(0)] if has_start else []
     if is_last:
-        cot_ref, gate_ref, pick_ref, router_ref, low_ref, back_ref, out_ref, gs_ref = refs[:8]
+        cot_ref, gate_ref, pick_ref, router_ref = refs[:4]
+        made_refs, (out_ref, gs_ref) = (refs[4:5], refs[5:7]) if joint else (refs[4:6], refs[6:8])
         late = start + [cot_ref]
     else:
         out_ref, gs_ref = refs[:2]
@@ -341,11 +370,15 @@
             high = weigh.astype(BF16)
             low = (weigh - high.astype(F32)).astype(BF16)
             router = router_ref[...]
-            back_ref[...] = (back + mm(high, router, NT) + mm(low, router, NT)).astype(BF16)
-            low_ref[...] = (share * made).astype(BF16)
-
-
-def expert_pass(rows_in, grad_in, inner, down, l, down_from, start=None, last=None):
+            width = x_ref.shape[1]
+            made_refs[0][:, :width] = (back + mm(high, router, NT) + mm(low, router, NT)).astype(BF16)
+            if joint:
+                made_refs[0][:, width:] = (share * made).astype(BF16)
+            else:
+                made_refs[1][...] = (share * made).astype(BF16)
+
+
+def expert_pass(rows_in, grad_in, inner, down, l, down_from, start=None, last=None, joint=False):
     rows, width = rows_in.shape
     units = inner.shape[1] // 2
     tile = 512 if units % 512 == 0 and down_from % 512 == 0 else 256
@@ -355,14 +388,14 @@
         return once(array.shape, lambda i: (0,) * array.ndim)
 
     more = ([] if start is None else list(start)) + ([] if last is None else list(last))
-    kind = F32 if last is None else BF16
+    outs = [(2 * width, BF16)] if joint else [(width, F32 if last is None else BF16)] * 2
     late = ([] if start is None else [F32, F32]) + ([] if last is None else [BF16])
     away = len(late)
     scratch = [] if last is None else [pltpu.VMEM((rows, width), F32)] * 2
     if away:
         scratch += [pltpu.VMEM((rows, width), t) for t in late] + [pltpu.SemaphoreType.DMA((away,))]
     return pl.pallas_call(
-        functools.partial(expert_body, start is not None, last is not None),
+        functools.partial(expert_body, start is not None, last is not None, joint),
         grid=(units // tile,),
         in_specs=[
             whole(rows_in),
@@ -372,8 +405,8 @@
             pl.BlockSpec((None, tile, width), lambda i: (l, first + i, 0)),
         ]
         + [pl.BlockSpec(memory_space=pl.ANY) if i < away else whole(m) for i, m in enumerate(more)],
-        out_specs=[pl.BlockSpec((rows, width), lambda i: (0, 0))] * 2,
-        out_shape=[jax.ShapeDtypeStruct((rows, width), kind)] * 2,
+        out_specs=[once((rows, columns), lambda i: (0, 0)) for columns, _ in outs],
+        out_shape=[jax.ShapeDtypeStruct((rows, columns), kind) for columns, kind in outs],
         scratch_shapes=scratch,
         compiler_params=params("arbitrary"),
         name="expert",
@@ -427,7 +460,7 @@
 
 
 def last_body(
-    locals_, seq_len, dk_ref, dv_ref, dq_ref, table_ref, dots_ref, weigh_ref, mask_ref, up_ref, router_ref, down_ref, w_ref, *refs
+    locals_, seq_len, dk_ref, dv_ref, dq_ref, table_ref, dots_ref, weigh_ref, mask_ref, up_ref, router_ref, down_ref, wk_ref, wv_ref, *refs
 ):
     wq_refs, (out_ref, low_ref, source_ref, weigh_low_ref) = refs[:locals_], refs[locals_:]
     width = dk_ref.shape[1]
@@ -447,13 +480,15 @@
     for l in range(locals_):
         source = mm(dq_ref[l], wq_refs[l][...], NT) + mm(weigh_low_ref[l], router, NT)
         source_ref[pl.ds(l * slots, slots), :] = source.astype(BF16)
-    total = mm(dk_ref[...], w_ref[:, :width], NT) + mm(dv_ref[...], w_ref[:, width:], NT)
+    total = mm(dk_ref[...], wk_ref[...], NT) + mm(dv_ref[...], wv_ref[...], NT)
     total += mm(low_ref[...], down_ref[...], NT)
     total += mm(table_ref[0], source_ref[...])
     out_ref[...] = total.astype(BF16)
 
 
-def last_grad(s, dk, dv, dq, table, dots, weigh, mask, adapt_up, router, adapt_down, weights, query_column):
+def last_grad(
+    s, dk, dv, dq, table, dots, weigh, mask, adapt_up, router, adapt_down, weights, value_weights, query_column
+):
     seq_len, width = dk.shape
     locals_, slots, _ = dq.shape
     tile = 256
@@ -472,7 +507,8 @@
             once((2 * width, ranks), lambda i: (0, 0)),
             pl.BlockSpec((tile, EXPERTS), lambda i: (i, 0)),
             pl.BlockSpec((tile, ranks), lambda i: (i, 0)),
-            pl.BlockSpec((tile, 2 * width), lambda i: (i, 0)),
+            pl.BlockSpec((tile, width), lambda i: (i, 0)),
+            pl.BlockSpec((tile, width), lambda i: (i, 0)),
         ]
         + [
             pl.BlockSpec((tile, width), lambda i, l=l: (i, query_column // width + l))
@@ -492,7 +528,7 @@
         ],
         compiler_params=params("arbitrary"),
         name="last_grad",
-    )(dk, dv, dq, table, dots, weigh, mask, adapt_up, router, adapt_down, weights, *([weights] * locals_))
+    )(dk, dv, dq, table, dots, weigh, mask, adapt_up, router, adapt_down, weights, value_weights, *([weights] * locals_))
 
 
 def middle_back_body(back_ref, table_ref, part_ref, middle_ref, cot_ref, gain_ref, spread_ref, out_ref, rows_ref):
@@ -585,10 +621,10 @@
     slots = ranks * capacity
     here = lax.axis_index("expert")
 
-    query_column = 2 * width
+    query_column = width
     output_column = query_column + locals_ * width
     near = jnp.concatenate(
-        [kv_weight]
+        [kv_weight[:, :width]]
         + [query_weight[l] for l in range(locals_)]
         + [output_weight[l] for l in range(locals_)],
         axis=1,
@@ -685,31 +721,38 @@
         sums = mm(table, jnp.concatenate([both, jnp.ones_like(both)], axis=1))
         other_sum.append((sums[:, :1], sums[:, 1:]))
 
-    hidden_first, routes, adapters = lax.optimization_barrier((hidden_in, routes, adapters))
-    everyone = gather_line(
-        hidden_first,
+    hidden_first, routes = lax.optimization_barrier((hidden_in, routes))
+    hops = [(hidden_first, hidden_first)]
+    hops.append(hop(*hops[-1], "expert", ranks))
+
+    orders = halves_bits(groups)
+
+    def halves_of(block):
+        return [block[: block.shape[0] // 2], block[block.shape[0] // 2 :]]
+
+    def exchange_halves(halves, step):
+        return [exchange(half, "dp", groups, bits[step]) for half, bits in zip(halves, orders)]
+
+    part = width // ranks
+    value_half = halves_of(lax.dynamic_slice_in_dim(kv_weight, width + here * part, part, 1))
+    for step in range(len(orders[0])):
+        value_half = exchange_halves(value_half, step)
+    value_half = in_order(value_half, orders, groups // 2)
+    while len(hops) < ranks:
+        hops.append(hop(*hops[-1], "expert", ranks))
+    value_half, hops[-1] = lax.optimization_barrier((value_half, hops[-1]))
+    value_hops = [(value_half, value_half)]
+    while len(value_hops) < 3:
+        value_hops.append(hop(*value_hops[-1], "expert", ranks))
+    everyone = put_line(
+        hops,
         "expert",
-        ranks,
         lambda total, piece, at: lax.dynamic_update_slice(total, piece[:, None], (0, at, 0, 0)),
         jnp.zeros((seqs, ranks, row_count, width), BF16),
     ).reshape(seqs, seq_len, width)
-
-    flat_cot, everyone = lax.optimization_barrier((cotangent, everyone))
-    orders = halves_bits(groups)
-    beside = [[block[: block.shape[0] // 2], block[block.shape[0] // 2 :]] for block in beside]
-
-    def exchange_all(step):
-        return [
-            [exchange(half, "dp", groups, bits[step]) for half, bits in zip(halves, orders)]
-            for halves in beside
-        ]
-
-    flat_cot = flat_cot.reshape(seqs * row_count, width)
-    cot_rows = [send(mm(own_spread_m[l], flat_cot).astype(BF16)) for l in range(locals_)]
-
     tokens_all = everyone.astype(F32)
     scale_all = rms_scale(tokens_all)
-    normed_low = (tokens_all * scale_all * attn_gain).astype(BF16)
+    normed_low = lax.optimization_barrier((tokens_all * scale_all * attn_gain).astype(BF16))
     router_parts = jnp.concatenate(three_parts(attn_gain[:, None] * attn_router.astype(F32)), axis=1)
     parts = mm(everyone.reshape(seqs * seq_len, width), router_parts).reshape(seqs, seq_len, 3, EXPERTS)
     logits = scale_all * (parts[:, :, 0] + (parts[:, :, 1] + parts[:, :, 2]))
@@ -749,10 +792,6 @@
     )
     low_rank = mm(flat_low, adapt_down).reshape(seqs, seq_len, NADAPT * RANK)
     low_rank = jnp.where(own_adapter[:, None, :], low_rank, 0.0).astype(BF16)
-    key_value = make_key_value(
-        flat_low, low_rank.reshape(seqs * seq_len, -1), near_full, adapt_up, cos_k, sin_k, seqs
-    ).reshape(seqs, seq_len, 2 * width)
-
     picked = jnp.einsum(
         "slrt,std->lsrd",
         spread_a.reshape(seqs, locals_, slots, seq_len),
@@ -760,11 +799,37 @@
         preferred_element_type=F32,
     ).astype(BF16)
     beside, picked = lax.optimization_barrier((beside, picked))
-    beside = exchange_all(0)
+    beside = [exchange_halves(halves_of(block), 0) for block in beside]
     queries = project(picked.reshape(locals_, seqs * slots, width), near_full, query_column)
+    value_hops[2], normed_low = lax.optimization_barrier((value_hops[2], normed_low))
+    while len(value_hops) < ranks:
+        value_hops.append(hop(*value_hops[-1], "expert", ranks))
+    value_line = put_line(
+        value_hops,
+        "expert",
+        lambda total, piece, at: lax.dynamic_update_slice(total, piece[None], (at, 0, 0)),
+        jnp.zeros((ranks, *value_half.shape), BF16),
+    )
+    value_line, queries, low_rank = lax.optimization_barrier((value_line, queries, low_rank))
+    value_full = merge_halves(
+        value_line,
+        lax.ppermute(value_line, "dp", [(i, i ^ 1) for i in range(groups)]),
+        jnp.bitwise_and(lax.axis_index("dp"), 1).astype(jnp.int32).reshape(1),
+        kv_weight.shape[0],
+    )
+
+    flat_cot, value_full = lax.optimization_barrier((cotangent, value_full))
+    flat_cot = flat_cot.reshape(seqs * row_count, width)
+    cot_rows = [send(mm(own_spread_m[l], flat_cot).astype(BF16)) for l in range(locals_)]
+
+    key_value = make_key_value(
+        flat_low, low_rank.reshape(seqs * seq_len, -1), near_full, value_full, adapt_up, cos_k, sin_k, seqs
+    ).reshape(seqs, seq_len, 2 * width)
+
     query_rot, attended, probs = attend(
         queries.reshape(locals_, seqs, slots, width), key_value, cos_q, sin_q, query_blocks, key_blocks
     )
+    cot_rows[0], attended = lax.optimization_barrier((cot_rows[0], attended))
     gate_rows = gate_a[..., None]
     projected, gated = project(
         attended.reshape(locals_, seqs * slots, width),
@@ -773,10 +838,11 @@
         gate_rows.reshape(locals_, seqs * slots, 1),
     )
     beside, projected = lax.optimization_barrier((beside, projected))
-    for step in range(1, len(orders[0])):
-        beside = exchange_all(step)
     for l, halves in enumerate(beside):
-        inner_full[l][0] = (0, in_order(halves, orders, groups))
+        for step in range(1, len(orders[0])):
+            halves = exchange_halves(halves, step)
+        halves = [exchange(half, "dp", groups, 1) for half in halves]
+        inner_full[l][0] = (0, in_order(halves, [bits + [1] for bits in orders], groups))
     projected = projected.reshape(locals_, seqs, slots, width)
     gated = gated.reshape(locals_, seqs, slots, width)
     order = np.arange(locals_ * slots).reshape(locals_, ranks, capacity).transpose(1, 0, 2).reshape(-1)
@@ -805,16 +871,15 @@
         grad_rows = (gate_m * cot_rows[l].astype(F32)).astype(BF16)
         made = None
         for at, (low, inner) in enumerate(inner_full[l]):
-            if held is not None and at + 1 == len(inner_full[l]):
-                held, made = lax.optimization_barrier((held, made))
-                final = final + mm(own_collect_m[l - 1], held)
             ends = (cot_rows[l], gate_m, pick_m, mlp_router) if at + 1 == len(inner_full[l]) else None
-            made = expert_pass(rows_in, grad_rows, inner, down_full, l, low, made, ends)
-        gated_out, grad_source = made
-        grad_back = send(grad_source)
+            joint = ends is not None and l + 1 < locals_
+            made = expert_pass(rows_in, grad_rows, inner, down_full, l, low, made, ends, joint)
         if l + 1 < locals_:
-            grad_normed_two = grad_normed_two + mm(own_collect_m[l], grad_back)
-        held = send(gated_out) if l + 1 < locals_ else gated_out
+            both_back = send(made[0])
+            grad_normed_two = grad_normed_two + mm(own_collect_m[l], both_back[:, :width])
+            final = final + mm(own_collect_m[l], both_back[:, width:])
+        else:
+            grad_back, held = send(made[0]), made[1]
     grad_normed_two = grad_normed_two.reshape(seqs, row_count, width)
     late = (collect_a, own_adapter.astype(F32)[:, None, :], weigh_a, attn_router, to_slots)
     (collect_a, mask, weigh_a, router_near, to_slots), grad_normed_two = lax.optimization_barrier(
@@ -844,7 +909,7 @@
             held = send(held)
         part, grad_low = last_grad(
             s, dk, dv, dq, collect_a, dots, weigh_a, mask, adapt_up, router_near, adapt_down, near_full,
-            query_column,
+            value_full, query_column,
         )
         if s + 1 < seqs:
             arrived[s + 1], held, part = lax.optimization_barrier((arrived[s + 1], held, part))

time: 1350 us -> 1340 us (level)
  blocking collectives: 71.2 us -> 23.1 us
  starting transfers between devices: 113 us -> 155 us
  waiting for transfers between devices: 351 us -> 337 us
    all_to_all x1 -> x0, blocking collectives: 52.6 us -> none  [send(): lax.all_to_all(buffer, 'expert', split_axis=0, concat_axis=0, tiled=True)]
    ppermute x6 -> x13, starting transfers between devices: 15.6 us -> 52 us  [the longest x6 25.9 us: hop(): lax.ppermute(from_right, axis, leftward)]
    ppermute x6 -> x10, waiting for transfers between devices: 0.02 us -> 34.5 us  [exchange(): other = lax.ppermute(total, axis, [(i, i ^ bit) for i in range(size)])]
    all_to_all x12, waiting for transfers between devices: 219 us -> 190 us  [send(): lax.all_to_all(buffer, 'expert', split_axis=0, concat_axis=0, tiled=True)]
    pallas_call x1 -> x2, Pallas kernels: 53.1 us -> 60.8 us  [the longest x1 48.8 us: make_key_value(): pl.pallas_call(functools.partial(kv_body, seqs, seq_len, count), grid=(2...]
    ppermute x6 -> x13, waiting for transfers between devices: 96.5 us -> 98.1 us  [the longest x6 89 us: hop(): lax.ppermute(from_left, axis, rightward)]
  transfers between devices with their start and end apart: 32 -> 43, of which waited for: 16 -> 20; matrix products, arithmetic and copies ran while one was open for 17% -> 18% of each run, Pallas kernels for 39% -> 40%
where the time goes in v6:
time: 1340 us; the launch traced here: 1330 us
  Pallas kernels  541 us (40%)
  waiting for transfers between devices  337 us (25%)
  starting transfers between devices  155 us (12%)
  other arithmetic  105 us (8%)
  matrix products  81.1 us (6%)
  local copies, waits for them, and re-layouts  69.7 us (5%)
  blocking collectives  23.1 us (2%)
  between operations  18.1 us (1%)
    pallas_call x4, Pallas kernels, expert_pass(): pl.pallas_call(functools.partial(expert_body, start is not None, last is...  199 us
    all_to_all x12, waiting for transfers between devices, send(): lax.all_to_all(buffer, 'expert', split_axis=0, concat_axis=0, tiled=True)  190 us
    ppermute x6, waiting for transfers between devices, hop(): lax.ppermute(from_left, axis, rightward)  89 us
    all_to_all x12, starting transfers between devices, send(): lax.all_to_all(buffer, 'expert', split_axis=0, concat_axis=0, tiled=True)  83.2 us
    pallas_call x2, Pallas kernels, last_grad(): pl.pallas_call(functools.partial(last_body, locals_, seq_len), grid=(widt...  77.4 us
    dot_general x23, matrix products, mm(): return lax.dot_general(left, right, dims, preferred_element_type=F32)  69 us
    pallas_call x2, Pallas kernels, attend_back(): pl.pallas_call(attend_back_body, grid=(HEADS,), in_specs=[pl.BlockSpec((l...  63.9 us
    pallas_call x1, Pallas kernels, attend(): pl.pallas_call(attend_body, grid=(seqs, HEADS), in_specs=[q_spec, pl.Bloc...  55.9 us
  transfers between devices with their start and end apart: 43, of which 20 were waited for; matrix products, arithmetic and copies ran while one was open for 18% of the time, Pallas kernels for 40%

profile of v6, /device:TPU:9, one launch (start us, length us, event | category | flops | bytes accessed | tf_op | source)
XLA Modules:
  0.0 1330.2 jit_solution(16867420203058001429)
XLA Ops:
  50.7 35.4 %collective-permute-done.4 = bf16[2,256,2048]{2,1,0:T(8,128)(2,1)} collective-permute-done((bf16[2,256,2048]{2,1,0:T(8,128)(2,1)S(1)}, bf16[2,256,2048]{2,1,0:T(8,128)(2,1)}, u32[]{:S(2)}, u32[]{:S(2)}) %collective-permute-start.4) | collective-permute-done | bytes 2097184 | tf_op jit(solution)/shard_map/ppermute | solution.py:78
  105.3 26.0 %collective-permute-done.5 = bf16[2,256,2048]{2,1,0:T(8,128)(2,1)} collective-permute-done((bf16[2,256,2048]{2,1,0:T(8,128)(2,1)}, bf16[2,256,2048]{2,1,0:T(8,128)(2,1)}, u32[]{:S(2)}, u32[]{:S(2)}) %collective-permute-start.5) | collective-permute-done | bytes 2097184 | tf_op jit(solution)/shard_map/ppermute | solution.py:78
  152.7 22.9 %collective-permute-done.6 = bf16[2,256,2048]{2,1,0:T(8,128)(2,1)} collective-permute-done((bf16[2,256,2048]{2,1,0:T(8,128)(2,1)}, bf16[2,256,2048]{2,1,0:T(8,128)(2,1)}, u32[]{:S(2)}, u32[]{:S(2)}) %collective-permute-start.6) | collective-permute-done | bytes 2097184 | tf_op jit(solution)/shard_map/ppermute | solution.py:78
  255.7 16.1 %project.2 = bf16[2,544,2048]{2,1,0:T(8,128)(2,1)} custom-call(bf16[2,544,2048]{2,1,0:T(8,128)(2,1)} %bitcast.373, bf16[2048,10240]{1,0:T(8,128)(2,1)} %all-gather.6.cloned.1.call-done.w_ref.wk_ref.refs_0_.refs_1_), custom_call_target="tpu_custom_call" | custom-call | tf_op jit(solution)/shard_map/project/pallas_call | solution.py:209
  332.0 48.8 %key_value.1 = bf16[2048,4096]{1,0:T(8,128)(2,1)} custom-call(bf16[2048,2048]{1,0:T(8,128)(2,1)} %bitcast.356, bf16[2048,128]{1,0:T(8,128)(2,1)} %bitcast.380, bf16[2048,10240]{1,0:T(8,128)(2,1)} %all-gather.6.cloned.1.call-done.w_ref.wk_ref.refs_0_.refs_1_, bf16[2048,2048]{1,0:T(8,128)(2,1)} %merge_halves.1.wv_ref, bf16[4096,128]{1,0:T(8,128)(2,1)} %up_ref.5, ...), custom_call_target="tpu_custom_call" | custom-call | tf_op jit(solution)/shard_map/key_value/pallas_call | solution.py:166
  380.8 55.9 %attend.1 = (bf16[2,2,272,2048]{3,2,1,0:T(8,128)(2,1)}, bf16[2,2,272,2048]{3,2,1,0:T(8,128)(2,1)}, bf16[2,2,16,272,1024]{4,3,2,1,0:T(8,128)(2,1)}) custom-call(bf16[2,2,272,2048]{3,2,1,0:T(8,128)(2,1)} %bitcast.371, bf16[2,1024,4096]{2,1,0:T(8,128)(2,1)} %bitcast.348, bf16[2,1024,4096]{2,1,0:T(8,128)(2,1)} %bitcast.349, ...), custom_call_target="tpu_custom_call" | custom-call | tf_op jit(solution)/shard_map/attend/pallas_call | solution.py:246
  436.7 18.2 %project.3 = (bf16[2,544,2048]{2,1,0:T(8,128)(2,1)}, bf16[2,544,2048]{2,1,0:T(8,128)(2,1)}) custom-call(bf16[2,544,2048]{2,1,0:T(8,128)(2,1)} %bitcast.381, bf16[2048,10240]{1,0:T(8,128)(2,1)} %all-gather.6.cloned.1.call-done.w_ref.wk_ref.refs_0_.refs_1_, f32[2,544,1]{2,1,0:T(8,128)} %fusion.88.refs_0_), custom_call_target="tpu_custom_call" | custom-call | tf_op jit(solution)/shard_map/project/pallas_call | solution.py:209
  479.7 35.3 %all-to-all-done.1 = bf16[4,136,2048]{2,1,0:T(8,128)(2,1)} async-done(((bf16[4,136,2048]{2,1,0:T(8,128)(2,1)}), bf16[4,136,2048]{2,1,0:T(8,128)(2,1)}, u32[]{:S(2)}, u32[]{:S(2)}) %all-to-all-start.1) | async-done | bytes 2228256 | tf_op jit(solution)/shard_map/all_to_all | solution.py:114
  538.4 31.0 %all-to-all-done.2 = bf16[4,136,2048]{2,1,0:T(8,128)(2,1)} async-done(((bf16[4,136,2048]{2,1,0:T(8,128)(2,1)}), bf16[4,136,2048]{2,1,0:T(8,128)(2,1)}, u32[]{:S(2)}, u32[]{:S(2)}) %all-to-all-start.2) | async-done | bytes 2228256 | tf_op jit(solution)/shard_map/all_to_all | solution.py:114
  577.0 24.0 %collective-permute-done.21 = bf16[2,128,3072]{2,1,0:T(8,128)(2,1)} collective-permute-done((bf16[2,128,3072]{2,1,0:T(8,128)(2,1)}, bf16[2,128,3072]{2,1,0:T(8,128)(2,1)}, u32[]{:S(2)}, u32[]{:S(2)}) %collective-permute-start.21) | collective-permute-done | bytes 1572896 | tf_op jit(solution)/shard_map/ppermute | solution.py:92
  649.1 29.7 %all-to-all-done.3 = bf16[4,136,2048]{2,1,0:T(8,128)(2,1)} async-done(((bf16[4,136,2048]{2,1,0:T(8,128)(2,1)}), bf16[4,136,2048]{2,1,0:T(8,128)(2,1)}, u32[]{:S(2)}, u32[]{:S(2)}) %all-to-all-start.3) | async-done | bytes 2228256 | tf_op jit(solution)/shard_map/all_to_all | solution.py:114
  713.1 29.6 %expert.4 = (f32[544,2048]{1,0:T(8,128)}, f32[544,2048]{1,0:T(8,128)}) custom-call(bf16[544,2048]{1,0:T(8,128)(2,1)} %bitcast.84.x_ref, bf16[544,2048]{1,0:T(8,128)(2,1)} %multiply_convert_fusion.2.c_ref, bf16[2048,3072]{1,0:T(8,128)(2,1)} %bitcast.354, bf16[2048,3072]{1,0:T(8,128)(2,1)} %bitcast.355, bf16[2,5632,2048]{2,1,0:T(8,128)(2,1)} %all-gather.10.cloned.1.call-done.wd_ref), custom_call_target="tpu_custom_call" | custom-call | tf_op jit(solution)/shard_map/expert/pallas_call | solution.py:397
  742.7 69.6 %expert.5 = bf16[544,4096]{1,0:T(8,128)(2,1)} custom-call(bf16[544,2048]{1,0:T(8,128)(2,1)} %bitcast.84.x_ref, bf16[544,2048]{1,0:T(8,128)(2,1)} %multiply_convert_fusion.2.c_ref, bf16[2048,8192]{1,0:T(8,128)(2,1)} %all-gather.8.cloned.1.call-done.wg_ref.wu_ref, bf16[2048,8192]{1,0:T(8,128)(2,1)} %all-gather.8.cloned.1.call-done.wg_ref.wu_ref, ...), custom_call_target="tpu_custom_call" | custom-call | tf_op jit(solution)/shard_map/expert/pallas_call | solution.py:397
  821.1 67.7 %expert.6 = (f32[544,2048]{1,0:T(8,128)}, f32[544,2048]{1,0:T(8,128)}) custom-call(bf16[544,2048]{1,0:T(8,128)(2,1)} %bitcast.364, bf16[544,2048]{1,0:T(8,128)(2,1)} %multiply_convert_fusion.1.c_ref, bf16[2048,8192]{1,0:T(8,128)(2,1)} %all-gather.14.cloned.1.call-done.wg_ref.wu_ref, bf16[2048,8192]{1,0:T(8,128)(2,1)} %all-gather.14.cloned.1.call-done.wg_ref.wu_ref, ...), custom_call_target="tpu_custom_call" | custom-call | tf_op jit(solution)/shard_map/expert/pallas_call | solution.py:397
  888.8 32.2 %expert.7 = (bf16[544,2048]{1,0:T(8,128)(2,1)}, bf16[544,2048]{1,0:T(8,128)(2,1)}) custom-call(bf16[544,2048]{1,0:T(8,128)(2,1)} %bitcast.365, bf16[544,2048]{1,0:T(8,128)(2,1)} %multiply_convert_fusion.1.c_ref, bf16[2048,3072]{1,0:T(8,128)(2,1)} %all-gather.12.cloned.1.call-done.wg_ref.wu_ref, ...), custom_call_target="tpu_custom_call" | custom-call | tf_op jit(solution)/shard_map/expert/pallas_call | solution.py:397
  937.9 34.4 %all-to-all-done.7 = bf16[4,136,2048]{2,1,0:T(8,128)(2,1)S(1)} async-done(((bf16[4,136,2048]{2,1,0:T(8,128)(2,1)}), bf16[4,136,2048]{2,1,0:T(8,128)(2,1)S(1)}, u32[]{:S(2)}, u32[]{:S(2)}) %all-to-all-start.7) | async-done | bytes 2228256 | tf_op jit(solution)/shard_map/all_to_all | solution.py:114
  996.0 39.4 %all-to-all-done.8 = bf16[4,136,2048]{2,1,0:T(8,128)(2,1)S(1)} async-done(((bf16[4,136,2048]{2,1,0:T(8,128)(2,1)}), bf16[4,136,2048]{2,1,0:T(8,128)(2,1)S(1)}, u32[]{:S(2)}, u32[]{:S(2)}) %all-to-all-start.8) | async-done | bytes 2228256 | tf_op jit(solution)/shard_map/all_to_all | solution.py:114
  1044.3 13.5 %out_back.2 = (bf16[2,272,2048]{2,1,0:T(8,128)(2,1)}, f32[2,272,1]{2,1,0:T(8,128)}) custom-call(bf16[544,2048]{1,0:T(8,128)(2,1)} %bitcast.377, bf16[544,544]{1,0:T(8,128)(2,1)} %constant.176.clone.order_ref, f32[2,2,272,1]{3,2,1,0:T(8,128)} %get-tuple-element.183.gate_ref, bf16[2,2,272,2048]{3,2,1,0:T(8,128)(2,1)} %bitcast.369, ...), custom_call_target="tpu_custom_call" | custom-call | tf_op jit(solution)/shard_map/out_back/pallas_call | solution.py:435
  1057.8 31.9 %attend_back.2 = (bf16[2,272,2048]{2,1,0:T(8,128)(2,1)}, bf16[1024,2048]{1,0:T(8,128)(2,1)}, bf16[1024,2048]{1,0:T(8,128)(2,1)}) custom-call(bf16[2,2,272,2048]{3,2,1,0:T(8,128)(2,1)} %get-tuple-element.96.q_ref, bf16[2,1024,4096]{2,1,0:T(8,128)(2,1)} %bitcast.350, bf16[2,1024,4096]{2,1,0:T(8,128)(2,1)} %bitcast.351, ...), custom_call_target="tpu_custom_call" | custom-call | tf_op jit(solution)/shard_map/attend_back/pallas_call | solution.py:299
  1100.2 38.7 %last_grad.2 = (bf16[1024,2048]{1,0:T(8,128)(2,1)}, bf16[1024,128]{1,0:T(8,128)(2,1)}) custom-call(bf16[1024,2048]{1,0:T(8,128)(2,1)} %get-tuple-element.105.dk_ref, bf16[1024,2048]{1,0:T(8,128)(2,1)} %get-tuple-element.106.dv_ref, bf16[2,272,2048]{2,1,0:T(8,128)(2,1)} %get-tuple-element.107.dq_ref, bf16[2,1024,544]{2,1,0:T(8,128)(2,1)} %fusion.3.table_ref, ...), custom_call_target="tpu_custom_call" | custom-call | tf_op jit(solution)/shard_map/last_grad/pallas_call | solution.py:496
  1145.9 14.3 %out_back.3 = (bf16[2,272,2048]{2,1,0:T(8,128)(2,1)}, f32[2,272,1]{2,1,0:T(8,128)}) custom-call(bf16[544,2048]{1,0:T(8,128)(2,1)} %bitcast.376, bf16[544,544]{1,0:T(8,128)(2,1)} %constant.176.clone.order_ref, f32[2,2,272,1]{3,2,1,0:T(8,128)} %get-tuple-element.183.gate_ref, bf16[2,2,272,2048]{3,2,1,0:T(8,128)(2,1)} %bitcast.370, ...), custom_call_target="tpu_custom_call" | custom-call | tf_op jit(solution)/shard_map/out_back/pallas_call | solution.py:435
  1160.2 31.9 %attend_back.3 = (bf16[2,272,2048]{2,1,0:T(8,128)(2,1)}, bf16[1024,2048]{1,0:T(8,128)(2,1)}, bf16[1024,2048]{1,0:T(8,128)(2,1)}) custom-call(bf16[2,2,272,2048]{3,2,1,0:T(8,128)(2,1)} %get-tuple-element.96.q_ref, bf16[2,1024,4096]{2,1,0:T(8,128)(2,1)} %bitcast.352, bf16[2,1024,4096]{2,1,0:T(8,128)(2,1)} %bitcast.353, ...), custom_call_target="tpu_custom_call" | custom-call | tf_op jit(solution)/shard_map/attend_back/pallas_call | solution.py:299
  1192.2 38.8 %last_grad.3 = (bf16[1024,2048]{1,0:T(8,128)(2,1)}, bf16[1024,128]{1,0:T(8,128)(2,1)}) custom-call(bf16[1024,2048]{1,0:T(8,128)(2,1)} %get-tuple-element.117.dk_ref, bf16[1024,2048]{1,0:T(8,128)(2,1)} %get-tuple-element.118.dv_ref, bf16[2,272,2048]{2,1,0:T(8,128)(2,1)} %get-tuple-element.119.dq_ref, bf16[2,1024,544]{2,1,0:T(8,128)(2,1)} %fusion.3.table_ref, ...), custom_call_target="tpu_custom_call" | custom-call | tf_op jit(solution)/shard_map/last_grad/pallas_call | solution.py:496
  1305.8 13.2 reduce-scatter.3.cloned.1.call-done.grad_ref
  (465 shorter events, 513.7 us)
Async XLA Ops:
  7.2 248.5 %all-gather.6.cloned.1.call-start = ((), (), s32[]{:S(2)}) async-start(), calls=%async_computation.15 | async-start | bytes 47185920 | tf_op jit(solution)/shard_map/all_gather | solution.py:632
  15.2 697.9 %all-gather.10.cloned.1.call-start = ((), (), s32[]{:S(2)}) async-start(), calls=%async_computation.17 | async-start | bytes 51904512 | tf_op jit(solution)/shard_map/all_gather | solution.py:633
  15.9 726.8 %all-gather.8.cloned.1.call-start = ((), (), s32[]{:S(2)}) async-start(), calls=%async_computation.16 | async-start | bytes 37748736 | tf_op jit(solution)/shard_map/all_gather | solution.py:648
  23.3 797.8 %all-gather.14.cloned.1.call-start = ((), (), s32[]{:S(2)}) async-start(), calls=%async_computation.19 | async-start | bytes 37748736 | tf_op jit(solution)/shard_map/all_gather | solution.py:647
  47.7 90.3 %collective-permute-start = (bf16[128,512]{1,0:T(8,128)(2,1)S(1)}, bf16[128,512]{1,0:T(8,128)(2,1)S(1)}, u32[]{:S(2)}, u32[]{:S(2)}) collective-permute-start(bf16[128,512]{1,0:T(8,128)(2,1)S(1)} %get-tuple-element.175), channel_id=1, source_target_pairs={{0,8},{4,12},{8,0},{12,4},{16,24},{20,28},{24,16},{28,20},{1,9},{5... | collective-permute-start | bytes 393224 | tf_op jit(solution)/shard_map/ppermute | solution.py:92
  49.0 90.4 %collective-permute-start.2 = (bf16[128,512]{1,0:T(8,128)(2,1)S(1)}, bf16[128,512]{1,0:T(8,128)(2,1)}, u32[]{:S(2)}, u32[]{:S(2)}) collective-permute-start(bf16[128,512]{1,0:T(8,128)(2,1)S(1)} %get-tuple-element.176), channel_id=1, source_target_pairs={{0,16},{4,20},{8,24},{12,28},{16,0},{20,4},{24,8},{28,12},{1,17},{... | collective-permute-start | bytes 393224 | tf_op jit(solution)/shard_map/ppermute | solution.py:92
  306.7 130.0 %all-to-all-start = ((bf16[4,136,2048]{2,1,0:T(8,128)(2,1)}), bf16[4,136,2048]{2,1,0:T(8,128)(2,1)}, u32[]{:S(2)}, u32[]{:S(2)}) async-start(bf16[4,136,2048]{2,1,0:T(8,128)(2,1)} %bitcast.389), calls=%async_computation | async-start | bytes 4456448 | tf_op jit(solution)/shard_map/all_to_all | solution.py:114
  463.1 51.8 %all-to-all-start.1 = ((bf16[4,136,2048]{2,1,0:T(8,128)(2,1)}), bf16[4,136,2048]{2,1,0:T(8,128)(2,1)}, u32[]{:S(2)}, u32[]{:S(2)}) async-start(bf16[4,136,2048]{2,1,0:T(8,128)(2,1)} %bitcast.395), calls=%async_computation.1 | async-start | bytes 4456448 | tf_op jit(solution)/shard_map/all_to_all | solution.py:114
  467.7 421.1 %all-gather.12.cloned.1.call-start = ((), (), s32[]{:S(2)}) async-start(), calls=%async_computation.18 | async-start | bytes 14155776 | tf_op jit(solution)/shard_map/all_gather | solution.py:648
  472.9 53.3 %collective-permute-start.17 = (bf16[128,3072]{1,0:T(8,128)(2,1)}, bf16[128,3072]{1,0:T(8,128)(2,1)}, u32[]{:S(2)}, u32[]{:S(2)}) collective-permute-start(bf16[128,3072]{1,0:T(8,128)(2,1)} %get-tuple-element.180), channel_id=1, source_target_pairs={{0,8},{4,12},{8,0},{12,4},{16,24},{20,28},{24,16},{28,20},{1,9},{5... | collective-permute-start | bytes 2359304 | tf_op jit(solution)/shard_map/ppermute | solution.py:92
  474.4 51.9 %collective-permute-start.18 = (bf16[128,3072]{1,0:T(8,128)(2,1)S(1)}, bf16[128,3072]{1,0:T(8,128)(2,1)}, u32[]{:S(2)}, u32[]{:S(2)}) collective-permute-start(bf16[128,3072]{1,0:T(8,128)(2,1)S(1)} %get-tuple-element.179), channel_id=1, source_target_pairs={{0,16},{4,20},{8,24},{12,28},{16,0},{20,4},{24,8},{28,12},{1,17},{... | collective-permute-start | bytes 2359304 | tf_op jit(solution)/shard_map/ppermute | solution.py:92
  514.9 54.4 %all-to-all-start.2 = ((bf16[4,136,2048]{2,1,0:T(8,128)(2,1)}), bf16[4,136,2048]{2,1,0:T(8,128)(2,1)}, u32[]{:S(2)}, u32[]{:S(2)}) async-start(bf16[4,136,2048]{2,1,0:T(8,128)(2,1)} %bitcast.388), calls=%async_computation.2 | async-start | bytes 4456448 | tf_op jit(solution)/shard_map/all_to_all | solution.py:114
  531.2 69.7 %collective-permute-start.21 = (bf16[2,128,3072]{2,1,0:T(8,128)(2,1)}, bf16[2,128,3072]{2,1,0:T(8,128)(2,1)}, u32[]{:S(2)}, u32[]{:S(2)}) collective-permute-start(bf16[2,128,3072]{2,1,0:T(8,128)(2,1)} %get-tuple-element.85), channel_id=1, source_target_pairs={{0,8},{4,12},{8,0},{12,4},{16,24},{20,28},{24,16},{28,20},{1,9},{5... | collective-permute-start | bytes 4718600 | tf_op jit(solution)/shard_map/ppermute | solution.py:92
  537.5 94.8 %collective-permute-start.19 = (bf16[2,128,3072]{2,1,0:T(8,128)(2,1)}, bf16[2,128,3072]{2,1,0:T(8,128)(2,1)}, u32[]{:S(2)}, u32[]{:S(2)}) collective-permute-start(bf16[2,128,3072]{2,1,0:T(8,128)(2,1)} %get-tuple-element.84), channel_id=1, source_target_pairs={{0,16},{4,20},{8,24},{12,28},{16,0},{20,4},{24,8},{28,12},{1,17},{... | collective-permute-start | bytes 4718600 | tf_op jit(solution)/shard_map/ppermute | solution.py:92
  569.4 54.1 %all-to-all-start.6 = ((bf16[4,136,2048]{2,1,0:T(8,128)(2,1)}), bf16[4,136,2048]{2,1,0:T(8,128)(2,1)S(1)}, u32[]{:S(2)}, u32[]{:S(2)}) async-start(bf16[4,136,2048]{2,1,0:T(8,128)(2,1)} %bitcast.392), calls=%async_computation.6 | async-start | bytes 4456448 | tf_op jit(solution)/shard_map/all_to_all | solution.py:114
  623.5 55.4 %all-to-all-start.3 = ((bf16[4,136,2048]{2,1,0:T(8,128)(2,1)}), bf16[4,136,2048]{2,1,0:T(8,128)(2,1)}, u32[]{:S(2)}, u32[]{:S(2)}) async-start(bf16[4,136,2048]{2,1,0:T(8,128)(2,1)} %bitcast.391), calls=%async_computation.3 | async-start | bytes 4456448 | tf_op jit(solution)/shard_map/all_to_all | solution.py:114
  637.0 53.4 %collective-permute-start.20 = (bf16[2,2,128,3072]{3,2,1,0:T(8,128)(2,1)}, bf16[2,2,128,3072]{3,2,1,0:T(8,128)(2,1)}, u32[]{:S(2)}, u32[]{:S(2)}) collective-permute-start(bf16[2,2,128,3072]{3,2,1,0:T(8,128)(2,1)} %pad_maximum_fusion.5), channel_id=1, source_target_pairs={{0,4},{4,0},{8,12},{12,8},{16,20},{20,16},{24,28},{28,24},{1,5},{5... | collective-permute-start | bytes 9437192 | tf_op jit(solution)/shard_map/ppermute | solution.py:92
  678.9 133.5 %all-to-all-start.5 = ((bf16[4,136,2048]{2,1,0:T(8,128)(2,1)}), bf16[4,136,2048]{2,1,0:T(8,128)(2,1)S(1)}, u32[]{:S(2)}, u32[]{:S(2)}) async-start(bf16[4,136,2048]{2,1,0:T(8,128)(2,1)} %bitcast.390), calls=%async_computation.5 | async-start | bytes 4456448 | tf_op jit(solution)/shard_map/all_to_all | solution.py:114
  812.4 108.7 %all-to-all-start.4 = ((bf16[4,136,4096]{2,1,0:T(8,128)(2,1)}), bf16[4,136,4096]{2,1,0:T(8,128)(2,1)}, u32[]{:S(2)}, u32[]{:S(2)}) async-start(bf16[4,136,4096]{2,1,0:T(8,128)(2,1)} %bitcast.372), calls=%async_computation.4 | async-start | bytes 8912896 | tf_op jit(solution)/shard_map/all_to_all | solution.py:114
  980.8 54.6 %all-to-all-start.8 = ((bf16[4,136,2048]{2,1,0:T(8,128)(2,1)}), bf16[4,136,2048]{2,1,0:T(8,128)(2,1)S(1)}, u32[]{:S(2)}, u32[]{:S(2)}) async-start(bf16[4,136,2048]{2,1,0:T(8,128)(2,1)} %bitcast.397), calls=%async_computation.8 | async-start | bytes 4456448 | tf_op jit(solution)/shard_map/all_to_all | solution.py:114
  1036.8 54.1 %all-to-all-start.9 = ((bf16[4,136,2048]{2,1,0:T(8,128)(2,1)}), bf16[4,136,2048]{2,1,0:T(8,128)(2,1)S(1)}, u32[]{:S(2)}, u32[]{:S(2)}) async-start(bf16[4,136,2048]{2,1,0:T(8,128)(2,1)} %bitcast.396), calls=%async_computation.9 | async-start | bytes 4456448 | tf_op jit(solution)/shard_map/all_to_all | solution.py:114
  1090.9 54.9 %all-to-all-start.10 = ((bf16[4,136,2048]{2,1,0:T(8,128)(2,1)}), bf16[4,136,2048]{2,1,0:T(8,128)(2,1)}, u32[]{:S(2)}, u32[]{:S(2)}) async-start(bf16[4,136,2048]{2,1,0:T(8,128)(2,1)} %bitcast.387), calls=%async_computation.10 | async-start | bytes 4456448 | tf_op jit(solution)/shard_map/all_to_all | solution.py:114
  1099.2 202.7 %reduce-scatter.5.cloned.1.call-start = ((), (), s32[]{:S(2)}) async-start(), calls=%async_computation.21 | async-start | bytes 5242880 | tf_op jit(solution)/shard_map/reduce_scatter | solution.py:916
  1145.8 173.2 %reduce-scatter.3.cloned.1.call-start = ((), (), s32[]{:S(2)}) async-start(), calls=%async_computation.20 | async-start | bytes 5242880 | tf_op jit(solution)/shard_map/reduce_scatter | solution.py:916
  (106 other events, 1846.8 us)
Sparse Core Ops, SparseCore 0:
  15.3 207.1 all-gather.5
  224.4 214.1 all-gather.9
  440.4 211.3 all-gather.7
  653.5 160.7 all-gather.13
  816.1 72.1 all-gather.11
  1146.0 79.9 reduce-scatter.4
  1231.1 87.8 reduce-scatter.2

commit v7 on v6

--- a/solution.py
+++ b/solution.py
@@ -639,7 +639,7 @@
     inner_full, beside = [], []
     for l in range(locals_):
         pieces = []
-        cut = 3 * 512 if l + 1 < locals_ else FF * 3 // 4 // 512 * 512
+        cut = 2 * 512 if l + 1 < locals_ else FF * 3 // 4 // 512 * 512
         if l + 1 < locals_:
             pieces.append((0, None))
             beside.append(stretch(inner_weight, l, 0, cut))

time: 1340 us -> 1350 us (level)
  waiting for transfers between devices: 337 us -> 353 us
    all_to_all x12, waiting for transfers between devices: 190 us -> 207 us  [send(): lax.all_to_all(buffer, 'expert', split_axis=0, concat_axis=0, tiled=True)]
  transfers between devices with their start and end apart: 43 -> 43, of which waited for: 20 -> 20; matrix products, arithmetic and copies ran while one was open for 18% -> 17% of each run, Pallas kernels for 40% -> 40%
where the time goes in v7:
time: 1350 us; the launch traced here: 1340 us
  Pallas kernels  543 us (40%)
  waiting for transfers between devices  353 us (26%)
  starting transfers between devices  154 us (11%)
  other arithmetic  92.4 us (7%)
  matrix products  83.7 us (6%)
  local copies, waits for them, and re-layouts  71.6 us (5%)
  blocking collectives  23.2 us (2%)
  between operations  18 us (1%)
    all_to_all x12, waiting for transfers between devices, send(): lax.all_to_all(buffer, 'expert', split_axis=0, concat_axis=0, tiled=True)  207 us
    pallas_call x4, Pallas kernels, expert_pass(): pl.pallas_call(functools.partial(expert_body, start is not None, last is...  201 us
    ppermute x6, waiting for transfers between devices, hop(): lax.ppermute(from_left, axis, rightward)  93.8 us
    all_to_all x12, starting transfers between devices, send(): lax.all_to_all(buffer, 'expert', split_axis=0, concat_axis=0, tiled=True)  83.3 us
    pallas_call x2, Pallas kernels, last_grad(): pl.pallas_call(functools.partial(last_body, locals_, seq_len), grid=(widt...  77.4 us
    dot_general x23, matrix products, mm(): return lax.dot_general(left, right, dims, preferred_element_type=F32)  71.6 us
    pallas_call x2, Pallas kernels, attend_back(): pl.pallas_call(attend_back_body, grid=(HEADS,), in_specs=[pl.BlockSpec((l...  63.9 us
    pallas_call x1, Pallas kernels, attend(): pl.pallas_call(attend_body, grid=(seqs, HEADS), in_specs=[q_spec, pl.Bloc...  56 us
  transfers between devices with their start and end apart: 43, of which 20 were waited for; matrix products, arithmetic and copies ran while one was open for 17% of the time, Pallas kernels for 40%

profile of v7, /device:TPU:9, one launch (start us, length us, event | category | flops | bytes accessed | tf_op | source)
XLA Modules:
  0.0 1338.7 jit_solution(5875317866480594630)
XLA Ops:
  48.8 34.7 %collective-permute-done.4 = bf16[2,256,2048]{2,1,0:T(8,128)(2,1)} collective-permute-done((bf16[2,256,2048]{2,1,0:T(8,128)(2,1)S(1)}, bf16[2,256,2048]{2,1,0:T(8,128)(2,1)}, u32[]{:S(2)}, u32[]{:S(2)}) %collective-permute-start.4) | collective-permute-done | bytes 2097184 | tf_op jit(solution)/shard_map/ppermute | solution.py:78
  98.8 29.8 %collective-permute-done.5 = bf16[2,256,2048]{2,1,0:T(8,128)(2,1)} collective-permute-done((bf16[2,256,2048]{2,1,0:T(8,128)(2,1)}, bf16[2,256,2048]{2,1,0:T(8,128)(2,1)}, u32[]{:S(2)}, u32[]{:S(2)}) %collective-permute-start.5) | collective-permute-done | bytes 2097184 | tf_op jit(solution)/shard_map/ppermute | solution.py:78
  149.0 23.7 %collective-permute-done.6 = bf16[2,256,2048]{2,1,0:T(8,128)(2,1)} collective-permute-done((bf16[2,256,2048]{2,1,0:T(8,128)(2,1)}, bf16[2,256,2048]{2,1,0:T(8,128)(2,1)}, u32[]{:S(2)}, u32[]{:S(2)}) %collective-permute-start.6) | collective-permute-done | bytes 2097184 | tf_op jit(solution)/shard_map/ppermute | solution.py:78
  252.7 16.0 %project.2 = bf16[2,544,2048]{2,1,0:T(8,128)(2,1)} custom-call(bf16[2,544,2048]{2,1,0:T(8,128)(2,1)} %bitcast.371, bf16[2048,10240]{1,0:T(8,128)(2,1)} %all-gather.6.cloned.1.call-done.w_ref.wk_ref.refs_0_.refs_1_), custom_call_target="tpu_custom_call" | custom-call | tf_op jit(solution)/shard_map/project/pallas_call | solution.py:209
  328.3 48.8 %key_value.1 = bf16[2048,4096]{1,0:T(8,128)(2,1)} custom-call(bf16[2048,2048]{1,0:T(8,128)(2,1)} %bitcast.354, bf16[2048,128]{1,0:T(8,128)(2,1)} %bitcast.380, bf16[2048,10240]{1,0:T(8,128)(2,1)} %all-gather.6.cloned.1.call-done.w_ref.wk_ref.refs_0_.refs_1_, bf16[2048,2048]{1,0:T(8,128)(2,1)} %merge_halves.1.wv_ref, bf16[4096,128]{1,0:T(8,128)(2,1)} %up_ref.5, ...), custom_call_target="tpu_custom_call" | custom-call | tf_op jit(solution)/shard_map/key_value/pallas_call | solution.py:166
  377.0 56.0 %attend.1 = (bf16[2,2,272,2048]{3,2,1,0:T(8,128)(2,1)}, bf16[2,2,272,2048]{3,2,1,0:T(8,128)(2,1)}, bf16[2,2,16,272,1024]{4,3,2,1,0:T(8,128)(2,1)}) custom-call(bf16[2,2,272,2048]{3,2,1,0:T(8,128)(2,1)} %bitcast.369, bf16[2,1024,4096]{2,1,0:T(8,128)(2,1)} %bitcast.348, bf16[2,1024,4096]{2,1,0:T(8,128)(2,1)} %bitcast.349, ...), custom_call_target="tpu_custom_call" | custom-call | tf_op jit(solution)/shard_map/attend/pallas_call | solution.py:246
  433.0 18.4 %project.3 = (bf16[2,544,2048]{2,1,0:T(8,128)(2,1)}, bf16[2,544,2048]{2,1,0:T(8,128)(2,1)}) custom-call(bf16[2,544,2048]{2,1,0:T(8,128)(2,1)} %bitcast.381, bf16[2048,10240]{1,0:T(8,128)(2,1)} %all-gather.6.cloned.1.call-done.w_ref.wk_ref.refs_0_.refs_1_, f32[2,544,1]{2,1,0:T(8,128)} %fusion.88.refs_0_), custom_call_target="tpu_custom_call" | custom-call | tf_op jit(solution)/shard_map/project/pallas_call | solution.py:209
  472.2 38.8 %all-to-all-done.1 = bf16[4,136,2048]{2,1,0:T(8,128)(2,1)} async-done(((bf16[4,136,2048]{2,1,0:T(8,128)(2,1)}), bf16[4,136,2048]{2,1,0:T(8,128)(2,1)}, u32[]{:S(2)}, u32[]{:S(2)}) %all-to-all-start.1) | async-done | bytes 2228256 | tf_op jit(solution)/shard_map/all_to_all | solution.py:114
  529.7 36.3 %all-to-all-done.2 = bf16[4,136,2048]{2,1,0:T(8,128)(2,1)} async-done(((bf16[4,136,2048]{2,1,0:T(8,128)(2,1)}), bf16[4,136,2048]{2,1,0:T(8,128)(2,1)}, u32[]{:S(2)}, u32[]{:S(2)}) %all-to-all-start.2) | async-done | bytes 2228256 | tf_op jit(solution)/shard_map/all_to_all | solution.py:114
  590.6 29.5 %all-to-all-done.6 = bf16[4,136,2048]{2,1,0:T(8,128)(2,1)S(1)} async-done(((bf16[4,136,2048]{2,1,0:T(8,128)(2,1)}), bf16[4,136,2048]{2,1,0:T(8,128)(2,1)S(1)}, u32[]{:S(2)}, u32[]{:S(2)}) %all-to-all-start.6) | async-done | bytes 2228256 | tf_op jit(solution)/shard_map/all_to_all | solution.py:114
  636.3 16.8 %collective-permute-done.19 = bf16[2,128,2048]{2,1,0:T(8,128)(2,1)S(1)} collective-permute-done((bf16[2,128,2048]{2,1,0:T(8,128)(2,1)}, bf16[2,128,2048]{2,1,0:T(8,128)(2,1)S(1)}, u32[]{:S(2)}, u32[]{:S(2)}) %collective-permute-start.19) | collective-permute-done | bytes 1048608 | tf_op jit(solution)/shard_map/ppermute | solution.py:92
  718.2 25.9 %expert.4 = (f32[544,2048]{1,0:T(8,128)}, f32[544,2048]{1,0:T(8,128)}) custom-call(bf16[544,2048]{1,0:T(8,128)(2,1)} %bitcast.84.x_ref, bf16[544,2048]{1,0:T(8,128)(2,1)} %multiply_convert_fusion.2.c_ref, bf16[2048,2048]{1,0:T(8,128)(2,1)} %bitcast.357, bf16[2048,2048]{1,0:T(8,128)(2,1)} %bitcast.358, bf16[2,5632,2048]{2,1,0:T(8,128)(2,1)} %all-gather.10.cloned.1.call-done.wd_ref), custom_call_target="tpu_custom_call" | custom-call | tf_op jit(solution)/shard_map/expert/pallas_call | solution.py:397
  744.1 76.4 %expert.5 = bf16[544,4096]{1,0:T(8,128)(2,1)} custom-call(bf16[544,2048]{1,0:T(8,128)(2,1)} %bitcast.84.x_ref, bf16[544,2048]{1,0:T(8,128)(2,1)} %multiply_convert_fusion.2.c_ref, bf16[2048,9216]{1,0:T(8,128)(2,1)} %all-gather.8.cloned.1.call-done.wg_ref.wu_ref, bf16[2048,9216]{1,0:T(8,128)(2,1)} %all-gather.8.cloned.1.call-done.wg_ref.wu_ref, ...), custom_call_target="tpu_custom_call" | custom-call | tf_op jit(solution)/shard_map/expert/pallas_call | solution.py:397
  829.5 66.4 %expert.6 = (f32[544,2048]{1,0:T(8,128)}, f32[544,2048]{1,0:T(8,128)}) custom-call(bf16[544,2048]{1,0:T(8,128)(2,1)} %bitcast.362, bf16[544,2048]{1,0:T(8,128)(2,1)} %multiply_convert_fusion.1.c_ref, bf16[2048,8192]{1,0:T(8,128)(2,1)} %all-gather.14.cloned.1.call-done.wg_ref.wu_ref, bf16[2048,8192]{1,0:T(8,128)(2,1)} %all-gather.14.cloned.1.call-done.wg_ref.wu_ref, ...), custom_call_target="tpu_custom_call" | custom-call | tf_op jit(solution)/shard_map/expert/pallas_call | solution.py:397
  895.8 32.3 %expert.7 = (bf16[544,2048]{1,0:T(8,128)(2,1)}, bf16[544,2048]{1,0:T(8,128)(2,1)}) custom-call(bf16[544,2048]{1,0:T(8,128)(2,1)} %bitcast.363, bf16[544,2048]{1,0:T(8,128)(2,1)} %multiply_convert_fusion.1.c_ref, bf16[2048,3072]{1,0:T(8,128)(2,1)} %all-gather.12.cloned.1.call-done.wg_ref.wu_ref, ...), custom_call_target="tpu_custom_call" | custom-call | tf_op jit(solution)/shard_map/expert/pallas_call | solution.py:397
  945.1 34.3 %all-to-all-done.7 = bf16[4,136,2048]{2,1,0:T(8,128)(2,1)S(1)} async-done(((bf16[4,136,2048]{2,1,0:T(8,128)(2,1)}), bf16[4,136,2048]{2,1,0:T(8,128)(2,1)S(1)}, u32[]{:S(2)}, u32[]{:S(2)}) %all-to-all-start.7) | async-done | bytes 2228256 | tf_op jit(solution)/shard_map/all_to_all | solution.py:114
  1003.0 39.4 %all-to-all-done.8 = bf16[4,136,2048]{2,1,0:T(8,128)(2,1)S(1)} async-done(((bf16[4,136,2048]{2,1,0:T(8,128)(2,1)}), bf16[4,136,2048]{2,1,0:T(8,128)(2,1)S(1)}, u32[]{:S(2)}, u32[]{:S(2)}) %all-to-all-start.8) | async-done | bytes 2228256 | tf_op jit(solution)/shard_map/all_to_all | solution.py:114
  1051.3 13.6 %out_back.2 = (bf16[2,272,2048]{2,1,0:T(8,128)(2,1)}, f32[2,272,1]{2,1,0:T(8,128)}) custom-call(bf16[544,2048]{1,0:T(8,128)(2,1)} %bitcast.377, bf16[544,544]{1,0:T(8,128)(2,1)} %constant.176.clone.order_ref, f32[2,2,272,1]{3,2,1,0:T(8,128)} %get-tuple-element.183.gate_ref, bf16[2,2,272,2048]{3,2,1,0:T(8,128)(2,1)} %bitcast.367, ...), custom_call_target="tpu_custom_call" | custom-call | tf_op jit(solution)/shard_map/out_back/pallas_call | solution.py:435
  1064.9 32.0 %attend_back.2 = (bf16[2,272,2048]{2,1,0:T(8,128)(2,1)}, bf16[1024,2048]{1,0:T(8,128)(2,1)}, bf16[1024,2048]{1,0:T(8,128)(2,1)}) custom-call(bf16[2,2,272,2048]{3,2,1,0:T(8,128)(2,1)} %get-tuple-element.96.q_ref, bf16[2,1024,4096]{2,1,0:T(8,128)(2,1)} %bitcast.350, bf16[2,1024,4096]{2,1,0:T(8,128)(2,1)} %bitcast.351, ...), custom_call_target="tpu_custom_call" | custom-call | tf_op jit(solution)/shard_map/attend_back/pallas_call | solution.py:299
  1108.7 38.6 %last_grad.2 = (bf16[1024,2048]{1,0:T(8,128)(2,1)}, bf16[1024,128]{1,0:T(8,128)(2,1)}) custom-call(bf16[1024,2048]{1,0:T(8,128)(2,1)} %get-tuple-element.105.dk_ref, bf16[1024,2048]{1,0:T(8,128)(2,1)} %get-tuple-element.106.dv_ref, bf16[2,272,2048]{2,1,0:T(8,128)(2,1)} %get-tuple-element.107.dq_ref, bf16[2,1024,544]{2,1,0:T(8,128)(2,1)} %fusion.3.table_ref, ...), custom_call_target="tpu_custom_call" | custom-call | tf_op jit(solution)/shard_map/last_grad/pallas_call | solution.py:496
  1154.3 14.3 %out_back.3 = (bf16[2,272,2048]{2,1,0:T(8,128)(2,1)}, f32[2,272,1]{2,1,0:T(8,128)}) custom-call(bf16[544,2048]{1,0:T(8,128)(2,1)} %bitcast.376, bf16[544,544]{1,0:T(8,128)(2,1)} %constant.176.clone.order_ref, f32[2,2,272,1]{3,2,1,0:T(8,128)} %get-tuple-element.183.gate_ref, bf16[2,2,272,2048]{3,2,1,0:T(8,128)(2,1)} %bitcast.368, ...), custom_call_target="tpu_custom_call" | custom-call | tf_op jit(solution)/shard_map/out_back/pallas_call | solution.py:435
  1168.7 31.9 %attend_back.3 = (bf16[2,272,2048]{2,1,0:T(8,128)(2,1)}, bf16[1024,2048]{1,0:T(8,128)(2,1)}, bf16[1024,2048]{1,0:T(8,128)(2,1)}) custom-call(bf16[2,2,272,2048]{3,2,1,0:T(8,128)(2,1)} %get-tuple-element.96.q_ref, bf16[2,1024,4096]{2,1,0:T(8,128)(2,1)} %bitcast.352, bf16[2,1024,4096]{2,1,0:T(8,128)(2,1)} %bitcast.353, ...), custom_call_target="tpu_custom_call" | custom-call | tf_op jit(solution)/shard_map/attend_back/pallas_call | solution.py:299
  1200.6 38.8 %last_grad.3 = (bf16[1024,2048]{1,0:T(8,128)(2,1)}, bf16[1024,128]{1,0:T(8,128)(2,1)}) custom-call(bf16[1024,2048]{1,0:T(8,128)(2,1)} %get-tuple-element.117.dk_ref, bf16[1024,2048]{1,0:T(8,128)(2,1)} %get-tuple-element.118.dv_ref, bf16[2,272,2048]{2,1,0:T(8,128)(2,1)} %get-tuple-element.119.dq_ref, bf16[2,1024,544]{2,1,0:T(8,128)(2,1)} %fusion.3.table_ref, ...), custom_call_target="tpu_custom_call" | custom-call | tf_op jit(solution)/shard_map/last_grad/pallas_call | solution.py:496
  1314.1 13.4 %reduce-scatter.3.cloned.1.call-done.grad_ref = bf16[256,2048]{1,0:T(8,128)(2,1)} async-done(((bf16[1024,2048]{1,0:T(8,128)(2,1)}), bf16[256,2048]{1,0:T(8,128)(2,1)}) %reduce-scatter.3.cloned.1.call-update) | async-done | bytes 1048592 | tf_op jit(solution)/shard_map/reduce_scatter | solution.py:916
  (451 shorter events, 514.7 us)
Async XLA Ops:
  7.2 245.6 %all-gather.6.cloned.1.call-start = ((), (), s32[]{:S(2)}) async-start(), calls=%async_computation.15 | async-start | bytes 47185920 | tf_op jit(solution)/shard_map/all_gather | solution.py:632
  13.9 704.4 %all-gather.10.cloned.1.call-start = ((), (), s32[]{:S(2)}) async-start(), calls=%async_computation.17 | async-start | bytes 51904512 | tf_op jit(solution)/shard_map/all_gather | solution.py:633
  14.6 729.5 %all-gather.8.cloned.1.call-start = ((), (), s32[]{:S(2)}) async-start(), calls=%async_computation.16 | async-start | bytes 42467328 | tf_op jit(solution)/shard_map/all_gather | solution.py:648
  20.0 809.5 %all-gather.14.cloned.1.call-start = ((), (), s32[]{:S(2)}) async-start(), calls=%async_computation.19 | async-start | bytes 37748736 | tf_op jit(solution)/shard_map/all_gather | solution.py:647
  45.4 89.9 %collective-permute-start = (bf16[128,512]{1,0:T(8,128)(2,1)S(1)}, bf16[128,512]{1,0:T(8,128)(2,1)S(1)}, u32[]{:S(2)}, u32[]{:S(2)}) collective-permute-start(bf16[128,512]{1,0:T(8,128)(2,1)S(1)} %get-tuple-element.171), channel_id=1, source_target_pairs={{0,8},{4,12},{8,0},{12,4},{16,24},{20,28},{24,16},{28,20},{1,9},{5... | collective-permute-start | bytes 393224 | tf_op jit(solution)/shard_map/ppermute | solution.py:92
  46.7 90.0 %collective-permute-start.2 = (bf16[128,512]{1,0:T(8,128)(2,1)S(1)}, bf16[128,512]{1,0:T(8,128)(2,1)S(1)}, u32[]{:S(2)}, u32[]{:S(2)}) collective-permute-start(bf16[128,512]{1,0:T(8,128)(2,1)S(1)} %get-tuple-element.172), channel_id=1, source_target_pairs={{0,16},{4,20},{8,24},{12,28},{16,0},{20,4},{24,8},{28,12},{1,17},{... | collective-permute-start | bytes 393224 | tf_op jit(solution)/shard_map/ppermute | solution.py:92
  302.2 130.8 %all-to-all-start = ((bf16[4,136,2048]{2,1,0:T(8,128)(2,1)}), bf16[4,136,2048]{2,1,0:T(8,128)(2,1)}, u32[]{:S(2)}, u32[]{:S(2)}) async-start(bf16[4,136,2048]{2,1,0:T(8,128)(2,1)} %bitcast.390), calls=%async_computation | async-start | bytes 4456448 | tf_op jit(solution)/shard_map/all_to_all | solution.py:114
  459.3 51.8 %all-to-all-start.1 = ((bf16[4,136,2048]{2,1,0:T(8,128)(2,1)}), bf16[4,136,2048]{2,1,0:T(8,128)(2,1)}, u32[]{:S(2)}, u32[]{:S(2)}) async-start(bf16[4,136,2048]{2,1,0:T(8,128)(2,1)} %bitcast.395), calls=%async_computation.1 | async-start | bytes 4456448 | tf_op jit(solution)/shard_map/all_to_all | solution.py:114
  464.0 431.9 %all-gather.12.cloned.1.call-start = ((), (), s32[]{:S(2)}) async-start(), calls=%async_computation.18 | async-start | bytes 14155776 | tf_op jit(solution)/shard_map/all_gather | solution.py:648
  511.1 54.9 %all-to-all-start.2 = ((bf16[4,136,2048]{2,1,0:T(8,128)(2,1)}), bf16[4,136,2048]{2,1,0:T(8,128)(2,1)}, u32[]{:S(2)}, u32[]{:S(2)}) async-start(bf16[4,136,2048]{2,1,0:T(8,128)(2,1)} %bitcast.392), calls=%async_computation.2 | async-start | bytes 4456448 | tf_op jit(solution)/shard_map/all_to_all | solution.py:114
  524.9 48.9 %collective-permute-start.17 = (bf16[128,2048]{1,0:T(8,128)(2,1)}, bf16[128,2048]{1,0:T(8,128)(2,1)}, u32[]{:S(2)}, u32[]{:S(2)}) collective-permute-start(bf16[128,2048]{1,0:T(8,128)(2,1)} %get-tuple-element.180), channel_id=1, source_target_pairs={{0,8},{4,12},{8,0},{12,4},{16,24},{20,28},{24,16},{28,20},{1,9},{5... | collective-permute-start | bytes 1572872 | tf_op jit(solution)/shard_map/ppermute | solution.py:92
  526.0 48.1 %collective-permute-start.18 = (bf16[128,2048]{1,0:T(8,128)(2,1)}, bf16[128,2048]{1,0:T(8,128)(2,1)}, u32[]{:S(2)}, u32[]{:S(2)}) collective-permute-start(bf16[128,2048]{1,0:T(8,128)(2,1)} %get-tuple-element.179), channel_id=1, source_target_pairs={{0,16},{4,20},{8,24},{12,28},{16,0},{20,4},{24,8},{28,12},{1,17},{... | collective-permute-start | bytes 1572872 | tf_op jit(solution)/shard_map/ppermute | solution.py:92
  566.0 54.1 %all-to-all-start.6 = ((bf16[4,136,2048]{2,1,0:T(8,128)(2,1)}), bf16[4,136,2048]{2,1,0:T(8,128)(2,1)S(1)}, u32[]{:S(2)}, u32[]{:S(2)}) async-start(bf16[4,136,2048]{2,1,0:T(8,128)(2,1)} %bitcast.391), calls=%async_computation.6 | async-start | bytes 4456448 | tf_op jit(solution)/shard_map/all_to_all | solution.py:114
  576.7 54.3 %collective-permute-start.21 = (bf16[2,128,2048]{2,1,0:T(8,128)(2,1)S(1)}, bf16[2,128,2048]{2,1,0:T(8,128)(2,1)}, u32[]{:S(2)}, u32[]{:S(2)}) collective-permute-start(bf16[2,128,2048]{2,1,0:T(8,128)(2,1)S(1)} %get-tuple-element.85), channel_id=1, source_target_pairs={{0,8},{4,12},{8,0},{12,4},{16,24},{20,28},{24,16},{28,20},{1,9},{5... | collective-permute-start | bytes 3145736 | tf_op jit(solution)/shard_map/ppermute | solution.py:92
  621.5 54.9 %all-to-all-start.3 = ((bf16[4,136,2048]{2,1,0:T(8,128)(2,1)}), bf16[4,136,2048]{2,1,0:T(8,128)(2,1)}, u32[]{:S(2)}, u32[]{:S(2)}) async-start(bf16[4,136,2048]{2,1,0:T(8,128)(2,1)} %bitcast.388), calls=%async_computation.3 | async-start | bytes 4456448 | tf_op jit(solution)/shard_map/all_to_all | solution.py:114
  634.3 52.3 %collective-permute-start.22 = (bf16[2,2,128,2048]{3,2,1,0:T(8,128)(2,1)}, bf16[2,2,128,2048]{3,2,1,0:T(8,128)(2,1)}, u32[]{:S(2)}, u32[]{:S(2)}) collective-permute-start(bf16[2,2,128,2048]{3,2,1,0:T(8,128)(2,1)} %pad_maximum_fusion.6), channel_id=1, source_target_pairs={{0,4},{4,0},{8,12},{12,8},{16,20},{20,16},{24,28},{28,24},{1,5},{5... | collective-permute-start | bytes 6291464 | tf_op jit(solution)/shard_map/ppermute | solution.py:92
  676.4 144.1 %all-to-all-start.5 = ((bf16[4,136,2048]{2,1,0:T(8,128)(2,1)}), bf16[4,136,2048]{2,1,0:T(8,128)(2,1)S(1)}, u32[]{:S(2)}, u32[]{:S(2)}) async-start(bf16[4,136,2048]{2,1,0:T(8,128)(2,1)} %bitcast.389), calls=%async_computation.5 | async-start | bytes 4456448 | tf_op jit(solution)/shard_map/all_to_all | solution.py:114
  820.5 107.7 %all-to-all-start.4 = ((bf16[4,136,4096]{2,1,0:T(8,128)(2,1)}), bf16[4,136,4096]{2,1,0:T(8,128)(2,1)}, u32[]{:S(2)}, u32[]{:S(2)}) async-start(bf16[4,136,4096]{2,1,0:T(8,128)(2,1)} %bitcast.370), calls=%async_computation.4 | async-start | bytes 8912896 | tf_op jit(solution)/shard_map/all_to_all | solution.py:114
  928.3 51.1 %all-to-all-start.7 = ((bf16[4,136,2048]{2,1,0:T(8,128)(2,1)}), bf16[4,136,2048]{2,1,0:T(8,128)(2,1)S(1)}, u32[]{:S(2)}, u32[]{:S(2)}) async-start(bf16[4,136,2048]{2,1,0:T(8,128)(2,1)} %bitcast.393), calls=%async_computation.7 | async-start | bytes 4456448 | tf_op jit(solution)/shard_map/all_to_all | solution.py:114
  987.7 54.7 %all-to-all-start.8 = ((bf16[4,136,2048]{2,1,0:T(8,128)(2,1)}), bf16[4,136,2048]{2,1,0:T(8,128)(2,1)S(1)}, u32[]{:S(2)}, u32[]{:S(2)}) async-start(bf16[4,136,2048]{2,1,0:T(8,128)(2,1)} %bitcast.397), calls=%async_computation.8 | async-start | bytes 4456448 | tf_op jit(solution)/shard_map/all_to_all | solution.py:114
  1043.8 54.1 %all-to-all-start.9 = ((bf16[4,136,2048]{2,1,0:T(8,128)(2,1)}), bf16[4,136,2048]{2,1,0:T(8,128)(2,1)S(1)}, u32[]{:S(2)}, u32[]{:S(2)}) async-start(bf16[4,136,2048]{2,1,0:T(8,128)(2,1)} %bitcast.396), calls=%async_computation.9 | async-start | bytes 4456448 | tf_op jit(solution)/shard_map/all_to_all | solution.py:114
  1099.3 55.0 %all-to-all-start.10 = ((bf16[4,136,2048]{2,1,0:T(8,128)(2,1)}), bf16[4,136,2048]{2,1,0:T(8,128)(2,1)}, u32[]{:S(2)}, u32[]{:S(2)}) async-start(bf16[4,136,2048]{2,1,0:T(8,128)(2,1)} %bitcast.387), calls=%async_computation.10 | async-start | bytes 4456448 | tf_op jit(solution)/shard_map/all_to_all | solution.py:114
  1107.7 202.6 %reduce-scatter.5.cloned.1.call-start = ((), (), s32[]{:S(2)}) async-start(), calls=%async_computation.21 | async-start | bytes 5242880 | tf_op jit(solution)/shard_map/reduce_scatter | solution.py:916
  1154.3 173.3 %reduce-scatter.3.cloned.1.call-start = ((), (), s32[]{:S(2)}) async-start(), calls=%async_computation.20 | async-start | bytes 5242880 | tf_op jit(solution)/shard_map/reduce_scatter | solution.py:916
  (98 other events, 2411.0 us)
Sparse Core Ops, SparseCore 0:
  14.0 207.1 all-gather.5
  223.1 214.1 all-gather.9
  439.1 211.6 all-gather.7
  652.5 160.7 all-gather.13
  815.1 72.1 all-gather.11
  1154.4 80.0 reduce-scatter.4
  1239.5 87.9 reduce-scatter.2
